TPU v7x, 256 devices: a whole 4x4x8 slice. The times are simulated.
256 devices in a mesh: section: 8 (over z_lo, core), dp: 32 (over z_hi, y, x).
Axes of the slice: x: 4, y: 4, z: 8 (z_hi: 2, z_lo: 4; z = z_hi * 4 + z_lo), core: 2. Of those that a mesh axis runs over, the one named last changes fastest.
Arguments:
- tokens: bfloat16 [2, 32, 256, 2048], P(None, 'dp'), may hold values from -0.14941406 to 0.14941406
- cotangent: bfloat16 [2, 32, 256, 2048], P(None, 'dp'), may hold values from -6 to 6
- inflow: bfloat16 [8, 32, 256, 2048], P('section', 'dp'), may hold values from -0.14941406 to 0.14941406
- backflow: bfloat16 [8, 32, 256, 2048], P('section', 'dp'), may hold values from -6 to 6
- norm_gain: float32 [8, 2048], P('section'), may hold values from 0.5 to 1.5
- slot_scale: float32 [8], P('section'), may hold values from 20 to 60
- router_weight: bfloat16 [8, 2048, 128], P('section', None, 'dp'), may hold values from -6 to 6
- expert_in: bfloat16 [8, 2048, 8192], P('section', None, 'dp'), may hold values from -2 to 2
- expert_back: bfloat16 [8, 8192, 2048], P('section', 'dp'), may hold values from -0.0625 to 0.0625
Outputs:
- section_grads: bfloat16 [8, 2, 32, 256, 2048], P('section', None, 'dp')
- slot_out: bfloat16 [8, 2, 32, 2048], P('section', None, 'dp')
- slot_grad: bfloat16 [8, 2, 32, 2048], P('section', None, 'dp')
- expert_in_grad: bfloat16 [8, 2048, 8192], P('section', None, 'dp')
- expert_back_grad: bfloat16 [8, 8192, 2048], P('section', 'dp')
- router_grad: bfloat16 [8, 2048, 128], P('section', None, 'dp')
- gain_grad: float32 [8, 2048], P('section')
All inputs are finite; a program needn't handle non-finite values.
Results may differ from a plain program's by a relative error of at most 0.039.
Values may be sent and summed in bfloat16 or wider, within the bound.
No kernel may reach another device: no remote copies, remote signals or barrier semaphores. Data moves between devices by JAX's collectives and lax.ppermute only.
A program may use at most 64 MiB of HBM per device.

v0:
```python
import jax
import jax.numpy as jnp
from jax import lax
from jax.sharding import PartitionSpec as P

EPSILON = 1e-06
precise = lax.Precision.HIGHEST


def shifted(block, axis, distance):
    devices = range(lax.axis_size(axis))
    route = [(i - distance, i) for i in devices if i - distance in devices]
    return lax.ppermute(block, axis, route)


def norm_tokens(act_in, gain_row):
    meansq = jnp.mean(act_in * act_in, axis=-1, keepdims=True)
    return act_in * lax.rsqrt(meansq + EPSILON) * gain_row


def normalize_cols(weights):
    wide = weights.astype(jnp.float32)
    return wide * lax.rsqrt(jnp.sum(wide * wide, axis=0, keepdims=True) + EPSILON)


def mix_slots(hidden, scores, scale_val):
    sumsq = jnp.sum(hidden * hidden, axis=-1, keepdims=True)
    logits = scale_val * scores * lax.rsqrt(sumsq + EPSILON)
    expo = jnp.exp(logits)
    first_col = expo[..., 0]
    combine = first_col / jnp.sum(expo, axis=-1)
    dispatch = (first_col / jnp.sum(first_col, axis=-1, keepdims=True)).astype(jnp.bfloat16)
    slot_rows = jnp.einsum("ip,ipd->id", dispatch.astype(jnp.float32), hidden, precision=precise)
    return (slot_rows.astype(jnp.bfloat16), combine)


def dot_last(left_side, right_side):
    return lax.dot_general(
        left_side, right_side, (((1,), (1,)), ((), ())), preferred_element_type=jnp.float32
    )


def dot_rows(left_side, right_side):
    return lax.dot_general(
        left_side, right_side, (((0,), (0,)), ((), ())), preferred_element_type=jnp.float32
    )


def pick_row(buffer, position):
    return lax.dynamic_index_in_dim(buffer, position, 0, keepdims=False)


def store_row(buffer, position, entry_value):
    return lax.dynamic_update_index_in_dim(buffer, entry_value, position, 0)


def shards(
    tokens,
    cotangent,
    inflow,
    backflow,
    norm_gain,
    slot_scale,
    router_weight,
    expert_in,
    expert_back,
):
    section_index = lax.axis_index("section")
    section_count = lax.axis_size("section")
    group_size = lax.axis_size("dp")
    micro_count = tokens.shape[0]
    img_dev = tokens.shape[1]
    patches = tokens.shape[2]
    model_width = tokens.shape[3]
    gain_row = norm_gain[0]
    scale_val = slot_scale[0]
    first_weight = expert_in[0]
    second_weight = expert_back[0]
    hidden_units = first_weight.shape[1]
    local_cols = normalize_cols(router_weight[0]).astype(jnp.bfloat16)
    columns = lax.all_gather(local_cols, "dp", axis=1, tiled=True)
    slot_count = columns.shape[1]
    rows_all = img_dev * group_size

    def front_scores(section_in):
        normed = norm_tokens(section_in.astype(jnp.float32), gain_row)
        hidden_bf = normed.astype(jnp.bfloat16)
        scores = jnp.dot(
            hidden_bf.reshape(-1, model_width), columns, preferred_element_type=jnp.float32
        )
        return (hidden_bf, scores.reshape(img_dev, patches, slot_count))

    def forward_layer(section_in):
        hidden_bf, scores = front_scores(section_in)
        slot_rows, combine = mix_slots(hidden_bf.astype(jnp.float32), scores, scale_val)
        slot_all = lax.all_gather(slot_rows, "dp", axis=0, tiled=True)
        pre_act = jnp.dot(slot_all, first_weight, preferred_element_type=jnp.float32)
        activation = jax.nn.gelu(pre_act).astype(jnp.bfloat16)
        mixed_out = lax.psum_scatter(
            jnp.dot(activation, second_weight, preferred_element_type=jnp.float32),
            "dp",
            scatter_dimension=0,
            tiled=True,
        ).astype(jnp.bfloat16)
        return (slot_all, pre_act, activation, mixed_out, combine)

    def residual_add(section_in, combine, mixed_out):
        widened = (
            section_in.astype(jnp.float32)
            + combine[..., None] * mixed_out.astype(jnp.float32)[:, None, :]
        )
        return widened.astype(jnp.bfloat16)

    saved_start = (
        jnp.zeros((micro_count, img_dev, patches, model_width), jnp.bfloat16),
        jnp.zeros((micro_count, rows_all, model_width), jnp.bfloat16),
        jnp.zeros((micro_count, rows_all, hidden_units), jnp.float32),
        jnp.zeros((micro_count, rows_all, hidden_units), jnp.bfloat16),
        jnp.zeros((micro_count, img_dev, model_width), jnp.bfloat16),
        jnp.zeros((micro_count, img_dev, patches), jnp.float32),
    )

    def forward_tick(tick_index, state_tuple):
        incoming, saved_all = state_tuple
        arrived = jnp.where(tick_index == 0, inflow[0], incoming)
        section_in = jnp.where(section_index == 0, pick_row(tokens, tick_index), arrived)
        slot_all, pre_act, activation, mixed_out, combine = forward_layer(section_in)
        outgoing = residual_add(section_in, combine, mixed_out)
        incoming = shifted(outgoing, "section", 1)
        values = (section_in, slot_all, pre_act, activation, mixed_out, combine)
        saved_all = tuple(
            (
                store_row(buffer, tick_index, entry_value)
                for buffer, entry_value in zip(saved_all, values)
            )
        )
        return (incoming, saved_all)

    start_link = jnp.zeros((img_dev, patches, model_width), jnp.bfloat16)
    link_end, saved_all = lax.fori_loop(0, micro_count, forward_tick, (start_link, saved_start))
    saved_in, saved_slot, saved_pre, saved_act, saved_mixed, saved_comb = saved_all
    router_shape = (model_width, slot_count)

    def backward_tick(tick_index, state_tuple):
        (
            incoming,
            grads_buf,
            dslot_buf,
            pregrad_buf,
            dmixed_buf,
            router_acc,
            gain_acc,
            first_acc,
            second_acc,
        ) = state_tuple
        position = micro_count - 1 - tick_index
        arrived = jnp.where(tick_index == 0, backflow[0], incoming)
        upstream = jnp.where(
            section_index == section_count - 1, pick_row(cotangent, position), arrived
        )
        upstream_f = upstream.astype(jnp.float32)
        combine = pick_row(saved_comb, position)
        mixed_out = pick_row(saved_mixed, position)
        dmixed = jnp.einsum("ip,ipd->id", combine, upstream_f, precision=precise).astype(
            jnp.bfloat16
        )
        dmixed_all = lax.all_gather(dmixed, "dp", axis=0, tiled=True)
        pre_act = pick_row(saved_pre, position)
        gelu_pull = jax.vjp(jax.nn.gelu, pre_act)[1]
        pre_grad = gelu_pull(dot_last(dmixed_all, second_weight))[0].astype(jnp.bfloat16)
        slot_back = lax.psum_scatter(
            dot_last(pre_grad, first_weight).astype(jnp.bfloat16),
            "dp",
            scatter_dimension=0,
            tiled=True,
        )
        dcombine = jnp.einsum(
            "ipd,id->ip", upstream_f, mixed_out.astype(jnp.float32), precision=precise
        )
        section_in = pick_row(saved_in, position)
        normed, pull_norm = jax.vjp(norm_tokens, section_in.astype(jnp.float32), gain_row)
        hidden_bf = normed.astype(jnp.bfloat16)
        scores = jnp.dot(
            hidden_bf.reshape(-1, model_width), columns, preferred_element_type=jnp.float32
        )
        scores = scores.reshape(img_dev, patches, slot_count)
        pull_mix = jax.vjp(
            lambda left_side, right_side: mix_slots(left_side, right_side, scale_val),
            hidden_bf.astype(jnp.float32),
            scores,
        )[1]
        dhidden, dscores = pull_mix((slot_back, dcombine))
        dscores_bf = dscores.astype(jnp.bfloat16).reshape(-1, slot_count)
        dhidden = dhidden + dot_last(dscores_bf, columns).reshape(dhidden.shape)
        router_term = dot_rows(hidden_bf.reshape(-1, model_width), dscores_bf)
        router_acc = router_acc + router_term
        dinput, dgain = pull_norm(dhidden)
        gain_acc = gain_acc + dgain
        new_grad = (upstream_f + dinput).astype(jnp.bfloat16)
        first_acc = first_acc + dot_rows(pick_row(saved_slot, position), pre_grad)
        second_acc = second_acc + dot_rows(pick_row(saved_act, position), dmixed_all)
        incoming = shifted(new_grad, "section", -1)
        grads_buf = store_row(grads_buf, position, new_grad)
        dslot_buf = store_row(dslot_buf, position, slot_back)
        pregrad_buf = store_row(pregrad_buf, position, pre_grad)
        dmixed_buf = store_row(dmixed_buf, position, dmixed_all)
        return (
            incoming,
            grads_buf,
            dslot_buf,
            pregrad_buf,
            dmixed_buf,
            router_acc,
            gain_acc,
            first_acc,
            second_acc,
        )

    back_start = (
        jnp.zeros((img_dev, patches, model_width), jnp.bfloat16),
        jnp.zeros((micro_count, img_dev, patches, model_width), jnp.bfloat16),
        jnp.zeros((micro_count, img_dev, model_width), jnp.bfloat16),
        jnp.zeros((micro_count, rows_all, hidden_units), jnp.bfloat16),
        jnp.zeros((micro_count, rows_all, model_width), jnp.bfloat16),
        jnp.zeros(router_shape, jnp.float32),
        jnp.zeros((model_width,), jnp.float32),
        jnp.zeros((model_width, hidden_units), jnp.float32),
        jnp.zeros((hidden_units, model_width), jnp.float32),
    )
    back_end = lax.fori_loop(0, micro_count, backward_tick, back_start)
    (
        link_back,
        grads_buf,
        dslot_buf,
        pregrad_buf,
        dmixed_buf,
        router_acc,
        gain_acc,
        first_acc,
        second_acc,
    ) = back_end
    router_local = lax.psum_scatter(
        router_acc.astype(jnp.bfloat16), "dp", scatter_dimension=1, tiled=True
    ).astype(jnp.float32)
    gain_total = lax.psum(gain_acc, "dp")
    pull_cols = jax.vjp(normalize_cols, router_weight[0])[1]
    router_grad = pull_cols(router_local)[0]
    return (
        grads_buf[None],
        saved_mixed[None],
        dslot_buf[None],
        first_acc.astype(jnp.bfloat16)[None],
        second_acc.astype(jnp.bfloat16)[None],
        router_grad[None],
        gain_total[None],
    )


def solution(mesh):
    in_specs = (
        P(None, "dp", None, None),
        P(None, "dp", None, None),
        P("section", "dp", None, None),
        P("section", "dp", None, None),
        P("section", None),
        P("section"),
        P("section", None, "dp"),
        P("section", None, "dp"),
        P("section", "dp", None),
    )
    out_specs = (
        P("section", None, "dp", None, None),
        P("section", None, "dp", None),
        P("section", None, "dp", None),
        P("section", None, "dp"),
        P("section", "dp", None),
        P("section", None, "dp"),
        P("section", None),
    )
    return jax.shard_map(shards, mesh=mesh, in_specs=in_specs, out_specs=out_specs, check_vma=False)
```

profile of v0, /device:TPU:32, one launch (start us, length us, event | category | flops | bytes accessed | tf_op | source)
XLA Modules:
  0.0 2363.2 jit_solution(7621150961722676558)
XLA Ops:
  10.7 120.3 %all-gather.2 = bf16[32,4,2048]{2,1,0:T(4,128)(2,1)S(1)} all-gather(bf16[1,4,2048]{2,1,0:T(4,128)(2,1)S(1)} %fusion.103), channel_id=1, replica_groups=mesh['section'=8,'dp'=32] {'dp'}, dimensions={0}, use_global_device_ids=true | all-gather | bytes 540672 | tf_op jit(solution)/shard_map/all_gather | solution.py:81
  133.5 715.7 %while.55 = (s32[]{:T(128)}, bf16[1,256,2048]{2,1,0:T(8,128)(2,1)}, bf16[2,1,256,2048]{3,2,1,0:T(8,128)(2,1)S(1)}, bf16[2,32,2048]{2,1,0:T(8,128)(2,1)}, f32[2,3...) while((s32[]{:T(128)}, bf16[1,256,2048]{2,1,0:T(8,128)(2,1)}, ...), condition=%wide.region_7.8_spmd, body=%wide.region_1.7_spmd.sunk | while | flops 215274752 | bytes 27840060 | solution.py:140
  133.5 2.2 bitcast_dynamic-update-slice_fusion.10
  139.7 107.2 %all-gather.6 = bf16[65536]{0:T(1024)(128)(2,1)S(1)} all-gather(bf16[2048]{0:T(1024)(128)(2,1)S(1)} %convert_element_type.630), channel_id=2, replica_groups=mesh['section'=8,'dp'=32] {'dp'}, dimensions={0}, use_global_device_ids=true | all-gather | bytes 135168 | tf_op jit(solution)/shard_map/while/body/eval_jaxpr/all_gather | solution.py:96
  246.9 2.1 bitcast_dynamic-update-slice_fusion.11
  249.7 1.5 fusion.176
  251.1 218.6 %all-reduce.15 = bf16[32,2048]{1,0:T(8,128)(2,1)} all-reduce(f32[32,2048]{1,0:T(8,128)S(1)} %fusion.176), channel_id=4, replica_groups=mesh['section'=8,'dp'=32] {'dp'}, use_global_device_ids=true, to_apply=%region_6.6.clone | all-reduce | flops 65536 | bytes 393216 | tf_op jit(solution)/shard_map/while
  473.9 1.9 collective-permute-start
  475.9 1.5 bitcast_dynamic-update-slice_fusion.13
  479.3 10.9 collective-permute-done
  491.2 2.5 bitcast_dynamic-update-slice_fusion.10
  497.7 107.2 %all-gather.6 = bf16[65536]{0:T(1024)(128)(2,1)S(1)} all-gather(bf16[2048]{0:T(1024)(128)(2,1)S(1)} %convert_element_type.630), channel_id=2, replica_groups=mesh['section'=8,'dp'=32] {'dp'}, dimensions={0}, use_global_device_ids=true | all-gather | bytes 135168 | tf_op jit(solution)/shard_map/while/body/eval_jaxpr/all_gather | solution.py:96
  604.9 2.1 bitcast_dynamic-update-slice_fusion.11
  607.7 1.5 fusion.176
  609.2 218.6 %all-reduce.15 = bf16[32,2048]{1,0:T(8,128)(2,1)} all-reduce(f32[32,2048]{1,0:T(8,128)S(1)} %fusion.176), channel_id=4, replica_groups=mesh['section'=8,'dp'=32] {'dp'}, use_global_device_ids=true, to_apply=%region_6.6.clone | all-reduce | flops 65536 | bytes 393216 | tf_op jit(solution)/shard_map/while
  831.9 1.9 collective-permute-start
  833.9 1.5 bitcast_dynamic-update-slice_fusion.13
  837.3 10.9 collective-permute-done
  849.2 1.6 broadcast.585
  852.5 1074.0 %while.56 = (s32[]{:T(128)}, bf16[1,256,2048]{2,1,0:T(8,128)(2,1)}, bf16[2,1,256,2048]{3,2,1,0:T(8,128)(2,1)}, bf16[2,1,2048]{2,0,1:T(2,128)(2,1)}, f32[2048,128...) while((s32[]{:T(128)}, bf16[1,256,2048]{2,1,0:T(8,128)(2,1)}, ...), condition=%wide.region_18.19_spmd.clone, body=%wide.region_8.18_spmd.clone.sunk | while | flops 574010368 | bytes 99640032 | solution.py:230
  852.5 1.7 fusion.202
  855.4 107.2 %all-gather.7 = bf16[65536]{0:T(1024)(128)(2,1)S(1)} all-gather(bf16[2048]{0:T(1024)(128)(2,1)S(1)} %convert_element_type.649), channel_id=3, replica_groups=mesh['section'=8,'dp'=32] {'dp'}, dimensions={0}, use_global_device_ids=true | all-gather | bytes 135168 | tf_op jit(solution)/shard_map/while/body/eval_jaxpr/all_gather | solution.py:167
  962.7 1.7 fusion.205
  964.3 2.3 convolution_convert_fusion.2
  972.0 1.7 fusion.203
  976.3 382.0 %all-reduce.14.cloned.1.call-done = bf16[32,2048]{1,0:T(8,128)(2,1)} async-done(((bf16[32,2048]{1,0:T(8,128)(2,1)}), bf16[32,2048]{1,0:T(8,128)(2,1)}) %all-reduce.14.cloned.1.call-update) | async-done | bytes 131088 | tf_op jit(solution)/shard_map/while
  1358.3 1.8 fusion.206
  1365.7 3.1 fusion.211
  1368.8 1.7 bitcast_dynamic-update-slice_fusion.14
  1370.5 1.9 collective-permute-start.1
  1376.2 2.3 convolution_add_fusion.6
  1378.4 6.6 collective-permute-done.1
  1386.0 2.0 fusion.202
  1389.2 113.3 %all-gather.7 = bf16[65536]{0:T(1024)(128)(2,1)S(1)} all-gather(bf16[2048]{0:T(1024)(128)(2,1)S(1)} %convert_element_type.649), channel_id=3, replica_groups=mesh['section'=8,'dp'=32] {'dp'}, dimensions={0}, use_global_device_ids=true | all-gather | bytes 135168 | tf_op jit(solution)/shard_map/while/body/eval_jaxpr/all_gather | solution.py:167
  1502.6 1.7 fusion.205
  1504.3 2.3 convolution_convert_fusion.2
  1512.0 1.7 fusion.203
  1516.3 382.4 %all-reduce.14.cloned.1.call-done = bf16[32,2048]{1,0:T(8,128)(2,1)} async-done(((bf16[32,2048]{1,0:T(8,128)(2,1)}), bf16[32,2048]{1,0:T(8,128)(2,1)}) %all-reduce.14.cloned.1.call-update) | async-done | bytes 131088 | tf_op jit(solution)/shard_map/while
  1898.7 1.8 fusion.206
  1906.1 3.1 fusion.211
  1909.3 1.7 bitcast_dynamic-update-slice_fusion.14
  1911.0 1.9 collective-permute-start.1
  1916.6 3.5 convolution_add_fusion.6
  1920.1 5.4 collective-permute-done.1
  1926.5 2.3 copy.21
  1929.9 2.7 convert_bitcast_fusion.2
  1932.7 115.8 %psum.7 = f32[1,2048]{1,0:T(1,128)} all-reduce(f32[1,2048]{1,0:T(1,128)S(1)} %bitcast.336), channel_id=1, replica_groups=mesh['section'=8,'dp'=32] {'dp'}, use_global_device_ids=true, to_apply=%region_21.22 | all-reduce | flops 2048 | bytes 16384 | tf_op jit(solution)/shard_map/psum | solution.py:245
  2050.2 303.1 %all-reduce.12.cloned.1.call-done = bf16[2048,128]{0,1:T(8,128)(2,1)} async-done(((bf16[2048,128]{0,1:T(8,128)(2,1)}), bf16[2048,128]{0,1:T(8,128)(2,1)}) %all-reduce.12.cloned.1.call-update) | async-done | bytes 524304
  (264 shorter events, 69.2 us)
Async XLA Ops:
  469.8 6.1 copy-start.32
  469.8 8.9 copy-start.8
  469.8 8.9 copy-start.29
  473.9 16.4 collective-permute-start
  477.3 12.9 copy-start.33
  478.7 11.6 copy-start.30
  827.8 6.1 copy-start.32
  827.8 8.9 copy-start.8
  827.8 8.9 copy-start.29
  831.9 16.4 collective-permute-start
  835.4 12.9 copy-start.33
  836.7 11.6 copy-start.30
  852.5 115.0 %copy-start.10 = (f32[1,2048]{1,0:T(1,128)}, f32[1,2048]{1,0:T(1,128)S(1)}, u32[]{:S(2)}) copy-start(f32[1,2048]{1,0:T(1,128)S(1)} %get-tuple-element.1468) | copy-start | bytes 24580 | tf_op jit(solution)/shard_map/while
  852.5 505.8 %all-reduce.14.cloned.1.call-start = ((), (), s32[]{:S(2)}) async-start(), calls=%async_computation.1 | async-start | bytes 262144 | tf_op jit(solution)/shard_map/while
  976.3 387.8 %copy-start.28 = (f32[256]{0:T(256)S(1)}, f32[256]{0:T(256)}, u32[]{:S(2)}) copy-start(f32[256]{0:T(256)} %copy-done.27) | copy-start | bytes 3076 | tf_op jit(solution)/shard_map/while
  976.3 389.3 %copy-start.11 = (f32[1,2048]{1,0:T(1,128)S(1)}, f32[1,2048]{1,0:T(1,128)}, u32[]{:S(2)}) copy-start(f32[1,2048]{1,0:T(1,128)} %copy-done.10) | copy-start | bytes 24580 | tf_op jit(solution)/shard_map/while
  976.3 389.3 %copy-start.16 = (f32[256]{0:T(256)S(1)}, f32[256]{0:T(256)}, u32[]{:S(2)}) copy-start(f32[256]{0:T(256)} %copy-done.15) | copy-start | bytes 3076 | tf_op jit(solution)/shard_map/while
  976.3 389.3 %copy-start.20 = (f32[256]{0:T(256)S(1)}, f32[256]{0:T(256)}, u32[]{:S(2)}) copy-start(f32[256]{0:T(256)} %copy-done.19) | copy-start | bytes 3076 | tf_op jit(solution)/shard_map/while
  976.3 389.3 %copy-start.35 = (f32[1,256,1]{1,2,0:T(1,128)S(1)}, f32[1,256,1]{1,2,0:T(1,128)}, u32[]{:S(2)}) copy-start(f32[1,256,1]{1,2,0:T(1,128)} %get-tuple-element.1327) | copy-start | bytes 3076 | tf_op jit(solution)/shard_map/while
  1365.6 3.2 copy-start.26
  1365.6 3.2 copy-start.12
  1368.8 3.6 copy-start
  1368.8 3.6 copy-start.14
  1370.5 2.7 copy-start.13
  1370.5 14.5 collective-permute-start.1
  1376.1 8.9 copy-start.37
  1376.2 8.9 copy-start.22
  1386.0 121.5 %copy-start.10 = (f32[1,2048]{1,0:T(1,128)}, f32[1,2048]{1,0:T(1,128)S(1)}, u32[]{:S(2)}) copy-start(f32[1,2048]{1,0:T(1,128)S(1)} %get-tuple-element.1468) | copy-start | bytes 24580 | tf_op jit(solution)/shard_map/while
  1386.0 512.7 %all-reduce.14.cloned.1.call-start = ((), (), s32[]{:S(2)}) async-start(), calls=%async_computation.1 | async-start | bytes 262144 | tf_op jit(solution)/shard_map/while
  1516.3 388.3 %copy-start.28 = (f32[256]{0:T(256)S(1)}, f32[256]{0:T(256)}, u32[]{:S(2)}) copy-start(f32[256]{0:T(256)} %copy-done.27) | copy-start | bytes 3076 | tf_op jit(solution)/shard_map/while
  1516.3 389.7 %copy-start.11 = (f32[1,2048]{1,0:T(1,128)S(1)}, f32[1,2048]{1,0:T(1,128)}, u32[]{:S(2)}) copy-start(f32[1,2048]{1,0:T(1,128)} %copy-done.10) | copy-start | bytes 24580 | tf_op jit(solution)/shard_map/while
  1516.3 389.7 %copy-start.16 = (f32[256]{0:T(256)S(1)}, f32[256]{0:T(256)}, u32[]{:S(2)}) copy-start(f32[256]{0:T(256)} %copy-done.15) | copy-start | bytes 3076 | tf_op jit(solution)/shard_map/while
  1516.3 389.8 %copy-start.20 = (f32[256]{0:T(256)S(1)}, f32[256]{0:T(256)}, u32[]{:S(2)}) copy-start(f32[256]{0:T(256)} %copy-done.19) | copy-start | bytes 3076 | tf_op jit(solution)/shard_map/while
  1516.3 389.8 %copy-start.35 = (f32[1,256,1]{1,2,0:T(1,128)S(1)}, f32[1,256,1]{1,2,0:T(1,128)}, u32[]{:S(2)}) copy-start(f32[1,256,1]{1,2,0:T(1,128)} %get-tuple-element.1327) | copy-start | bytes 3076 | tf_op jit(solution)/shard_map/while
  1906.1 3.2 copy-start.26
  1906.1 3.2 copy-start.12
  1909.2 3.6 copy-start
  1909.2 3.6 copy-start.14
  1911.0 14.5 collective-permute-start.1
  1916.6 8.9 copy-start.37
  1916.6 8.9 copy-start.22
  1926.5 2.9 copy-start.43
  1926.5 426.9 %all-reduce.12.cloned.1.call-start = ((), (), s32[]{:S(2)}) async-start(), calls=%async_computation | async-start | bytes 1048576
  1928.7 4.0 copy-start.23
  1928.7 120.5 %copy-start.2 = (f32[2048,256]{1,0:T(8,128)S(1)}, f32[2048,256]{1,0:T(8,128)}, u32[]{:S(2)}) copy-start(f32[2048,256]{1,0:T(8,128)} %get-tuple-element.893) | copy-start | bytes 6291460
  1932.7 420.7 %copy-start.24 = (bf16[1,2048,4]{1,2,0:T(4,128)(2,1)S(1)}, bf16[1,2048,4]{1,2,0:T(4,128)(2,1)}, u32[]{:S(2)}) copy-start(bf16[1,2048,4]{1,2,0:T(4,128)(2,1)} %param.19) | copy-start | bytes 49156
  1932.7 421.6 %copy-start.42 = (f32[4]{0:T(128)S(1)}, f32[4]{0:T(128)}, u32[]{:S(2)}) copy-start(f32[4]{0:T(128)} %copy-done.41) | copy-start | bytes 52
  1932.7 421.6 %copy-start.39 = (f32[4]{0:T(128)S(1)}, f32[4]{0:T(128)}, u32[]{:S(2)}) copy-start(f32[4]{0:T(128)} %copy-done.38) | copy-start | bytes 52
  (37 other events, 49.1 us)
Sparse Core Ops, SparseCore 0:
  966.8 391.4 all-reduce.13
  1506.7 391.9 all-reduce.13
Sparse Core Ops, SparseCore 1:
  1929.5 423.8 all-reduce.11
where the time goes:
time: 2370 us; the launch traced here: 2360 us
  blocking collectives  1110 us (47%)
  waiting for transfers between devices  1100 us (46%)
  matrix products  46.5 us (2%)
  other arithmetic  44 us (2%)
  local copies, waits for them, and re-layouts  34.1 us (1%)
    while x4, waiting for transfers between devices  764 us
    while x2, blocking collectives  437 us
    unnamed x2, waiting for transfers between devices  303 us
    all_gather x2, blocking collectives, backward_tick(): dmixed_all = lax.all_gather(dmixed, 'dp', axis=0, tiled=True)  221 us
    all_gather x2, blocking collectives, forward_layer(): slot_all = lax.all_gather(slot_rows, 'dp', axis=0, tiled=True)  214 us
    all_gather x1, blocking collectives, shards(): columns = lax.all_gather(local_cols, 'dp', axis=1, tiled=True)  120 us
    psum x1, blocking collectives, shards(): gain_total = lax.psum(gain_acc, 'dp')  116 us
  transfers between devices with their start and end apart: 7, of which 7 were waited for; matrix products, arithmetic and copies ran while one was open for 2% of the time, Pallas kernels for 0%

commit v1 on v0

v1 whole, which is shorter than its diff:
```python
import jax
import jax.numpy as jnp
from jax import lax
from jax.sharding import Mesh
from jax.sharding import PartitionSpec as P

EPSILON = 1e-06
BF = jnp.bfloat16
F32 = jnp.float32
AXES = ("section", "zh", "y", "x")
DP = ("zh", "y", "x")


def dot_last(left_side, right_side):
    return lax.dot_general(
        left_side, right_side, (((1,), (1,)), ((), ())), preferred_element_type=F32
    )


def dot_rows(left_side, right_side):
    return lax.dot_general(
        left_side, right_side, (((0,), (0,)), ((), ())), preferred_element_type=F32
    )


def dot_plain(left_side, right_side):
    return jnp.dot(left_side, right_side, preferred_element_type=F32)


def split_wide(value):
    high = lax.reduce_precision(value, 8, 7)
    return high.astype(BF), (value - high).astype(BF)


def exchange(chunks, axes):
    return lax.all_to_all(chunks, axes, 0, 0, tiled=True)


def gather(rows, axes):
    count = lax.axis_size(axes)
    return exchange(jnp.broadcast_to(rows[None], (count,) + rows.shape), axes)


def section_shift(block, distance):
    sections = lax.axis_size("section")
    route = [(i, i + distance) for i in range(sections) if 0 <= i + distance < sections]
    return lax.ppermute(block, "section", route)


def front(section_in, gain_row, columns, scale_val):
    wide = section_in.astype(F32)
    inverse = lax.rsqrt(jnp.mean(wide * wide, axis=-1, keepdims=True) + EPSILON)
    hidden = (wide * inverse * gain_row).astype(BF)
    hidden_f = hidden.astype(F32)
    product = dot_last(hidden, columns)
    inv_len = lax.rsqrt(jnp.sum(hidden_f * hidden_f, axis=-1, keepdims=True) + EPSILON)
    logits = scale_val * product * inv_len
    expo = jnp.exp(logits)
    first = expo[:, :1]
    norm = jnp.sum(expo, axis=-1, keepdims=True)
    spread = first / jnp.sum(first, axis=0, keepdims=True)
    slot = dot_rows(spread.astype(BF), hidden).astype(BF)
    return dict(
        wide=wide,
        inverse=inverse,
        hidden=hidden,
        inv_len=inv_len,
        logits=logits,
        prob=expo / norm,
        combine=first / norm,
        spread=spread,
        slot=slot,
    )


def mix_upstream(combine, upstream):
    high, low = split_wide(combine)
    pair = dot_rows(jnp.concatenate([high, low], axis=1), upstream)
    return (pair[:1] + pair[1:]).astype(BF)


def back(saved, gain_row, columns, scale_val, upstream, slot_out, slot_grad):
    combine = saved["combine"]
    spread = saved["spread"]
    hidden = saved["hidden"]
    dcombine = dot_last(upstream, slot_out)
    dspread = dot_last(hidden, slot_grad).astype(BF).astype(F32)
    first_term = spread * (dspread - jnp.sum(dspread * spread, axis=0, keepdims=True))
    mixed = combine * dcombine
    is_first = lax.broadcasted_iota(jnp.int32, saved["prob"].shape, 1) == 0
    dlogits = jnp.where(is_first, mixed + first_term, 0.0) - saved["prob"] * mixed
    dproduct = (dlogits * scale_val * saved["inv_len"]).astype(BF)
    pull = jnp.sum(dlogits * saved["logits"], axis=-1, keepdims=True)
    pull = pull * saved["inv_len"] * saved["inv_len"]
    spread_bf = spread.astype(BF).astype(F32)
    dhidden = (
        spread_bf * slot_grad.astype(F32)
        - hidden.astype(F32) * pull
        + dot_plain(dproduct, columns)
    )
    scaled = saved["wide"] * saved["inverse"]
    gain_part = jnp.sum(dhidden * scaled, axis=0, keepdims=True)
    through = dhidden * gain_row
    mean_term = jnp.mean(through * scaled, axis=-1, keepdims=True)
    dinput = saved["inverse"] * (through - scaled * mean_term)
    grads = (upstream.astype(F32) + dinput).astype(BF)
    router_part = dot_rows(dproduct, hidden)
    return grads, router_part, gain_part


def shards(
    tokens,
    cotangent,
    inflow,
    backflow,
    norm_gain,
    slot_scale,
    router_weight,
    expert_in,
    expert_back,
):
    section_index = lax.axis_index("section")
    is_first = section_index == 0
    is_last = section_index == lax.axis_size("section") - 1
    group = lax.axis_size(DP)
    width = tokens.shape[3]
    gain_row = norm_gain
    scale_val = slot_scale[0]
    first_weight = expert_in[0]
    second_weight = expert_back[0]
    weights = router_weight[0].T.astype(F32)
    weight_inv = lax.rsqrt(jnp.sum(weights * weights, axis=1, keepdims=True) + EPSILON)
    local_cols = (weights * weight_inv).astype(BF)

    start_in = jnp.where(is_first, tokens[0, 0], inflow[0, 0])
    sent_in = section_shift(start_in, 1)
    columns = gather(local_cols, DP).reshape(-1, width)

    early = front(start_in, gain_row, columns, scale_val)
    slot_early = gather(early["slot"], DP).reshape(group, width)
    pre_early = dot_plain(slot_early, first_weight)
    act_early, pull_early = jax.vjp(jax.nn.gelu, pre_early)
    act_early = act_early.astype(BF)
    part = dot_plain(act_early, second_weight)

    sums_early = exchange(part.reshape(group, 1, width), DP).reshape(group, width).sum(0)
    out_early = sums_early[None].astype(BF)
    flat_comb = early["combine"].reshape(1, -1)
    moved = section_shift(jnp.concatenate([out_early.astype(F32), flat_comb], axis=1), 1)
    out_before = moved[:, :width].astype(BF)
    comb_before = moved[:, width:].reshape(-1, 1)

    relayed = (sent_in.astype(F32) + comb_before * out_before.astype(F32)).astype(BF)
    late_in = jnp.where(is_first, tokens[1, 0], relayed)
    late = front(late_in, gain_row, columns, scale_val)
    late_up = jnp.where(is_last, cotangent[1, 0], backflow[0, 0])
    dmixed_late = mix_upstream(late["combine"], late_up)
    pair = jnp.concatenate([late["slot"], dmixed_late], axis=0)
    pairs = gather(pair, DP).reshape(group, 2, width)
    slot_late = pairs[:, 0]
    dmixed_late_all = pairs[:, 1]
    pre_late = dot_plain(slot_late, first_weight)
    act_late, pull_late = jax.vjp(jax.nn.gelu, pre_late)
    act_late = act_late.astype(BF)
    pre_grad_late = pull_late(dot_last(dmixed_late_all, second_weight))[0].astype(BF)
    part_out = dot_plain(act_late, second_weight)
    part_grad = dot_last(pre_grad_late, first_weight)
    parts = jnp.stack([part_out, part_grad], axis=1)
    sums = exchange(parts, DP).reshape(group, 2, width).sum(0)
    out_late = sums[:1].astype(BF)
    slot_grad_late = sums[1:].astype(BF)
    grads_late, router_late, gain_late = back(
        late, gain_row, columns, scale_val, late_up, out_late, slot_grad_late
    )

    dmixed_last = mix_upstream(early["combine"], cotangent[0, 0])
    dmixed_before = mix_upstream(comb_before, grads_late)
    moved_back = section_shift(dmixed_before, -1)
    sent_grads = section_shift(grads_late, -1)
    dmixed_early = jnp.where(is_last, dmixed_last, moved_back)
    dmixed_early_all = gather(dmixed_early, DP).reshape(group, width)
    pre_grad_early = pull_early(dot_last(dmixed_early_all, second_weight))[0].astype(BF)
    part_early = dot_last(pre_grad_early, first_weight)
    slot_grad_early = (
        exchange(part_early.reshape(group, 1, width), DP).reshape(group, width).sum(0)
    ).astype(BF)[None]
    early_up = jnp.where(is_last, cotangent[0, 0], sent_grads)
    grads_early, router_early, gain_early = back(
        early, gain_row, columns, scale_val, early_up, out_early, slot_grad_early
    )

    router_sum = (router_late + router_early).astype(BF).reshape(group, -1, width)
    gain_high, gain_low = split_wide(gain_late + gain_early)
    gain_pair = jnp.broadcast_to(
        jnp.concatenate([gain_high, gain_low], axis=0)[None], (group, 2, width)
    )
    finals = exchange(jnp.concatenate([router_sum, gain_pair], axis=1), DP)
    finals = finals.reshape(group, -1, width).astype(F32).sum(0)
    local = router_weight.shape[2]
    gain_total = finals[local : local + 1] + finals[local + 1 :]
    pulled = finals[:local]
    dots = jnp.sum(pulled * weights, axis=1, keepdims=True)
    router_grad = weight_inv * (pulled - weights * (dots * weight_inv * weight_inv))

    first_grad = dot_rows(
        jnp.concatenate([slot_early, slot_late], axis=0),
        jnp.concatenate([pre_grad_early, pre_grad_late], axis=0),
    )
    second_grad = dot_rows(
        jnp.concatenate([act_early, act_late], axis=0),
        jnp.concatenate([dmixed_early_all, dmixed_late_all], axis=0),
    )
    return (
        jnp.stack([grads_early, grads_late])[None, :, None],
        jnp.stack([out_early, out_late])[None],
        jnp.stack([slot_grad_early, slot_grad_late])[None],
        first_grad.astype(BF)[None],
        second_grad.astype(BF)[None],
        router_grad.astype(BF).T[None],
        gain_total,
    )


def solution(mesh):
    fine = Mesh(mesh.devices.reshape(mesh.shape["section"], 2, 4, 4), AXES)
    in_specs = (
        P(None, DP, None, None),
        P(None, DP, None, None),
        P("section", DP, None, None),
        P("section", DP, None, None),
        P("section", None),
        P("section"),
        P("section", None, DP),
        P("section", None, DP),
        P("section", DP, None),
    )
    out_specs = (
        P("section", None, DP, None, None),
        P("section", None, DP, None),
        P("section", None, DP, None),
        P("section", None, DP),
        P("section", DP, None),
        P("section", None, DP),
        P("section", None),
    )
    return jax.shard_map(shards, mesh=fine, in_specs=in_specs, out_specs=out_specs, check_vma=False)
```

time: 2370 us -> 254 us (0.11)
  blocking collectives: 1110 us -> 56.5 us
  waiting for transfers between devices: 1100 us -> 65.1 us
  starting transfers between devices: 7.64 us -> 45.8 us
    while x4 -> x0, waiting for transfers between devices: 764 us -> none
    all_gather x5 -> x0, blocking collectives: 555 us -> none  [the longest x2 221 us: backward_tick(): dmixed_all = lax.all_gather(dmixed, 'dp', axis=0, tiled=True)]
    while x2 -> x0, blocking collectives: 437 us -> none
    unnamed x2 -> x0, waiting for transfers between devices: 303 us -> none
    psum x1 -> x0, blocking collectives: 116 us -> none  [shards(): gain_total = lax.psum(gain_acc, 'dp')]
    all_to_all x0 -> x5, waiting for transfers between devices: none -> 62.5 us  [exchange(): return lax.all_to_all(chunks, axes, 0, 0, tiled=True)]
    all_to_all x0 -> x3, blocking collectives: none -> 56.5 us  [exchange(): return lax.all_to_all(chunks, axes, 0, 0, tiled=True)]
    all_to_all x0 -> x5, starting transfers between devices: none -> 38 us  [exchange(): return lax.all_to_all(chunks, axes, 0, 0, tiled=True)]
  transfers between devices with their start and end apart: 7 -> 9, of which waited for: 7 -> 7; matrix products, arithmetic and copies ran while one was open for 2% -> 11% of each run, Pallas kernels for 0% -> 0%
where the time goes in v1:
time: 254 us; the launch traced here: 253 us
  waiting for transfers between devices  65.1 us (26%)
  blocking collectives  56.5 us (22%)
  starting transfers between devices  45.8 us (18%)
  other arithmetic  35.9 us (14%)
  matrix products  28.8 us (11%)
  local copies, waits for them, and re-layouts  18.2 us (7%)
    all_to_all x5, waiting for transfers between devices, exchange(): return lax.all_to_all(chunks, axes, 0, 0, tiled=True)  62.5 us
    all_to_all x3, blocking collectives, exchange(): return lax.all_to_all(chunks, axes, 0, 0, tiled=True)  56.5 us
    all_to_all x5, starting transfers between devices, exchange(): return lax.all_to_all(chunks, axes, 0, 0, tiled=True)  38 us
    dot_general x9, matrix products, dot_rows(): lax.dot_general(left_side, right_side, (((0,), (0,)), ((), ())), preferre...  11 us
    dot_general x10, matrix products, dot_last(): lax.dot_general(left_side, right_side, (((1,), (1,)), ((), ())), preferre...  10 us
    unnamed x152, local copies, waits for them, and re-layouts  8.13 us
    ppermute x4, starting transfers between devices, section_shift(): return lax.ppermute(block, 'section', route)  7.83 us
    dot_general x6, matrix products, dot_plain(): return jnp.dot(left_side, right_side, preferred_element_type=F32)  7.78 us
  transfers between devices with their start and end apart: 9, of which 7 were waited for; matrix products, arithmetic and copies ran while one was open for 11% of the time, Pallas kernels for 0%

profile of v1, /device:TPU:32, one launch (start us, length us, event | category | flops | bytes accessed | tf_op | source)
XLA Modules:
  0.0 252.5 jit_solution(15095885081347116111)
XLA Ops:
  4.6 13.2 %all-to-all-start = ((bf16[32,4,2048]{2,1,0:T(4,128)(2,1)}), bf16[32,4,2048]{2,1,0:T(4,128)(2,1)S(1)}, u32[]{:S(2)}, u32[]{:S(2)}) async-start(bf16[32,4,2048]{2,1,0:T(4,128)(2,1)} %broadcast_in_dim.50), calls=%async_computation | async-start | bytes 1048576 | tf_op jit(solution)/shard_map/all_to_all | solution.py:36
  18.5 2.6 %fusion.18 = (f32[256]{0:T(256)S(1)}, bf16[1,1,256,2048]{3,2,1,0:T(8,128)(2,1)}) fusion(bf16[1,1,256,2048]{3,2,1,0:T(8,128)(2,1)S(1)} %copy-done.17, bf16[2,1,256,2048]{3,2,1,0:T(8,128)(2,1)} %param.9, pred[]{:T(512)S(6)} %eq.14), kind=kLoop, calls=%fused_computation.35 | loop fusion | flops 2096896 | bytes 3146753 | tf_op jit(solution)/shard_map/reduce_sum | solution.py:52
  21.1 1.7 fusion.19
  23.3 15.6 %all-to-all-done = bf16[32,4,2048]{2,1,0:T(4,128)(2,1)S(1)} async-done(((bf16[32,4,2048]{2,1,0:T(4,128)(2,1)}), bf16[32,4,2048]{2,1,0:T(4,128)(2,1)S(1)}, u32[]{:S(2)}, u32[]{:S(2)}) %all-to-all-start) | async-done | bytes 524320 | tf_op jit(solution)/shard_map/all_to_all | solution.py:36
  39.1 2.6 %fusion.140 = (f32[256,128]{0,1:T(8,128)S(1)}, f32[256]{0:T(256)S(1)}, f32[256,128]{0,1:T(8,128)}) fusion(f32[256]{0:T(256)S(1)} %add_rsqrt_fusion.2, bf16[128,2048]{1,0:T(8,128)(2,1)S(1)} %reshape.309, bf16[1,1,256,2048]{3,2,1,0:T(8,128)(2,1)} %get-tuple-element.52, f32[2048]{0:T(1024)S(1)} %bitcast.209, f32[256]{0:T(256)S(1)} %add_rsqrt_fusion.3, ...), kind=kOutput, calls=%fused_computation.228 | convolution fusion | flops 136412928 | bytes 1846276 | tf_op jit(solution)/shard_map/dot_general | solution.py:15
  41.7 1.1 reduce-precision_convert_fusion.2
  42.8 1.1 convert_reduce_fusion.2
  44.0 1.6 fusion.56
  46.4 1.4 reduce.14
  47.9 16.3 %all_to_all.40 = bf16[32,2,1024]{2,1,0:T(2,128)(2,1)S(1)} all-to-all(bf16[32,2,1024]{2,1,0:T(2,128)(2,1)S(1)} %reshape.342), channel_id=1, replica_groups=mesh['section'=8,'zh'=2,'y'=4,'x'=4] {'zh','y','x'}, dimensions={0} | all-to-all | bytes 262144 | tf_op jit(solution)/shard_map/all_to_all | solution.py:36
  66.5 3.9 %all-to-all-start.2 = ((f32[32,1,2048]{2,1,0:T(1,128)}), f32[32,1,2048]{2,1,0:T(1,128)S(1)}, u32[]{:S(2)}, u32[]{:S(2)}) async-start(f32[32,1,2048]{2,1,0:T(1,128)} %copy.23), calls=%async_computation.2 | async-start | bytes 524288 | tf_op jit(solution)/shard_map/all_to_all | solution.py:36
  70.4 1.9 collective-permute-start
  72.4 11.0 %all-to-all-done.2 = f32[32,1,2048]{2,1,0:T(1,128)S(1)} async-done(((f32[32,1,2048]{2,1,0:T(1,128)}), f32[32,1,2048]{2,1,0:T(1,128)S(1)}, u32[]{:S(2)}, u32[]{:S(2)}) %all-to-all-start.2) | async-done | bytes 262176 | tf_op jit(solution)/shard_map/all_to_all | solution.py:36
  83.6 1.9 collective-permute-start.1
  85.5 1.7 slice_select_fusion.1
  87.2 1.5 collective-permute-done.1
  88.7 1.9 fusion.28
  93.0 1.2 convert_reduce_fusion.1
  94.9 23.5 %all_to_all.41 = bf16[32,2,2048]{2,1,0:T(2,128)(2,1)S(1)} all-to-all(bf16[32,2,2048]{2,1,0:T(2,128)(2,1)S(1)} %broadcast_in_dim.100), channel_id=1, replica_groups=mesh['section'=8,'zh'=2,'y'=4,'x'=4] {'zh','y','x'}, dimensions={0} | all-to-all | bytes 524288 | tf_op jit(solution)/shard_map/all_to_all | solution.py:36
  121.2 1.2 copy.26
  122.4 4.9 %all-to-all-start.4 = ((f32[32,2,2048]{2,1,0:T(2,128)}), f32[32,2,2048]{2,1,0:T(2,128)}, u32[]{:S(2)}, u32[]{:S(2)}) async-start(f32[32,2,2048]{2,1,0:T(2,128)} %copy.26), calls=%async_computation.4 | async-start | bytes 1048576 | tf_op jit(solution)/shard_map/all_to_all | solution.py:36
  128.0 14.6 %all-to-all-done.4 = f32[32,2,2048]{2,1,0:T(2,128)} async-done(((f32[32,2,2048]{2,1,0:T(2,128)}), f32[32,2,2048]{2,1,0:T(2,128)}, u32[]{:S(2)}, u32[]{:S(2)}) %all-to-all-start.4) | async-done | bytes 524320 | tf_op jit(solution)/shard_map/all_to_all | solution.py:36
  142.7 1.2 reduce_sum.208
  146.8 1.8 fusion.27
  150.5 1.9 collective-permute-start.3
  154.7 2.3 reduce.15
  157.8 16.7 %all_to_all.42 = bf16[32,2,1024]{2,1,0:T(2,128)(2,1)S(1)} all-to-all(bf16[32,2,1024]{2,1,0:T(2,128)(2,1)} %reshape.344), channel_id=1, replica_groups=mesh['section'=8,'zh'=2,'y'=4,'x'=4] {'zh','y','x'}, dimensions={0} | all-to-all | bytes 262144 | tf_op jit(solution)/shard_map/all_to_all | solution.py:36
  176.3 1.2 fusion.71
  179.5 4.6 %all-to-all-start.6 = ((f32[32,1,2048]{2,1,0:T(1,128)}), f32[32,1,2048]{2,1,0:T(1,128)}, u32[]{:S(2)}, u32[]{:S(2)}) async-start(f32[32,1,2048]{2,1,0:T(1,128)} %copy.27), calls=%async_computation.6 | async-start | bytes 524288 | tf_op jit(solution)/shard_map/all_to_all | solution.py:36
  184.1 1.2 mul.512
  185.3 1.3 reshape.330
  186.5 1.3 convert_element_type.318
  187.8 2.1 collective-permute-start.2
  189.9 2.0 fusion.132
  191.9 6.2 %all-to-all-done.6 = f32[32,1,2048]{2,1,0:T(1,128)} async-done(((f32[32,1,2048]{2,1,0:T(1,128)}), f32[32,1,2048]{2,1,0:T(1,128)}, u32[]{:S(2)}, u32[]{:S(2)}) %all-to-all-start.6) | async-done | bytes 262176 | tf_op jit(solution)/shard_map/all_to_all | solution.py:36
  198.1 1.1 reduce_sum.212
  199.9 1.8 fusion.134
  202.9 1.9 multiply_add_fusion
  205.1 4.3 %fusion.17 = (f32[2048]{0:T(1024)S(1)}, f32[256]{0:T(256)}, f32[256,2048]{1,0:T(8,128)}) fusion(f32[256]{0:T(256)S(1)} %copy-done.51, bf16[1,1,256,2048]{3,2,1,0:T(8,128)(2,1)} %get-tuple-element.52, f32[2048]{0:T(1024)S(1)} %bitcast.214, bf16[128,2048]{1,0:T(8,128)(2,1)S(1)} %copy-done.13, f32[256]{0:T(256)S(1)} %copy-done.67, f32[]{:T(128)} %bitcast.197, ...), kind=kOutput, calls=%fused_computation.34 | convolution fusion | flops 141784832 | bytes 3833988 | tf_op jit(solution)/shard_map/dot_general | solution.py:27
  209.4 1.8 fusion.10
  211.6 1.5 pad_maximum_fusion
  213.1 11.4 %all-to-all-start.7 = ((bf16[32,6,2048]{2,1,0:T(8,128)(2,1)}), bf16[32,6,2048]{2,1,0:T(8,128)(2,1)S(1)}, u32[]{:S(2)}, u32[]{:S(2)}) async-start(bf16[32,6,2048]{2,1,0:T(8,128)(2,1)} %pad_maximum_fusion), calls=%async_computation.7 | async-start | bytes 2097152 | tf_op jit(solution)/shard_map/all_to_all | solution.py:36
  224.5 1.5 maximum_bitcast_fusion.1
  226.0 2.3 fusion.9
  228.4 2.2 fusion.8
  231.2 3.0 %fusion.37 = bf16[1,256,2048]{2,1,0:T(8,128)(2,1)S(1)} fusion(f32[256,2048]{1,0:T(8,128)} %get-tuple-element.79, f32[256]{0:T(256)S(1)} %broadcast_multiply_fusion, f32[2048]{0:T(1024)S(1)} %bitcast.216, f32[256]{0:T(256)S(1)} %copy-done.52, bf16[256,2048]{1,0:T(8,128)(2,1)} %collective-permute-done.2, bf16[2,1,256,2048]{3,2,1,0:T(8,128)(2,1)S(1)} %copy-done.9, ...), kind=kLoop, calls=%fused_computation.62 | loop fusion | flops 5242880 | bytes 6301697 | tf_op jit(solution)/shard_map/stack | solution.py:214
  234.2 1.5 maximum_bitcast_fusion
  235.8 15.1 %all-to-all-done.7 = bf16[32,6,2048]{2,1,0:T(8,128)(2,1)S(1)} async-done(((bf16[32,6,2048]{2,1,0:T(8,128)(2,1)}), bf16[32,6,2048]{2,1,0:T(8,128)(2,1)S(1)}, u32[]{:S(2)}, u32[]{:S(2)}) %all-to-all-start.7) | async-done | bytes 786464 | tf_op jit(solution)/shard_map/all_to_all | solution.py:36
  (235 shorter events, 30.5 us)
Async XLA Ops:
  0.6 63.7 %copy-start = (bf16[1,2048,256]{2,1,0:T(8,128)(2,1)S(1)}, bf16[1,2048,256]{2,1,0:T(8,128)(2,1)}, u32[]{:S(2)}) copy-start(bf16[1,2048,256]{2,1,0:T(8,128)(2,1)} %param.16) | copy-start | bytes 3145732
  0.6 17.8 %copy-start.17 = (bf16[1,1,256,2048]{3,2,1,0:T(8,128)(2,1)S(1)}, bf16[1,1,256,2048]{3,2,1,0:T(8,128)(2,1)}, u32[]{:S(2)}) copy-start(bf16[1,1,256,2048]{3,2,1,0:T(8,128)(2,1)} %param.11) | copy-start | bytes 3145732
  4.6 16.5 %copy-start.23 = (f32[1,2048]{1,0:T(1,128)S(1)}, f32[1,2048]{1,0:T(1,128)}, u32[]{:S(2)}) copy-start(f32[1,2048]{1,0:T(1,128)} %param.13) | copy-start | bytes 24580
  4.6 34.3 %all-to-all-start = ((bf16[32,4,2048]{2,1,0:T(4,128)(2,1)}), bf16[32,4,2048]{2,1,0:T(4,128)(2,1)S(1)}, u32[]{:S(2)}, u32[]{:S(2)}) async-start(bf16[32,4,2048]{2,1,0:T(4,128)(2,1)} %broadcast_in_dim.50), calls=%async_computation | async-start | bytes 1048576 | tf_op jit(solution)/shard_map/all_to_all | solution.py:36
  21.1 22.9 %copy-start.50 = (f32[256]{0:T(256)}, f32[256]{0:T(256)S(1)}, u32[]{:S(2)}) copy-start(f32[256]{0:T(256)S(1)} %add_rsqrt_fusion.3) | copy-start | bytes 3076
  23.3 19.5 %copy-start.66 = (f32[256]{0:T(256)}, f32[256]{0:T(256)S(1)}, u32[]{:S(2)}) copy-start(f32[256]{0:T(256)S(1)} %add_rsqrt_fusion.2) | copy-start | bytes 3076
  42.8 40.7 %copy-start.47 = (f32[256,1]{0,1:T(1,128)}, f32[256,1]{0,1:T(1,128)S(1)}, u32[]{:S(2)}) copy-start(f32[256,1]{0,1:T(1,128)S(1)} %get-tuple-element.42) | copy-start | bytes 3076
  45.6 19.6 %copy-start.1 = (bf16[1,256,2048]{2,1,0:T(8,128)(2,1)S(1)}, bf16[1,256,2048]{2,1,0:T(8,128)(2,1)}, u32[]{:S(2)}) copy-start(bf16[1,256,2048]{2,1,0:T(8,128)(2,1)} %param.17) | copy-start | bytes 3145732
  66.5 16.8 %all-to-all-start.2 = ((f32[32,1,2048]{2,1,0:T(1,128)}), f32[32,1,2048]{2,1,0:T(1,128)S(1)}, u32[]{:S(2)}, u32[]{:S(2)}) async-start(f32[32,1,2048]{2,1,0:T(1,128)} %copy.23), calls=%async_computation.2 | async-start | bytes 524288 | tf_op jit(solution)/shard_map/all_to_all | solution.py:36
  70.4 18.3 %collective-permute-start = (bf16[256,2048]{1,0:T(8,128)(2,1)}, bf16[256,2048]{1,0:T(8,128)(2,1)S(1)}, u32[]{:S(2)}, u32[]{:S(2)}) collective-permute-start(bf16[256,2048]{1,0:T(8,128)(2,1)} %bitcast.3), channel_id=1, source_target_pairs={{0,32},{32,64},{64,96},{96,128},{128,160},{160,192},{192,224},{1,3... | collective-permute-start | bytes 3145736 | tf_op jit(solution)/shard_map/ppermute | solution.py:47
  83.6 7.1 %copy-start.28 = (bf16[2048]{0:T(1024)(128)(2,1)}, bf16[2048]{0:T(1024)(128)(2,1)S(1)}, u32[]{:S(2)}) copy-start(bf16[2048]{0:T(1024)(128)(2,1)S(1)} %reduce_sum.202) | copy-start | bytes 12292
  83.6 5.1 %collective-permute-start.1 = (f32[1,2304]{1,0:T(1,128)S(1)}, f32[1,2304]{1,0:T(1,128)S(1)}, u32[]{:S(2)}, u32[]{:S(2)}) collective-permute-start(f32[1,2304]{1,0:T(1,128)S(1)} %pad_maximum_fusion.2), channel_id=1, source_target_pairs={{0,32},{32,64},{64,96},{96,128},{128,160},{160,192},{192,224},{1,3... | collective-permute-start | bytes 27656 | tf_op jit(solution)/shard_map/ppermute | solution.py:47
  94.7 25.2 %copy-start.2 = (bf16[1,256,2048]{2,1,0:T(8,128)(2,1)S(1)}, bf16[1,256,2048]{2,1,0:T(8,128)(2,1)}, u32[]{:S(2)}) copy-start(bf16[1,256,2048]{2,1,0:T(8,128)(2,1)} %param.17) | copy-start | bytes 3145732
  120.8 6.6 %copy-start.48 = (f32[256,1]{0,1:T(1,128)S(1)}, f32[256,1]{0,1:T(1,128)}, u32[]{:S(2)}) copy-start(f32[256,1]{0,1:T(1,128)} %copy-done.47) | copy-start | bytes 3076
  120.8 6.6 %copy-start.71 = (bf16[256]{0:T(256)(128)(2,1)S(1)}, bf16[256]{0:T(256)(128)(2,1)}, u32[]{:S(2)}) copy-start(bf16[256]{0:T(256)(128)(2,1)} %get-tuple-element.43) | copy-start | bytes 1540
  121.1 23.8 %copy-start.35 = (f32[256,1]{0,1:T(1,128)S(1)}, f32[256,1]{0,1:T(1,128)}, u32[]{:S(2)}) copy-start(f32[256,1]{0,1:T(1,128)} %copy-done.34) | copy-start | bytes 3076
  121.1 25.0 %copy-start.46 = (f32[256,1]{0,1:T(1,128)S(1)}, f32[256,1]{0,1:T(1,128)}, u32[]{:S(2)}) copy-start(f32[256,1]{0,1:T(1,128)} %copy-done.45) | copy-start | bytes 3076
  122.4 24.2 %copy-start.33 = (f32[256]{0:T(256)S(1)}, f32[256]{0:T(256)}, u32[]{:S(2)}) copy-start(f32[256]{0:T(256)} %copy-done.32) | copy-start | bytes 3076
  122.4 24.3 %copy-start.42 = (f32[256]{0:T(256)S(1)}, f32[256]{0:T(256)}, u32[]{:S(2)}) copy-start(f32[256]{0:T(256)} %copy-done.41) | copy-start | bytes 3076
  122.4 24.4 %copy-start.24 = (f32[1,2048]{1,0:T(1,128)S(1)}, f32[1,2048]{1,0:T(1,128)}, u32[]{:S(2)}) copy-start(f32[1,2048]{1,0:T(1,128)} %param.13) | copy-start | bytes 24580
  122.4 24.4 %copy-start.38 = (f32[256]{0:T(256)S(1)}, f32[256]{0:T(256)}, u32[]{:S(2)}) copy-start(f32[256]{0:T(256)} %copy-done.37) | copy-start | bytes 3076
  122.4 24.4 %copy-start.40 = (f32[256]{0:T(256)S(1)}, f32[256]{0:T(256)}, u32[]{:S(2)}) copy-start(f32[256]{0:T(256)} %copy-done.39) | copy-start | bytes 3076
  122.4 20.3 %all-to-all-start.4 = ((f32[32,2,2048]{2,1,0:T(2,128)}), f32[32,2,2048]{2,1,0:T(2,128)}, u32[]{:S(2)}, u32[]{:S(2)}) async-start(f32[32,2,2048]{2,1,0:T(2,128)} %copy.26), calls=%async_computation.4 | async-start | bytes 1048576 | tf_op jit(solution)/shard_map/all_to_all | solution.py:36
  127.4 21.2 %copy-start.57 = (pred[128]{0:T(512)(128)(4,1)}, pred[128]{0:T(512)(128)(4,1)S(1)}, u32[]{:S(2)}) copy-start(pred[128]{0:T(512)(128)(4,1)S(1)} %iota_compare_fusion) | copy-start | bytes 388
  149.3 27.0 %copy-start.3 = (bf16[1,256,2048]{2,1,0:T(8,128)(2,1)S(1)}, bf16[1,256,2048]{2,1,0:T(8,128)(2,1)}, u32[]{:S(2)}) copy-start(bf16[1,256,2048]{2,1,0:T(8,128)(2,1)} %param.17) | copy-start | bytes 3145732
  150.5 3.3 %collective-permute-start.3 = (bf16[1,2048]{1,0:T(2,128)(2,1)S(1)}, bf16[1,2048]{1,0:T(2,128)(2,1)S(1)}, u32[]{:S(2)}, u32[]{:S(2)}) collective-permute-start(bf16[1,2048]{1,0:T(2,128)(2,1)S(1)} %fusion.102), channel_id=1, source_target_pairs={{32,0},{64,32},{96,64},{128,96},{160,128},{192,160},{224,192},{33,... | collective-permute-start | bytes 12296 | tf_op jit(solution)/shard_map/ppermute | solution.py:47
  178.1 9.7 %copy-start.7 = (bf16[256,2048]{1,0:T(8,128)(2,1)S(1)}, bf16[256,2048]{1,0:T(8,128)(2,1)}, u32[]{:S(2)}) copy-start(bf16[256,2048]{1,0:T(8,128)(2,1)} %copy-done.6) | copy-start | bytes 3145732
  179.5 18.6 %all-to-all-start.6 = ((f32[32,1,2048]{2,1,0:T(1,128)}), f32[32,1,2048]{2,1,0:T(1,128)}, u32[]{:S(2)}, u32[]{:S(2)}) async-start(f32[32,1,2048]{2,1,0:T(1,128)} %copy.27), calls=%async_computation.6 | async-start | bytes 524288 | tf_op jit(solution)/shard_map/all_to_all | solution.py:36
  187.8 15.1 %collective-permute-start.2 = (bf16[256,2048]{1,0:T(8,128)(2,1)S(1)}, bf16[256,2048]{1,0:T(8,128)(2,1)}, u32[]{:S(2)}, u32[]{:S(2)}) collective-permute-start(bf16[256,2048]{1,0:T(8,128)(2,1)S(1)} %copy-done.7), channel_id=1, source_target_pairs={{32,0},{64,32},{96,64},{128,96},{160,128},{192,160},{224,192},{33,... | collective-permute-start | bytes 3145736 | tf_op jit(solution)/shard_map/ppermute | solution.py:47
  191.9 9.7 %copy-start.62 = (f32[256,1]{0,1:T(1,128)S(1)}, f32[256,1]{0,1:T(1,128)}, u32[]{:S(2)}) copy-start(f32[256,1]{0,1:T(1,128)} %copy-done.61) | copy-start | bytes 3076
  191.9 11.0 %copy-start.49 = (f32[256,1]{0,1:T(1,128)S(1)}, f32[256,1]{0,1:T(1,128)}, u32[]{:S(2)}) copy-start(f32[256,1]{0,1:T(1,128)} %copy-done.47) | copy-start | bytes 3076
  191.9 11.0 %copy-start.56 = (bf16[2048,1]{0,1:T(2,128)(2,1)S(1)}, bf16[2048,1]{0,1:T(2,128)(2,1)}, u32[]{:S(2)}) copy-start(bf16[2048,1]{0,1:T(2,128)(2,1)} %reshape.330) | copy-start | bytes 12292
  199.8 5.2 %copy-start.13 = (bf16[128,2048]{1,0:T(8,128)(2,1)S(1)}, bf16[128,2048]{1,0:T(8,128)(2,1)}, u32[]{:S(2)}) copy-start(bf16[128,2048]{1,0:T(8,128)(2,1)} %copy-done.10) | copy-start | bytes 1572868
  199.8 5.2 %copy-start.25 = (f32[1,2048]{1,0:T(1,128)S(1)}, f32[1,2048]{1,0:T(1,128)}, u32[]{:S(2)}) copy-start(f32[1,2048]{1,0:T(1,128)} %param.13) | copy-start | bytes 24580
  199.8 5.2 %copy-start.51 = (f32[256]{0:T(256)S(1)}, f32[256]{0:T(256)}, u32[]{:S(2)}) copy-start(f32[256]{0:T(256)} %copy-done.50) | copy-start | bytes 3076
  199.9 5.2 %copy-start.67 = (f32[256]{0:T(256)S(1)}, f32[256]{0:T(256)}, u32[]{:S(2)}) copy-start(f32[256]{0:T(256)} %copy-done.66) | copy-start | bytes 3076
  199.9 5.2 %copy-start.72 = (f32[256]{0:T(256)S(1)}, f32[256]{0:T(256)}, u32[]{:S(2)}) copy-start(f32[256]{0:T(256)} %mul.512) | copy-start | bytes 3076
  213.1 15.3 %copy-start.15 = (bf16[32,2048]{1,0:T(8,128)(2,1)S(1)}, bf16[32,2048]{1,0:T(8,128)(2,1)}, u32[]{:S(2)}) copy-start(bf16[32,2048]{1,0:T(8,128)(2,1)} %copy-done.14) | copy-start | bytes 393220
  213.1 37.8 %all-to-all-start.7 = ((bf16[32,6,2048]{2,1,0:T(8,128)(2,1)}), bf16[32,6,2048]{2,1,0:T(8,128)(2,1)S(1)}, u32[]{:S(2)}, u32[]{:S(2)}) async-start(bf16[32,6,2048]{2,1,0:T(8,128)(2,1)} %pad_maximum_fusion), calls=%async_computation.7 | async-start | bytes 2097152 | tf_op jit(solution)/shard_map/all_to_all | solution.py:36
  224.5 6.1 %copy-start.30 = (bf16[2048]{0:T(1024)(128)(2,1)S(1)}, bf16[2048]{0:T(1024)(128)(2,1)}, u32[]{:S(2)}) copy-start(bf16[2048]{0:T(1024)(128)(2,1)} %copy-done.29) | copy-start | bytes 12292
  224.5 6.1 %copy-start.31 = (bf16[1,1,2048]{2,0,1:T(2,128)(2,1)S(1)}, bf16[1,1,2048]{2,0,1:T(2,128)(2,1)}, u32[]{:S(2)}) copy-start(bf16[1,1,2048]{2,0,1:T(2,128)(2,1)} %get-tuple-element.65) | copy-start | bytes 12292
  224.5 6.7 %copy-start.68 = (f32[256]{0:T(256)S(1)}, f32[256]{0:T(256)}, u32[]{:S(2)}) copy-start(f32[256]{0:T(256)} %get-tuple-element.36) | copy-start | bytes 3076
  224.5 6.7 %copy-start.9 = (bf16[2,1,256,2048]{3,2,1,0:T(8,128)(2,1)S(1)}, bf16[2,1,256,2048]{3,2,1,0:T(8,128)(2,1)}, u32[]{:S(2)}) copy-start(bf16[2,1,256,2048]{3,2,1,0:T(8,128)(2,1)} %param.10) | copy-start | bytes 6291460
  224.5 6.7 %copy-start.26 = (f32[1,2048]{1,0:T(1,128)S(1)}, f32[1,2048]{1,0:T(1,128)}, u32[]{:S(2)}) copy-start(f32[1,2048]{1,0:T(1,128)} %param.13) | copy-start | bytes 24580
  224.5 6.7 %copy-start.52 = (f32[256]{0:T(256)S(1)}, f32[256]{0:T(256)}, u32[]{:S(2)}) copy-start(f32[256]{0:T(256)} %copy-done.50) | copy-start | bytes 3076
  234.2 16.9 %copy-start.19 = (bf16[1,2048,4]{1,2,0:T(4,128)(2,1)S(1)}, bf16[1,2048,4]{1,2,0:T(4,128)(2,1)}, u32[]{:S(2)}) copy-start(bf16[1,2048,4]{1,2,0:T(4,128)(2,1)} %param.15) | copy-start | bytes 49156
  234.2 17.6 %copy-start.70 = (f32[4]{0:T(128)S(1)}, f32[4]{0:T(128)}, u32[]{:S(2)}) copy-start(f32[4]{0:T(128)} %copy-done.69) | copy-start | bytes 52
  234.2 17.6 %copy-start.65 = (f32[4]{0:T(128)S(1)}, f32[4]{0:T(128)}, u32[]{:S(2)}) copy-start(f32[4]{0:T(128)} %copy-done.64) | copy-start | bytes 52
  (34 other events, 84.4 us)

commit v2 on v1

v2 whole, which is shorter than its diff:
```python
import jax
import jax.numpy as jnp
from jax import lax
from jax.experimental import pallas as pl
from jax.experimental.pallas import tpu as pltpu
from jax.sharding import Mesh
from jax.sharding import PartitionSpec as P

EPSILON = 1e-06
BF = jnp.bfloat16
F32 = jnp.float32
AXES = ("section", "zh", "y", "x")
DP = ("zh", "y", "x")
LANES = 128
STEP = 16
VMEM_BYTES = 32 * 1024 * 1024


def dot_dims(left_side, right_side, left_dim, right_dim):
    return lax.dot_general(
        left_side,
        right_side,
        (((left_dim,), (right_dim,)), ((), ())),
        preferred_element_type=F32,
    )


def split_wide(value):
    high = lax.reduce_precision(value, 8, 7)
    return high.astype(BF), (value - high).astype(BF)


def exchange(chunks, axes):
    return lax.all_to_all(chunks, axes, 0, 0, tiled=True)


def gather(rows, axes):
    count = lax.axis_size(axes)
    return exchange(jnp.broadcast_to(rows[None], (count,) + rows.shape), axes)


def section_shift(block, distance):
    sections = lax.axis_size("section")
    route = [(i, i + distance) for i in range(sections) if 0 <= i + distance < sections]
    return lax.ppermute(block, "section", route)


def run(body, outs, scratch, flops, *operands):
    return pl.pallas_call(
        body,
        out_shape=[jax.ShapeDtypeStruct(shape, kind) for shape, kind in outs],
        in_specs=[
            pl.BlockSpec(memory_space=pltpu.SMEM if item.ndim == 1 else pltpu.VMEM)
            for item in operands
        ],
        out_specs=[pl.BlockSpec(memory_space=pltpu.VMEM) for _ in outs],
        scratch_shapes=[pltpu.VMEM(shape, kind) for shape, kind in scratch],
        compiler_params=pltpu.CompilerParams(vmem_limit_bytes=VMEM_BYTES),
        cost_estimate=pl.CostEstimate(flops=flops, bytes_accessed=4000000, transcendentals=0),
    )(*operands)


def to_chunk(row):
    count = row.shape[1] // LANES
    return jnp.concatenate([row[:, k * LANES : (k + 1) * LANES] for k in range(count)], axis=0)


def to_row(chunk):
    return jnp.concatenate([chunk[k : k + 1, :] for k in range(chunk.shape[0])], axis=1)


def to_column(row):
    return jnp.transpose(jnp.broadcast_to(row, (LANES, row.shape[1])))


def stack_rows(rows, count, kind):
    filler = jnp.zeros((count - len(rows), rows[0].shape[1]), F32)
    return jnp.concatenate(list(rows) + [filler], axis=0).astype(kind)


def first_rows(rows):
    return stack_rows(rows, STEP, BF)


def wide_rows(ref, offset, count):
    return jnp.concatenate([ref[:, offset + k, :] for k in range(count)], axis=1)


def put_rows(ref, offset, value):
    for k in range(value.shape[1] // LANES):
        ref[:, offset + k, :] = value[:, k * LANES : (k + 1) * LANES]


def two_parts(row):
    high = row.astype(BF).astype(F32)
    return high, row - high


def norm_step(wide, gain, window, hidden_ref, inverse_ref, length_ref):
    inverse = lax.rsqrt(jnp.mean(wide * wide, axis=-1, keepdims=True) + EPSILON)
    hidden = (wide * inverse * gain).astype(BF)
    hidden_ref[window, :] = hidden
    hidden_f = hidden.astype(F32)
    length = lax.rsqrt(jnp.sum(hidden_f * hidden_f, axis=-1, keepdims=True) + EPSILON)
    inverse_ref[window, :] = jnp.broadcast_to(inverse, (STEP, LANES))
    length_ref[window, :] = jnp.broadcast_to(length, (STEP, LANES))


def norm_kernel(in_ref, gain_ref, hidden_ref, inverse_ref, length_out, length_ref):
    gain = gain_ref[...]

    @pl.loop(0, in_ref.shape[0] // STEP)
    def _(index):
        window = pl.ds(index * STEP, STEP)
        wide = in_ref[window, :].astype(F32)
        norm_step(wide, gain, window, hidden_ref, inverse_ref, length_ref)

    length_out[...] = jnp.transpose(length_ref[...])[:8]


def slot_front(scale, columns_ref, hidden_ref, length, logits_ref, prob_ref, rows_ref):
    product = dot_dims(columns_ref[...], hidden_ref[...], 1, 1)
    logits = scale * product * length
    expo = jnp.exp(logits)
    first = expo[:1]
    norm = jnp.sum(expo, axis=0, keepdims=True)
    combine = first / norm
    spread = first / jnp.sum(first, axis=1, keepdims=True)
    logits_ref[...] = logits
    prob_ref[...] = expo / norm
    rows_ref[...] = stack_rows([length, combine, spread], 8, F32)
    slot = jnp.dot(first_rows([spread]), hidden_ref[...], preferred_element_type=F32)
    return combine, slot[:1].astype(BF).astype(F32)


def mix_rows(combine, upstream):
    mixed = jnp.dot(first_rows(two_parts(combine)), upstream, preferred_element_type=F32)
    return (mixed[:1] + mixed[1:2]).astype(BF).astype(F32)


def early_kernel(
    scale_ref, hidden_ref, length_ref, columns_ref, up_ref,
    send_ref, logits_ref, prob_ref, rows_ref, mixed_ref,
):
    length = length_ref[:1]
    combine, slot = slot_front(
        scale_ref[0], columns_ref, hidden_ref, length, logits_ref, prob_ref, rows_ref
    )
    send_ref[...] = jnp.broadcast_to(to_chunk(slot)[None], send_ref.shape)
    mixed_ref[...] = to_chunk(mix_rows(combine, up_ref[...]))


def pack_kernel(sums_ref, rows_ref, out_ref):
    total = jnp.sum(sums_ref[...], axis=0).astype(BF).astype(F32)
    combine = to_chunk(rows_ref[1:2])
    count = total.shape[0]
    out_ref[:count] = total
    out_ref[count:] = jnp.concatenate(
        [combine, jnp.zeros((out_ref.shape[0] - count - combine.shape[0], LANES), F32)], axis=0
    )


def late_kernel(
    scale_ref, base_ref, moved_ref, up_ref, columns_ref, gain_ref,
    send_ref, in_ref, hidden_ref, inverse_ref, logits_ref, prob_ref, rows_ref,
    length_ref, comb_ref,
):
    gain = gain_ref[...]
    chunk = gain.shape[1] // LANES
    out_row = to_row(moved_ref[:chunk])
    comb_ref[...] = to_column(to_row(moved_ref[chunk : chunk + 2]))

    @pl.loop(0, in_ref.shape[0] // STEP)
    def _(index):
        window = pl.ds(index * STEP, STEP)
        base = base_ref[window, :].astype(F32)
        value = (base + comb_ref[window, :1] * out_row).astype(BF)
        in_ref[window, :] = value
        norm_step(value.astype(F32), gain, window, hidden_ref, inverse_ref, length_ref)

    length = jnp.transpose(length_ref[...])[:1]
    combine, slot = slot_front(
        scale_ref[0], columns_ref, hidden_ref, length, logits_ref, prob_ref, rows_ref
    )
    mixed = mix_rows(combine, up_ref[...])
    both = jnp.concatenate([to_chunk(slot), to_chunk(mixed)], axis=0)
    send_ref[...] = jnp.broadcast_to(both[None], send_ref.shape)


def gelu_parts(value):
    rate = 0.7978845608028654
    cube = 0.044715
    bent = jnp.tanh(rate * (value + cube * value * value * value))
    half = 0.5 * (1.0 + bent)
    slope = half + 0.5 * value * (1.0 - bent * bent) * rate * (1.0 + 3.0 * cube * value * value)
    return value * half, slope


def expert_early_kernel(slots_ref, first_ref, second_ref, send_ref, slot_ref, act_ref, slope_ref):
    chunk = slots_ref.shape[1]
    slots = wide_rows(slots_ref, 0, chunk).astype(BF)
    slot_ref[...] = slots
    value, slope = gelu_parts(jnp.dot(slots, first_ref[...], preferred_element_type=F32))
    act = value.astype(BF)
    act_ref[...] = act
    slope_ref[...] = slope
    put_rows(send_ref, 0, jnp.dot(act, second_ref[...], preferred_element_type=F32))


def expert_late_kernel(
    pairs_ref, first_ref, second_ref, send_ref, slot_ref, mixed_ref, act_ref, grad_ref
):
    chunk = pairs_ref.shape[1] // 2
    slots = wide_rows(pairs_ref, 0, chunk).astype(BF)
    mixed = wide_rows(pairs_ref, chunk, chunk).astype(BF)
    slot_ref[...] = slots
    mixed_ref[...] = mixed
    value, slope = gelu_parts(jnp.dot(slots, first_ref[...], preferred_element_type=F32))
    act = value.astype(BF)
    act_ref[...] = act
    grad = (dot_dims(mixed, second_ref[...], 1, 1) * slope).astype(BF)
    grad_ref[...] = grad
    put_rows(send_ref, 0, jnp.dot(act, second_ref[...], preferred_element_type=F32))
    put_rows(send_ref, chunk, dot_dims(grad, first_ref[...], 1, 1))


def expert_back_kernel(
    mixed_in_ref, slope_ref, first_ref, second_ref, send_ref, mixed_ref, grad_ref
):
    mixed = wide_rows(mixed_in_ref, 0, mixed_in_ref.shape[1]).astype(BF)
    mixed_ref[...] = mixed
    grad = (dot_dims(mixed, second_ref[...], 1, 1) * slope_ref[...]).astype(BF)
    grad_ref[...] = grad
    put_rows(send_ref, 0, dot_dims(grad, first_ref[...], 1, 1))


def back_body(
    scale, out_row, grad_row, in_ref, hidden_ref, inverse_ref, logits_ref, prob_ref, rows_ref,
    up_ref, columns_ref, gain_ref, grads_ref, gain_out, hold_ref, pull_ref,
):
    gain = gain_ref[...]
    length = rows_ref[0:1]
    combine = rows_ref[1:2]
    spread = rows_ref[2:3]
    grad_rows = first_rows([grad_row])
    dcombine = dot_dims(first_rows([out_row]), up_ref[...], 1, 1)[:1]
    dspread = dot_dims(grad_rows, hidden_ref[...], 1, 1)[:1].astype(BF).astype(F32)
    first_term = spread * (dspread - jnp.sum(dspread * spread, axis=1, keepdims=True))
    mixed = combine * dcombine
    prob = prob_ref[...]
    top = lax.broadcasted_iota(jnp.int32, prob.shape, 0) == 0
    dlogits = jnp.where(top, mixed + first_term, 0.0) - prob * mixed
    dproduct = dlogits * scale * length
    pull = jnp.sum(dlogits * logits_ref[...], axis=0, keepdims=True) * length * length
    pull_ref[...] = to_column(pull)
    dproduct_bf = dproduct.astype(BF)
    hold_ref[...] = dot_dims(dproduct_bf, columns_ref[...], 0, 0) + dot_dims(
        first_rows([spread]), grad_rows, 0, 0
    )
    router = jnp.dot(dproduct_bf, hidden_ref[...], preferred_element_type=F32)
    gain_out[...] = jnp.zeros_like(gain_out)

    @pl.loop(0, in_ref.shape[0] // STEP)
    def _(index):
        window = pl.ds(index * STEP, STEP)
        inverse = inverse_ref[window, :1]
        dhidden = hold_ref[window, :] - hidden_ref[window, :].astype(F32) * pull_ref[window, :1]
        scaled = in_ref[window, :].astype(F32) * inverse
        product = dhidden * scaled
        gain_out[...] += product[:8] + product[8:]
        through = dhidden * gain
        mean_term = jnp.mean(product * gain, axis=-1, keepdims=True)
        dinput = inverse * (through - scaled * mean_term)
        grads_ref[window, :] = (up_ref[window, :].astype(F32) + dinput).astype(BF)

    return router


def back_late_kernel(
    scale_ref, sums_ref, in_ref, hidden_ref, inverse_ref, logits_ref, prob_ref, rows_ref,
    up_ref, columns_ref, gain_ref, moved_ref,
    grads_ref, mixed_ref, outs_ref, router_ref, gain_out, hold_ref, pull_ref,
):
    chunk = sums_ref.shape[1] // 2
    total = jnp.sum(sums_ref[...], axis=0).astype(BF).astype(F32)
    outs_ref[...] = total
    router = back_body(
        scale_ref[0], to_row(total[:chunk]), to_row(total[chunk:]), in_ref, hidden_ref,
        inverse_ref, logits_ref, prob_ref, rows_ref, up_ref, columns_ref, gain_ref, grads_ref,
        gain_out, hold_ref, pull_ref,
    )
    router_ref[...] = router
    combine = to_row(moved_ref[chunk : chunk + 2])
    mixed_ref[...] = to_chunk(mix_rows(combine, grads_ref[...]))


def back_early_kernel(
    scale_ref, sums_ref, packed_ref, in_ref, hidden_ref, inverse_ref, logits_ref, prob_ref,
    rows_ref, up_ref, columns_ref, gain_ref, router_in_ref, gain_in_ref,
    grads_ref, outs_ref, router_ref, gain_ref_out, gain_out, hold_ref, pull_ref,
):
    chunk = sums_ref.shape[1]
    total = jnp.sum(sums_ref[...], axis=0).astype(BF).astype(F32)
    outs_ref[...] = total
    router = back_body(
        scale_ref[0], to_row(packed_ref[:chunk]), to_row(total), in_ref, hidden_ref,
        inverse_ref, logits_ref, prob_ref, rows_ref, up_ref, columns_ref, gain_ref, grads_ref,
        gain_out, hold_ref, pull_ref,
    )
    router_ref[...] = (router + router_in_ref[...]).astype(BF)
    gain_sum = jnp.sum(gain_out[...] + gain_in_ref[...], axis=0, keepdims=True)
    gain_ref_out[...] = stack_rows(two_parts(gain_sum), 8, F32)


def shards(
    tokens,
    cotangent,
    inflow,
    backflow,
    norm_gain,
    slot_scale,
    router_weight,
    expert_in,
    expert_back,
):
    section_index = lax.axis_index("section")
    is_first = section_index == 0
    is_last = section_index == lax.axis_size("section") - 1
    group = lax.axis_size(DP)
    patches = tokens.shape[2]
    width = tokens.shape[3]
    chunk = width // LANES
    local = router_weight.shape[2]
    slots = local * group
    hidden_units = expert_in.shape[2]
    first_weight = expert_in[0]
    second_weight = expert_back[0]
    token_block = (patches, width)
    table = ((slots, patches), F32)
    weights = router_weight[0].T.astype(F32)
    weight_inv = lax.rsqrt(jnp.sum(weights * weights, axis=1, keepdims=True) + EPSILON)
    local_cols = (weights * weight_inv).astype(BF)

    start_in = jnp.where(is_first, tokens[0, 0], inflow[0, 0])
    sent_in = section_shift(start_in, 1)
    columns = gather(local_cols, DP).reshape(-1, width)

    hidden_early, inverse_early, length_early = run(
        norm_kernel,
        [(token_block, BF), ((patches, LANES), F32), ((8, patches), F32)],
        [((patches, LANES), F32)],
        10000000,
        start_in,
        norm_gain,
    )
    send, logits_early, prob_early, rows_early, mixed_last = run(
        early_kernel,
        [((group, chunk, LANES), F32), table, table, ((8, patches), F32), ((chunk, LANES), F32)],
        [],
        300000000,
        slot_scale,
        hidden_early,
        length_early,
        columns,
        cotangent[0, 0],
    )
    part, slot_early, act_early, slope_early = run(
        expert_early_kernel,
        [
            ((group, chunk, LANES), F32),
            ((group, width), BF),
            ((group, hidden_units), BF),
            ((group, hidden_units), F32),
        ],
        [],
        70000000,
        exchange(send, DP),
        first_weight,
        second_weight,
    )
    packed = run(
        pack_kernel,
        [((chunk + 8, LANES), F32)],
        [],
        1000000,
        exchange(part, DP),
        rows_early,
    )[0]
    moved = section_shift(packed, 1)

    base = jnp.where(is_first, tokens[1, 0], sent_in)
    late_up = jnp.where(is_last, cotangent[1, 0], backflow[0, 0])
    send, late_in, hidden_late, inverse_late, logits_late, prob_late, rows_late = run(
        late_kernel,
        [
            ((group, 2 * chunk, LANES), F32),
            (token_block, BF),
            (token_block, BF),
            ((patches, LANES), F32),
            table,
            table,
            ((8, patches), F32),
        ],
        [((patches, LANES), F32), ((patches, LANES), F32)],
        400000000,
        slot_scale,
        base,
        moved,
        late_up,
        columns,
        norm_gain,
    )
    parts, slot_late, mixed_late, act_late, pre_grad_late = run(
        expert_late_kernel,
        [
            ((group, 2 * chunk, LANES), F32),
            ((group, width), BF),
            ((group, width), BF),
            ((group, hidden_units), BF),
            ((group, hidden_units), BF),
        ],
        [],
        140000000,
        exchange(send, DP),
        first_weight,
        second_weight,
    )
    back_scratch = [(token_block, F32), ((patches, LANES), F32)]
    grads_late, mixed_before, outs_late, router_late, gain_late = run(
        back_late_kernel,
        [
            (token_block, BF),
            ((chunk, LANES), F32),
            ((2 * chunk, LANES), F32),
            ((slots, width), F32),
            ((8, width), F32),
        ],
        back_scratch,
        600000000,
        slot_scale,
        exchange(parts, DP),
        late_in,
        hidden_late,
        inverse_late,
        logits_late,
        prob_late,
        rows_late,
        late_up,
        columns,
        norm_gain,
        moved,
    )
    moved_back = section_shift(mixed_before, -1)
    sent_grads = section_shift(grads_late, -1)
    mixed_early = jnp.where(is_last, mixed_last, moved_back)
    part, mixed_early_all, pre_grad_early = run(
        expert_back_kernel,
        [
            ((group, chunk, LANES), F32),
            ((group, width), BF),
            ((group, hidden_units), BF),
        ],
        [],
        70000000,
        gather(mixed_early, DP),
        slope_early,
        first_weight,
        second_weight,
    )
    early_up = jnp.where(is_last, cotangent[0, 0], sent_grads)
    grads_early, outs_early, router_sum, gain_pair = run(
        back_early_kernel,
        [
            (token_block, BF),
            ((chunk, LANES), F32),
            ((slots, width), BF),
            ((8, width), F32),
        ],
        [((8, width), F32)] + back_scratch,
        600000000,
        slot_scale,
        exchange(part, DP),
        packed,
        start_in,
        hidden_early,
        inverse_early,
        logits_early,
        prob_early,
        rows_early,
        early_up,
        columns,
        norm_gain,
        router_late,
        gain_late,
    )

    gain_rows = jnp.broadcast_to(gain_pair[:2].astype(BF)[None], (group, 2, width))
    finals = exchange(
        jnp.concatenate([router_sum.reshape(group, local, width), gain_rows], axis=1), DP
    )
    finals = finals.reshape(group, -1, width).astype(F32).sum(0)
    gain_total = finals[local : local + 1] + finals[local + 1 :]
    pulled = finals[:local]
    dots = jnp.sum(pulled * weights, axis=1, keepdims=True)
    router_grad = weight_inv * (pulled - weights * (dots * weight_inv * weight_inv))

    first_grad = dot_dims(
        jnp.concatenate([slot_early, slot_late], axis=0),
        jnp.concatenate([pre_grad_early, pre_grad_late], axis=0),
        0,
        0,
    )
    second_grad = dot_dims(
        jnp.concatenate([act_early, act_late], axis=0),
        jnp.concatenate([mixed_early_all, mixed_late], axis=0),
        0,
        0,
    )
    slot_out = jnp.stack([packed[:chunk].reshape(1, width), outs_late[:chunk].reshape(1, width)])
    slot_grad = jnp.stack([outs_early.reshape(1, width), outs_late[chunk:].reshape(1, width)])
    return (
        jnp.stack([grads_early, grads_late])[None, :, None],
        slot_out.astype(BF)[None],
        slot_grad.astype(BF)[None],
        first_grad.astype(BF)[None],
        second_grad.astype(BF)[None],
        router_grad.astype(BF).T[None],
        gain_total,
    )


def solution(mesh):
    fine = Mesh(mesh.devices.reshape(mesh.shape["section"], 2, 4, 4), AXES)
    in_specs = (
        P(None, DP, None, None),
        P(None, DP, None, None),
        P("section", DP, None, None),
        P("section", DP, None, None),
        P("section", None),
        P("section"),
        P("section", None, DP),
        P("section", None, DP),
        P("section", DP, None),
    )
    out_specs = (
        P("section", None, DP, None, None),
        P("section", None, DP, None),
        P("section", None, DP, None),
        P("section", None, DP),
        P("section", DP, None),
        P("section", None, DP),
        P("section", None),
    )
    return jax.shard_map(shards, mesh=fine, in_specs=in_specs, out_specs=out_specs, check_vma=False)
```

time: 254 us -> 245 us (0.965)
  blocking collectives: 56.5 us -> 97.4 us
  Pallas kernels: 0 us -> 28.1 us
  matrix products: 28.8 us -> 2.87 us
  other arithmetic: 35.9 us -> 17.6 us
  starting transfers between devices: 45.8 us -> 29.4 us
  waiting for transfers between devices: 65.1 us -> 51.4 us
  local copies, waits for them, and re-layouts: 18.2 us -> 14.7 us
    all_to_all x3 -> x5, blocking collectives: 56.5 us -> 97.4 us  [exchange(): return lax.all_to_all(chunks, axes, 0, 0, tiled=True)]
    pallas_call x0 -> x9, Pallas kernels: none -> 28.1 us  [run(): pl.pallas_call(body, out_shape=[jax.ShapeDtypeStruct(shape, kind) for sha...]
    dot_general x25 -> x2, matrix products: 28.8 us -> 2.87 us  [dot_dims(): lax.dot_general(left_side, right_side, (((left_dim,), (right_dim,)), ((),...]
    all_to_all x5 -> x3, waiting for transfers between devices: 62.5 us -> 37.6 us  [exchange(): return lax.all_to_all(chunks, axes, 0, 0, tiled=True)]
    all_to_all x5 -> x3, starting transfers between devices: 38 us -> 21.7 us  [exchange(): return lax.all_to_all(chunks, axes, 0, 0, tiled=True)]
    ppermute x4, waiting for transfers between devices: 2.59 us -> 13.8 us  [section_shift(): return lax.ppermute(block, 'section', route)]
    reduce_sum x11 -> x0, other arithmetic: 10.7 us -> none  [the longest x2 4.54 us: front(): inverse = lax.rsqrt(jnp.mean(wide * wide, axis=-1, keepdims=True) + EPSILON)]
    broadcast_in_dim x4 -> x0, other arithmetic: 5.85 us -> none  [the longest x2 3.75 us: gather(): return exchange(jnp.broadcast_to(rows[None], (count,) + rows.shape), axes)]
  transfers between devices with their start and end apart: 9 -> 7, of which waited for: 7 -> 5; matrix products, arithmetic and copies ran while one was open for 11% -> 7% of each run, Pallas kernels for 0% -> 4%
where the time goes in v2:
time: 245 us; the launch traced here: 243 us
  blocking collectives  97.4 us (40%)
  waiting for transfers between devices  51.4 us (21%)
  starting transfers between devices  29.4 us (12%)
  Pallas kernels  28.1 us (11%)
  other arithmetic  17.6 us (7%)
  local copies, waits for them, and re-layouts  14.7 us (6%)
  matrix products  2.87 us (1%)
    all_to_all x5, blocking collectives, exchange(): return lax.all_to_all(chunks, axes, 0, 0, tiled=True)  97.4 us
    all_to_all x3, waiting for transfers between devices, exchange(): return lax.all_to_all(chunks, axes, 0, 0, tiled=True)  37.6 us
    pallas_call x9, Pallas kernels, run(): pl.pallas_call(body, out_shape=[jax.ShapeDtypeStruct(shape, kind) for sha...  28.1 us
    all_to_all x3, starting transfers between devices, exchange(): return lax.all_to_all(chunks, axes, 0, 0, tiled=True)  21.7 us
    ppermute x4, waiting for transfers between devices, section_shift(): return lax.ppermute(block, 'section', route)  13.8 us
    unnamed x96, local copies, waits for them, and re-layouts  11.6 us
    ppermute x4, starting transfers between devices, section_shift(): return lax.ppermute(block, 'section', route)  7.67 us
  transfers between devices with their start and end apart: 7, of which 5 were waited for; matrix products, arithmetic and copies ran while one was open for 7% of the time, Pallas kernels for 4%

profile of v2, /device:TPU:32, one launch (start us, length us, event | category | flops | bytes accessed | tf_op | source)
XLA Modules:
  0.0 243.2 jit_solution(9384151752802787761)
XLA Ops:
  0.6 0.9 fusion.18
  1.6 0.8 fusion.19
  2.4 1.0 broadcast_in_dim.14
  3.4 13.2 %all-to-all-start = ((bf16[32,4,2048]{2,1,0:T(4,128)(2,1)}), bf16[32,4,2048]{2,1,0:T(4,128)(2,1)S(1)}, u32[]{:S(2)}, u32[]{:S(2)}) async-start(bf16[32,4,2048]{2,1,0:T(4,128)(2,1)} %broadcast_in_dim.14), calls=%async_computation | async-start | bytes 1048576 | tf_op jit(solution)/shard_map/all_to_all | solution.py:34
  16.7 2.4 select_bitcast_fusion.1.in_ref
  19.0 1.9 collective-permute-start
  21.6 4.6 %shard_map.144 = (bf16[256,2048]{1,0:T(8,128)(2,1)S(1)}, f32[256,128]{1,0:T(8,128)S(1)}, f32[8,256]{1,0:T(8,128)S(1)}) custom-call(bf16[256,2048]{1,0:T(8,128)(2,1)} %select_bitcast_fusion.1.in_ref, f32[1,2048]{1,0:T(1,128)S(1)} %copy-done.11), custom_call_target="tpu_custom_call" | custom-call | flops 10000000 | bytes 4000000 | tf_op jit(solution)/shard_map/pallas_call | solution.py:49
  26.2 1.0 copy-done.3
  27.2 3.4 %select_bitcast_fusion = (bf16[256,2048]{1,0:T(8,128)(2,1)}, bf16[256,2048]{1,0:T(8,128)(2,1)}) fusion(bf16[1,1,256,2048]{3,2,1,0:T(8,128)(2,1)} %param.12, bf16[2,1,256,2048]{3,2,1,0:T(8,128)(2,1)} %param.10, pred[]{:T(512)S(6)} %eq.6), kind=kLoop, calls=%fused_computation.8 | loop fusion | flops 524288 | bytes 5242881 | tf_op jit(solution)/shard_map/jit(_where)/select_n | solution.py:392
  30.5 7.2 %all-to-all-done = bf16[32,4,2048]{2,1,0:T(4,128)(2,1)S(1)} async-done(((bf16[32,4,2048]{2,1,0:T(4,128)(2,1)}), bf16[32,4,2048]{2,1,0:T(4,128)(2,1)S(1)}, u32[]{:S(2)}, u32[]{:S(2)}) %all-to-all-start) | async-done | bytes 524320 | tf_op jit(solution)/shard_map/all_to_all | solution.py:34
  37.9 1.2 copy-done.4
  39.1 1.2 copy-done.6
  40.3 1.4 shard_map.145
  41.7 20.6 %all_to_all.40.slots_ref = f32[32,16,128]{2,1,0:T(8,128)S(1)} all-to-all(f32[32,16,128]{2,1,0:T(8,128)S(1)} %get-tuple-element.46), channel_id=1, replica_groups=mesh['section'=8,'zh'=2,'y'=4,'x'=4] {'zh','y','x'}, dimensions={0} | all-to-all | bytes 524288 | tf_op jit(solution)/shard_map/all_to_all | solution.py:34
  62.3 0.8 shard_map.146
  63.1 18.0 %all_to_all.41.sums_ref = f32[32,16,128]{2,1,0:T(8,128)S(1)} all-to-all(f32[32,16,128]{2,1,0:T(8,128)S(1)} %get-tuple-element.47), channel_id=1, replica_groups=mesh['section'=8,'zh'=2,'y'=4,'x'=4] {'zh','y','x'}, dimensions={0} | all-to-all | bytes 524288 | tf_op jit(solution)/shard_map/all_to_all | solution.py:34
  81.2 1.9 collective-permute-start.1
  83.2 1.3 bitcast_select_fusion.base_ref
  84.5 1.7 collective-permute-done.1.moved_ref
  86.2 6.0 %shard_map.148 = (f32[32,32,128]{2,1,0:T(8,128)S(1)}, bf16[256,2048]{1,0:T(8,128)(2,1)S(1)}, bf16[256,2048]{1,0:T(8,128)(2,1)S(1)}, f32[256,128]{1,0:T(8,128)S(1...) custom-call(f32[1]{0:T(128)S(6)} %copy.21.scale_ref, ...), custom_call_target="tpu_custom_call" | custom-call | flops 400000000 | bytes 4000000 | tf_op jit(solution)/shard_map/pallas_call | solution.py:49
  92.2 22.7 %all_to_all.42.pairs_ref = f32[32,32,128]{2,1,0:T(8,128)S(1)} all-to-all(f32[32,32,128]{2,1,0:T(8,128)S(1)} %get-tuple-element.49), channel_id=1, replica_groups=mesh['section'=8,'zh'=2,'y'=4,'x'=4] {'zh','y','x'}, dimensions={0} | all-to-all | bytes 1048576 | tf_op jit(solution)/shard_map/all_to_all | solution.py:34
  114.9 1.1 shard_map.149
  116.1 19.9 %all_to_all.43.sums_ref = f32[32,32,128]{2,1,0:T(8,128)S(1)} all-to-all(f32[32,32,128]{2,1,0:T(8,128)S(1)} %get-tuple-element.50), channel_id=1, replica_groups=mesh['section'=8,'zh'=2,'y'=4,'x'=4] {'zh','y','x'}, dimensions={0} | all-to-all | bytes 1048576 | tf_op jit(solution)/shard_map/all_to_all | solution.py:34
  136.0 5.9 %shard_map.150 = (bf16[256,2048]{1,0:T(8,128)(2,1)}, f32[16,128]{1,0:T(8,128)S(1)}, f32[32,128]{1,0:T(8,128)S(1)}, f32[128,2048]{1,0:T(8,128)S(1)}, f32[8,2048]{1,0:T(8,128)S(1)}) custom-call(f32[1]{0:T(128)S(6)} %copy.21.scale_ref, f32[32,32,128]{2,1,0:T(8,128)S(1)} %all_to_all.43.sums_ref, bf16[256,2048]{1,0:T(8,128)(2,1)S(1)} %get-tuple-element.51.in_ref, ...), custom_call_target="tpu_custom_call" | custom-call | flops 600000000 | bytes 4000000 | tf_op jit(solution)/shard_map/pallas_call | solution.py:49
  141.9 1.9 collective-permute-start.3
  143.9 1.9 collective-permute-start.2
  145.8 12.1 %collective-permute-done.2 = f32[16,128]{1,0:T(8,128)S(1)} collective-permute-done((f32[16,128]{1,0:T(8,128)S(1)}, f32[16,128]{1,0:T(8,128)S(1)}, u32[]{:S(2)}, u32[]{:S(2)}) %collective-permute-start.2) | collective-permute-done | bytes 8224 | tf_op jit(solution)/shard_map/ppermute | solution.py:45
  157.9 16.2 %all_to_all.44.mixed_in_ref = f32[32,16,128]{2,1,0:T(8,128)S(1)} all-to-all(f32[32,16,128]{2,1,0:T(8,128)S(1)} %broadcast_in_dim.15), channel_id=1, replica_groups=mesh['section'=8,'zh'=2,'y'=4,'x'=4] {'zh','y','x'}, dimensions={0} | all-to-all | bytes 524288 | tf_op jit(solution)/shard_map/all_to_all | solution.py:34
  174.1 2.0 shard_map.151
  177.4 4.3 %all-to-all-start.6 = ((f32[32,16,128]{2,1,0:T(8,128)}), f32[32,16,128]{2,1,0:T(8,128)S(1)}, u32[]{:S(2)}, u32[]{:S(2)}) async-start(f32[32,16,128]{2,1,0:T(8,128)} %get-tuple-element.59), calls=%async_computation.6 | async-start | bytes 524288 | tf_op jit(solution)/shard_map/all_to_all | solution.py:34
  181.6 1.7 broadcast_select_fusion.up_ref
  183.3 11.4 %all-to-all-done.6.sums_ref = f32[32,16,128]{2,1,0:T(8,128)S(1)} async-done(((f32[32,16,128]{2,1,0:T(8,128)}), f32[32,16,128]{2,1,0:T(8,128)S(1)}, u32[]{:S(2)}, u32[]{:S(2)}) %all-to-all-start.6) | async-done | bytes 262176 | tf_op jit(solution)/shard_map/all_to_all | solution.py:34
  194.7 1.2 copy-done.8
  196.0 0.9 copy-done.13
  196.9 0.9 copy-done.15
  197.8 0.7 copy-done.25
  198.5 0.8 copy-done.27
  199.3 6.2 %shard_map.152 = (bf16[256,2048]{1,0:T(8,128)(2,1)S(1)}, f32[16,128]{1,0:T(8,128)S(1)}, bf16[128,2048]{1,0:T(8,128)(2,1)S(1)}, f32[8,2048]{1,0:T(8,128)S(1)}) custom-call(f32[1]{0:T(128)S(6)} %copy.21.scale_ref, f32[32,16,128]{2,1,0:T(8,128)S(1)} %all-to-all-done.6.sums_ref, f32[24,128]{1,0:T(8,128)S(1)} %copy-done.25, ...), custom_call_target="tpu_custom_call" | custom-call | flops 600000000 | bytes 4000000 | tf_op jit(solution)/shard_map/pallas_call | solution.py:49
  205.6 1.0 copy-done.9
  208.0 0.8 slice.70
  209.0 1.5 pad_maximum_fusion
  210.5 4.3 %all-to-all-start.7 = ((bf16[32,6,2048]{2,1,0:T(8,128)(2,1)}), bf16[32,6,2048]{2,1,0:T(8,128)(2,1)S(1)}, u32[]{:S(2)}, u32[]{:S(2)}) async-start(bf16[32,6,2048]{2,1,0:T(8,128)(2,1)} %pad_maximum_fusion), calls=%async_computation.7 | async-start | bytes 2097152 | tf_op jit(solution)/shard_map/all_to_all | solution.py:34
  214.8 0.7 slice.71
  216.2 1.4 fusion.1
  217.7 1.4 fusion
  219.8 2.8 %maximum_bitcast_fusion = bf16[1,2,1,256,2048]{4,3,2,1,0:T(8,128)(2,1)} fusion(bf16[1,256,2048]{2,1,0:T(8,128)(2,1)} %bitcast.10, bf16[1,256,2048]{2,1,0:T(8,128)(2,1)S(1)} %bitcast.66), kind=kLoop, calls=%fused_computation.4 | loop fusion | flops 1048576 | bytes 4194304
  222.5 19.0 %all-to-all-done.7 = bf16[32,6,2048]{2,1,0:T(8,128)(2,1)S(1)} async-done(((bf16[32,6,2048]{2,1,0:T(8,128)(2,1)}), bf16[32,6,2048]{2,1,0:T(8,128)(2,1)S(1)}, u32[]{:S(2)}, u32[]{:S(2)}) %all-to-all-start.7) | async-done | bytes 786464 | tf_op jit(solution)/shard_map/all_to_all | solution.py:34
  242.5 0.7 fusion.24
  (109 shorter events, 5.4 us)
Async XLA Ops:
  0.6 16.0 %copy-start.42 = (bf16[1,1,256,2048]{3,2,1,0:T(8,128)(2,1)S(1)}, bf16[1,1,256,2048]{3,2,1,0:T(8,128)(2,1)}, u32[]{:S(2)}) copy-start(bf16[1,1,256,2048]{3,2,1,0:T(8,128)(2,1)} %param.11) | copy-start | bytes 3145732
  3.4 18.1 %copy-start.11 = (f32[1,2048]{1,0:T(1,128)S(1)}, f32[1,2048]{1,0:T(1,128)}, u32[]{:S(2)}) copy-start(f32[1,2048]{1,0:T(1,128)} %gain_ref.7) | copy-start | bytes 24580
  3.4 34.3 %all-to-all-start = ((bf16[32,4,2048]{2,1,0:T(4,128)(2,1)}), bf16[32,4,2048]{2,1,0:T(4,128)(2,1)S(1)}, u32[]{:S(2)}, u32[]{:S(2)}) async-start(bf16[32,4,2048]{2,1,0:T(4,128)(2,1)} %broadcast_in_dim.14), calls=%async_computation | async-start | bytes 1048576 | tf_op jit(solution)/shard_map/all_to_all | solution.py:34
  19.0 64.1 %collective-permute-start = (bf16[256,2048]{1,0:T(8,128)(2,1)}, bf16[256,2048]{1,0:T(8,128)(2,1)}, u32[]{:S(2)}, u32[]{:S(2)}) collective-permute-start(bf16[256,2048]{1,0:T(8,128)(2,1)} %select_bitcast_fusion.1.in_ref), channel_id=1, source_target_pairs={{0,32},{32,64},{64,96},{96,128},{128,160},{160,192},{192,224},{1,3... | collective-permute-start | bytes 3145736 | tf_op jit(solution)/shard_map/ppermute | solution.py:45
  26.2 1.0 copy-start.3
  30.5 31.8 %copy-start = (bf16[1,2048,256]{2,1,0:T(8,128)(2,1)S(1)}, bf16[1,2048,256]{2,1,0:T(8,128)(2,1)}, u32[]{:S(2)}) copy-start(bf16[1,2048,256]{2,1,0:T(8,128)(2,1)} %param.16) | copy-start | bytes 3145732
  30.5 31.8 %copy-start.1 = (bf16[1,256,2048]{2,1,0:T(8,128)(2,1)S(1)}, bf16[1,256,2048]{2,1,0:T(8,128)(2,1)}, u32[]{:S(2)}) copy-start(bf16[1,256,2048]{2,1,0:T(8,128)(2,1)} %param.17) | copy-start | bytes 3145732
  37.8 1.2 copy-start.4
  39.1 1.2 copy-start.6
  41.7 20.6 %copy-start.14 = (f32[128,256]{1,0:T(8,128)}, f32[128,256]{1,0:T(8,128)S(1)}, u32[]{:S(2)}) copy-start(f32[128,256]{1,0:T(8,128)S(1)} %get-tuple-element.62.prob_ref) | copy-start | bytes 393220
  41.7 41.4 %copy-start.12 = (f32[128,256]{1,0:T(8,128)}, f32[128,256]{1,0:T(8,128)S(1)}, u32[]{:S(2)}) copy-start(f32[128,256]{1,0:T(8,128)S(1)} %get-tuple-element.61.logits_ref) | copy-start | bytes 393220
  41.7 41.5 %copy-start.41 = (bf16[2,1,256,2048]{3,2,1,0:T(8,128)(2,1)S(1)}, bf16[2,1,256,2048]{3,2,1,0:T(8,128)(2,1)}, u32[]{:S(2)}) copy-start(bf16[2,1,256,2048]{3,2,1,0:T(8,128)(2,1)} %param.9) | copy-start | bytes 6291460
  63.1 20.0 %copy-start.16 = (bf16[32,2048]{1,0:T(8,128)(2,1)}, bf16[32,2048]{1,0:T(8,128)(2,1)S(1)}, u32[]{:S(2)}) copy-start(bf16[32,2048]{1,0:T(8,128)(2,1)S(1)} %get-tuple-element.69) | copy-start | bytes 393220
  63.1 20.0 %copy-start.28 = (bf16[32,256]{1,0:T(8,128)(2,1)}, bf16[32,256]{1,0:T(8,128)(2,1)S(1)}, u32[]{:S(2)}) copy-start(bf16[32,256]{1,0:T(8,128)(2,1)S(1)} %get-tuple-element.73) | copy-start | bytes 49156
  63.1 23.1 %copy-start.2 = (bf16[256,2048]{1,0:T(8,128)(2,1)S(1)}, bf16[256,2048]{1,0:T(8,128)(2,1)}, u32[]{:S(2)}) copy-start(bf16[256,2048]{1,0:T(8,128)(2,1)} %get-tuple-element.86.up_ref) | copy-start | bytes 3145732
  81.2 11.1 %copy-start.24 = (f32[24,128]{1,0:T(8,128)}, f32[24,128]{1,0:T(8,128)S(1)}, u32[]{:S(2)}) copy-start(f32[24,128]{1,0:T(8,128)S(1)} %shard_map.147.packed_ref) | copy-start | bytes 36868
  81.2 5.0 %collective-permute-start.1 = (f32[24,128]{1,0:T(8,128)S(1)}, f32[24,128]{1,0:T(8,128)S(1)}, u32[]{:S(2)}, u32[]{:S(2)}) collective-permute-start(f32[24,128]{1,0:T(8,128)S(1)} %shard_map.147.packed_ref), channel_id=1, source_target_pairs={{0,32},{32,64},{64,96},{96,128},{128,160},{160,192},{192,224},{1,3... | collective-permute-start | bytes 36872 | tf_op jit(solution)/shard_map/ppermute | solution.py:45
  116.1 19.9 %copy-start.32 = (bf16[32,256]{1,0:T(8,128)(2,1)}, bf16[32,256]{1,0:T(8,128)(2,1)S(1)}, u32[]{:S(2)}) copy-start(bf16[32,256]{1,0:T(8,128)(2,1)S(1)} %get-tuple-element.74) | copy-start | bytes 49156
  116.1 25.8 %copy-start.18 = (bf16[32,2048]{1,0:T(8,128)(2,1)}, bf16[32,2048]{1,0:T(8,128)(2,1)S(1)}, u32[]{:S(2)}) copy-start(bf16[32,2048]{1,0:T(8,128)(2,1)S(1)} %get-tuple-element.70) | copy-start | bytes 393220
  116.1 25.8 %copy-start.20 = (bf16[32,2048]{1,0:T(8,128)(2,1)}, bf16[32,2048]{1,0:T(8,128)(2,1)S(1)}, u32[]{:S(2)}) copy-start(bf16[32,2048]{1,0:T(8,128)(2,1)S(1)} %get-tuple-element.76) | copy-start | bytes 393220
  116.1 25.8 %copy-start.30 = (bf16[32,256]{1,0:T(8,128)(2,1)}, bf16[32,256]{1,0:T(8,128)(2,1)S(1)}, u32[]{:S(2)}) copy-start(bf16[32,256]{1,0:T(8,128)(2,1)S(1)} %get-tuple-element.72) | copy-start | bytes 49156
  141.9 34.2 %copy-start.7 = (f32[128,2048]{1,0:T(8,128)}, f32[128,2048]{1,0:T(8,128)S(1)}, u32[]{:S(2)}) copy-start(f32[128,2048]{1,0:T(8,128)S(1)} %get-tuple-element.64.router_in_ref) | copy-start | bytes 3145732
  141.9 34.2 %copy-start.26 = (f32[8,2048]{1,0:T(8,128)}, f32[8,2048]{1,0:T(8,128)S(1)}, u32[]{:S(2)}) copy-start(f32[8,2048]{1,0:T(8,128)S(1)} %get-tuple-element.65.gain_in_ref) | copy-start | bytes 196612
  141.9 34.2 %copy-start.36 = (f32[32,128]{1,0:T(8,128)}, f32[32,128]{1,0:T(8,128)S(1)}, u32[]{:S(2)}) copy-start(f32[32,128]{1,0:T(8,128)S(1)} %get-tuple-element.67) | copy-start | bytes 49156
  141.9 39.7 %collective-permute-start.3 = (bf16[256,2048]{1,0:T(8,128)(2,1)}, bf16[256,2048]{1,0:T(8,128)(2,1)}, u32[]{:S(2)}, u32[]{:S(2)}) collective-permute-start(bf16[256,2048]{1,0:T(8,128)(2,1)} %get-tuple-element.63), channel_id=1, source_target_pairs={{32,0},{64,32},{96,64},{128,96},{160,128},{192,160},{224,192},{33,... | collective-permute-start | bytes 3145736 | tf_op jit(solution)/shard_map/ppermute | solution.py:45
  143.9 14.0 %collective-permute-start.2 = (f32[16,128]{1,0:T(8,128)S(1)}, f32[16,128]{1,0:T(8,128)S(1)}, u32[]{:S(2)}, u32[]{:S(2)}) collective-permute-start(f32[16,128]{1,0:T(8,128)S(1)} %get-tuple-element.57), channel_id=1, source_target_pairs={{32,0},{64,32},{96,64},{128,96},{160,128},{192,160},{224,192},{33,... | collective-permute-start | bytes 24584 | tf_op jit(solution)/shard_map/ppermute | solution.py:45
  177.4 17.4 %copy-start.5 = (bf16[256,2048]{1,0:T(8,128)(2,1)S(1)}, bf16[256,2048]{1,0:T(8,128)(2,1)}, u32[]{:S(2)}) copy-start(bf16[256,2048]{1,0:T(8,128)(2,1)} %copy-done.3) | copy-start | bytes 3145732
  177.4 17.4 %all-to-all-start.6 = ((f32[32,16,128]{2,1,0:T(8,128)}), f32[32,16,128]{2,1,0:T(8,128)S(1)}, u32[]{:S(2)}, u32[]{:S(2)}) async-start(f32[32,16,128]{2,1,0:T(8,128)} %get-tuple-element.59), calls=%async_computation.6 | async-start | bytes 524288 | tf_op jit(solution)/shard_map/all_to_all | solution.py:34
  194.7 1.2 copy-start.8
  196.0 0.9 copy-start.13
  196.9 0.9 copy-start.15
  198.5 0.8 copy-start.27
  205.6 1.0 copy-start.9
  208.8 6.7 %copy-start.37 = (f32[32,128]{1,0:T(8,128)S(1)}, f32[32,128]{1,0:T(8,128)}, u32[]{:S(2)}) copy-start(f32[32,128]{1,0:T(8,128)} %copy-done.36) | copy-start | bytes 49156
  209.0 7.3 %copy-start.21 = (bf16[32,2048]{1,0:T(8,128)(2,1)S(1)}, bf16[32,2048]{1,0:T(8,128)(2,1)}, u32[]{:S(2)}) copy-start(bf16[32,2048]{1,0:T(8,128)(2,1)} %copy-done.20) | copy-start | bytes 393220
  209.0 7.3 %copy-start.23 = (bf16[32,2048]{1,0:T(8,128)(2,1)S(1)}, bf16[32,2048]{1,0:T(8,128)(2,1)}, u32[]{:S(2)}) copy-start(bf16[32,2048]{1,0:T(8,128)(2,1)} %copy-done.22) | copy-start | bytes 393220
  209.0 7.3 %copy-start.29 = (bf16[32,256]{1,0:T(8,128)(2,1)S(1)}, bf16[32,256]{1,0:T(8,128)(2,1)}, u32[]{:S(2)}) copy-start(bf16[32,256]{1,0:T(8,128)(2,1)} %copy-done.28) | copy-start | bytes 49156
  209.0 7.2 %copy-start.33 = (bf16[32,256]{1,0:T(8,128)(2,1)S(1)}, bf16[32,256]{1,0:T(8,128)(2,1)}, u32[]{:S(2)}) copy-start(bf16[32,256]{1,0:T(8,128)(2,1)} %copy-done.32) | copy-start | bytes 49156
  210.5 7.2 %copy-start.17 = (bf16[32,2048]{1,0:T(8,128)(2,1)S(1)}, bf16[32,2048]{1,0:T(8,128)(2,1)}, u32[]{:S(2)}) copy-start(bf16[32,2048]{1,0:T(8,128)(2,1)} %copy-done.16) | copy-start | bytes 393220
  210.5 7.2 %copy-start.19 = (bf16[32,2048]{1,0:T(8,128)(2,1)S(1)}, bf16[32,2048]{1,0:T(8,128)(2,1)}, u32[]{:S(2)}) copy-start(bf16[32,2048]{1,0:T(8,128)(2,1)} %copy-done.18) | copy-start | bytes 393220
  210.5 7.2 %copy-start.31 = (bf16[32,256]{1,0:T(8,128)(2,1)S(1)}, bf16[32,256]{1,0:T(8,128)(2,1)}, u32[]{:S(2)}) copy-start(bf16[32,256]{1,0:T(8,128)(2,1)} %copy-done.30) | copy-start | bytes 49156
  210.5 7.2 %copy-start.35 = (bf16[32,256]{1,0:T(8,128)(2,1)S(1)}, bf16[32,256]{1,0:T(8,128)(2,1)}, u32[]{:S(2)}) copy-start(bf16[32,256]{1,0:T(8,128)(2,1)} %copy-done.34) | copy-start | bytes 49156
  210.5 8.6 %copy-start.39 = (f32[16,128]{1,0:T(8,128)S(1)}, f32[16,128]{1,0:T(8,128)}, u32[]{:S(2)}) copy-start(f32[16,128]{1,0:T(8,128)} %copy-done.38) | copy-start | bytes 24580
  210.5 9.3 %copy-start.10 = (bf16[256,2048]{1,0:T(8,128)(2,1)S(1)}, bf16[256,2048]{1,0:T(8,128)(2,1)}, u32[]{:S(2)}) copy-start(bf16[256,2048]{1,0:T(8,128)(2,1)} %copy-done.9) | copy-start | bytes 3145732
  210.5 31.0 %all-to-all-start.7 = ((bf16[32,6,2048]{2,1,0:T(8,128)(2,1)}), bf16[32,6,2048]{2,1,0:T(8,128)(2,1)S(1)}, u32[]{:S(2)}, u32[]{:S(2)}) async-start(bf16[32,6,2048]{2,1,0:T(8,128)(2,1)} %pad_maximum_fusion), calls=%async_computation.7 | async-start | bytes 2097152 | tf_op jit(solution)/shard_map/all_to_all | solution.py:34
  219.8 21.9 %copy-start.43 = (bf16[1,2048,4]{1,2,0:T(4,128)(2,1)S(1)}, bf16[1,2048,4]{1,2,0:T(4,128)(2,1)}, u32[]{:S(2)}) copy-start(bf16[1,2048,4]{1,2,0:T(4,128)(2,1)} %param.15) | copy-start | bytes 49156
  219.8 22.7 %copy-start.47 = (f32[4]{0:T(128)S(1)}, f32[4]{0:T(128)}, u32[]{:S(2)}) copy-start(f32[4]{0:T(128)} %copy-done.46) | copy-start | bytes 52
  219.8 22.7 %copy-start.45 = (f32[4]{0:T(128)S(1)}, f32[4]{0:T(128)}, u32[]{:S(2)}) copy-start(f32[4]{0:T(128)} %copy-done.44) | copy-start | bytes 52
  (7 other events, 4.8 us)

commit v3 on v2

v3 whole, which is shorter than its diff:
```python
import jax
import jax.numpy as jnp
from jax import lax
from jax.experimental import pallas as pl
from jax.experimental.pallas import tpu as pltpu
from jax.sharding import Mesh
from jax.sharding import PartitionSpec as P

EPSILON = 1e-06
BF = jnp.bfloat16
F32 = jnp.float32
AXES = ("section", "zh", "y", "x")
DP = ("zh", "y", "x")
LANES = 128
STEP = 16
VMEM_BYTES = 24 * 1024 * 1024


def dot_dims(left_side, right_side, left_dim, right_dim):
    return lax.dot_general(
        left_side,
        right_side,
        (((left_dim,), (right_dim,)), ((), ())),
        preferred_element_type=F32,
    )


def exchange(chunks, axes):
    return lax.all_to_all(chunks, axes, 0, 0, tiled=True)


def section_shift(block, distance):
    sections = lax.axis_size("section")
    route = [(i, i + distance) for i in range(sections) if 0 <= i + distance < sections]
    return lax.ppermute(block, "section", route)


def run(body, outs, scratch, flops, near, *operands):
    def place(index, item):
        if item.ndim == 1:
            return pltpu.SMEM
        return pltpu.VMEM if index < near else pl.ANY

    return pl.pallas_call(
        body,
        out_shape=[jax.ShapeDtypeStruct(shape, kind) for shape, kind in outs],
        in_specs=[
            pl.BlockSpec(memory_space=place(index, item)) for index, item in enumerate(operands)
        ],
        out_specs=[pl.BlockSpec(memory_space=pltpu.VMEM) for _ in outs],
        scratch_shapes=[
            pltpu.VMEM(*item) if isinstance(item, tuple) else item for item in scratch
        ],
        compiler_params=pltpu.CompilerParams(vmem_limit_bytes=VMEM_BYTES),
        cost_estimate=pl.CostEstimate(flops=flops, bytes_accessed=4000000, transcendentals=0),
    )(*operands)


def to_chunk(row):
    count = row.shape[1] // LANES
    return jnp.concatenate([row[:, k * LANES : (k + 1) * LANES] for k in range(count)], axis=0)


def to_row(chunk):
    return jnp.concatenate([chunk[k : k + 1, :] for k in range(chunk.shape[0])], axis=1)


def to_column(row):
    return jnp.transpose(jnp.broadcast_to(row, (LANES, row.shape[1])))


def stack_rows(rows, count, kind):
    filler = jnp.zeros((count - len(rows), rows[0].shape[1]), F32)
    return jnp.concatenate(list(rows) + [filler], axis=0).astype(kind)


def first_rows(rows):
    return stack_rows(rows, STEP, BF)


def wide_rows(ref, offset, count):
    return jnp.concatenate([ref[:, offset + k, :] for k in range(count)], axis=1)


def put_rows(ref, offset, value):
    for k in range(value.shape[1] // LANES):
        ref[:, offset + k, :] = value[:, k * LANES : (k + 1) * LANES]


def two_parts(row):
    high = row.astype(BF).astype(F32)
    return high, row - high


def lane_sums(value):
    parts = [value[:, k * LANES : (k + 1) * LANES] for k in range(value.shape[1] // LANES)]
    while len(parts) > 1:
        parts = [x + y for x, y in zip(parts[::2], parts[1::2])]
    return parts[0]


def summed(chunks_ref):
    return jnp.sum(chunks_ref[...].astype(F32), axis=0).astype(BF).astype(F32)


def passes(ref, body):
    @pl.loop(0, ref.shape[0] // STEP)
    def _(index):
        body(pl.ds(index * STEP, STEP))


def begin_copy(flag, yes, no, target, sem):
    @pl.when(flag != 0)
    def _():
        pltpu.make_async_copy(yes, target, sem).start()

    @pl.when(flag == 0)
    def _():
        pltpu.make_async_copy(no, target, sem).start()


def end_copy(source, target, sem):
    pltpu.make_async_copy(source, target, sem).wait()


def scaled_weights(weights_ref):
    weights = weights_ref[...].astype(F32)
    total = jnp.sum(weights * weights, axis=1, keepdims=True)
    return weights, lax.rsqrt(total + EPSILON)


def columns_kernel(weights_ref, send_ref):
    weights, inverse = scaled_weights(weights_ref)
    columns = weights * inverse
    rows = [to_chunk(columns[k : k + 1]) for k in range(columns.shape[0])]
    block = jnp.concatenate(rows, axis=0).astype(BF)
    send_ref[...] = jnp.broadcast_to(block[None], send_ref.shape)


def norm_passes(in_ref, gain, hidden_ref, inverse_ref, sums_ref):
    rate = 1.0 / in_ref.shape[1]
    inverse = lax.rsqrt(jnp.sum(sums_ref[...], axis=1, keepdims=True) * rate + EPSILON)
    inverse_ref[...] = jnp.broadcast_to(inverse, inverse_ref.shape)

    def scale_rows(window):
        wide = in_ref[window, :].astype(F32)
        hidden = (wide * inverse_ref[window, :1] * gain).astype(BF)
        hidden_ref[window, :] = hidden
        hidden_f = hidden.astype(F32)
        sums_ref[window, :] = lane_sums(hidden_f * hidden_f)

    passes(in_ref, scale_rows)
    total = jnp.sum(jnp.transpose(sums_ref[...]), axis=0, keepdims=True)
    return lax.rsqrt(total + EPSILON)


def slot_front(scale, columns_ref, hidden_ref, length, logits_ref, prob_ref, rows_ref):
    product = dot_dims(columns_ref[...], hidden_ref[...], 1, 1)
    logits = scale * product * length
    expo = jnp.exp(logits)
    first = expo[:1]
    norm = jnp.sum(expo, axis=0, keepdims=True)
    combine = first / norm
    spread = first / jnp.sum(first, axis=1, keepdims=True)
    logits_ref[...] = logits
    prob_ref[...] = expo / norm
    rows_ref[...] = stack_rows([length, combine, spread], 8, F32)
    slot = jnp.dot(first_rows([spread]), hidden_ref[...], preferred_element_type=F32)
    return combine, slot[:1]


def mix_rows(combine, upstream):
    mixed = jnp.dot(first_rows(two_parts(combine)), upstream, preferred_element_type=F32)
    return mixed[:1] + mixed[1:2]


def early_kernel(
    scale_ref, flags_ref, chunks_ref, gain_ref, tokens_ref, inflow_ref, cotangent_ref,
    send_ref, in_ref, columns_ref, hidden_ref, inverse_ref, logits_ref, prob_ref, rows_ref,
    mixed_ref, up_ref, wide_ref, sums_ref, in_sem, up_sem,
):
    begin_copy(flags_ref[0], tokens_ref.at[0, 0], inflow_ref.at[0, 0], in_ref, in_sem)
    last = flags_ref[1] != 0

    @pl.when(last)
    def _():
        pltpu.make_async_copy(cotangent_ref.at[0, 0], up_ref, up_sem).start()

    peers = chunks_ref.shape[0]
    chunk = gain_ref.shape[1] // LANES
    wide_ref[...] = chunks_ref[...].astype(F32)
    for k in range(chunks_ref.shape[1] // chunk):
        columns_ref[k * peers : (k + 1) * peers] = wide_rows(wide_ref, k * chunk, chunk).astype(BF)
    end_copy(inflow_ref.at[0, 0], in_ref, in_sem)

    def square_rows(window):
        wide = in_ref[window, :].astype(F32)
        sums_ref[window, :] = lane_sums(wide * wide)

    passes(in_ref, square_rows)
    length = norm_passes(in_ref, gain_ref[...], hidden_ref, inverse_ref, sums_ref)
    combine, slot = slot_front(
        scale_ref[0], columns_ref, hidden_ref, length, logits_ref, prob_ref, rows_ref
    )
    send_ref[...] = jnp.broadcast_to(to_chunk(slot).astype(BF)[None], send_ref.shape)
    mixed_ref[...] = jnp.zeros_like(mixed_ref)

    @pl.when(last)
    def _():
        end_copy(cotangent_ref.at[0, 0], up_ref, up_sem)
        mixed_ref[...] = to_chunk(mix_rows(combine, up_ref[...])).astype(BF)


def pack_kernel(sums_ref, rows_ref, out_ref):
    total = summed(sums_ref)
    combine = to_chunk(rows_ref[1:2])
    count = total.shape[0]
    out_ref[:count] = total
    out_ref[count:] = jnp.concatenate(
        [combine, jnp.zeros((out_ref.shape[0] - count - combine.shape[0], LANES), F32)], axis=0
    )


def late_kernel(
    scale_ref, flags_ref, base_ref, moved_ref, columns_ref, gain_ref, cotangent_ref, backflow_ref,
    send_ref, in_ref, hidden_ref, inverse_ref, logits_ref, prob_ref, rows_ref, up_ref,
    sums_ref, comb_ref, up_sem,
):
    begin_copy(flags_ref[1], cotangent_ref.at[1, 0], backflow_ref.at[0, 0], up_ref, up_sem)
    chunk = gain_ref.shape[1] // LANES
    out_row = to_row(moved_ref[:chunk])
    comb_ref[...] = to_column(to_row(moved_ref[chunk : chunk + 2]))

    def add_rows(window):
        base = base_ref[window, :].astype(F32)
        value = (base + comb_ref[window, :1] * out_row).astype(BF)
        in_ref[window, :] = value
        wide = value.astype(F32)
        sums_ref[window, :] = lane_sums(wide * wide)

    passes(in_ref, add_rows)
    length = norm_passes(in_ref, gain_ref[...], hidden_ref, inverse_ref, sums_ref)
    combine, slot = slot_front(
        scale_ref[0], columns_ref, hidden_ref, length, logits_ref, prob_ref, rows_ref
    )
    end_copy(backflow_ref.at[0, 0], up_ref, up_sem)
    mixed = mix_rows(combine, up_ref[...])
    both = jnp.concatenate([to_chunk(slot), to_chunk(mixed)], axis=0).astype(BF)
    send_ref[...] = jnp.broadcast_to(both[None], send_ref.shape)


def gelu_parts(value):
    rate = 0.7978845608028654
    cube = 0.044715
    bent = jnp.tanh(rate * (value + cube * value * value * value))
    half = 0.5 * (1.0 + bent)
    slope = half + 0.5 * value * (1.0 - bent * bent) * rate * (1.0 + 3.0 * cube * value * value)
    return value * half, slope


def expert_early_kernel(
    slots_ref, first_ref, second_ref, send_ref, slot_ref, act_ref, slope_ref, wide_ref
):
    wide_ref[...] = slots_ref[...].astype(F32)
    slots = wide_rows(wide_ref, 0, slots_ref.shape[1]).astype(BF)
    slot_ref[...] = slots
    value, slope = gelu_parts(jnp.dot(slots, first_ref[...], preferred_element_type=F32))
    act = value.astype(BF)
    act_ref[...] = act
    slope_ref[...] = slope
    put_rows(wide_ref, 0, jnp.dot(act, second_ref[...], preferred_element_type=F32))
    send_ref[...] = wide_ref[...].astype(BF)


def expert_late_kernel(
    pairs_ref, first_ref, second_ref, send_ref, slot_ref, mixed_ref, act_ref, grad_ref, wide_ref
):
    chunk = pairs_ref.shape[1] // 2
    wide_ref[...] = pairs_ref[...].astype(F32)
    slots = wide_rows(wide_ref, 0, chunk).astype(BF)
    mixed = wide_rows(wide_ref, chunk, chunk).astype(BF)
    slot_ref[...] = slots
    mixed_ref[...] = mixed
    value, slope = gelu_parts(jnp.dot(slots, first_ref[...], preferred_element_type=F32))
    act = value.astype(BF)
    act_ref[...] = act
    grad = (dot_dims(mixed, second_ref[...], 1, 1) * slope).astype(BF)
    grad_ref[...] = grad
    put_rows(wide_ref, 0, jnp.dot(act, second_ref[...], preferred_element_type=F32))
    put_rows(wide_ref, chunk, dot_dims(grad, first_ref[...], 1, 1))
    send_ref[...] = wide_ref[...].astype(BF)


def expert_back_kernel(
    mixed_in_ref, slope_ref, first_ref, second_ref, send_ref, mixed_ref, grad_ref, wide_ref
):
    wide_ref[...] = mixed_in_ref[...].astype(F32)
    mixed = wide_rows(wide_ref, 0, mixed_in_ref.shape[1]).astype(BF)
    mixed_ref[...] = mixed
    grad = (dot_dims(mixed, second_ref[...], 1, 1) * slope_ref[...]).astype(BF)
    grad_ref[...] = grad
    put_rows(wide_ref, 0, dot_dims(grad, first_ref[...], 1, 1))
    send_ref[...] = wide_ref[...].astype(BF)


def spread_kernel(moved_ref, own_ref, send_ref):
    block = (moved_ref[...].astype(F32) + own_ref[...].astype(F32)).astype(BF)
    send_ref[...] = jnp.broadcast_to(block[None], send_ref.shape)


def back_body(
    scale, out_row, grad_row, in_ref, hidden_ref, inverse_ref, logits_ref, prob_ref, rows_ref,
    up_ref, columns_ref, gain_ref, grads_ref, hold_ref, pull_ref, mean_ref,
):
    gain = gain_ref[...]
    length = rows_ref[0:1]
    combine = rows_ref[1:2]
    spread = rows_ref[2:3]
    grad_rows = first_rows([grad_row])
    dcombine = dot_dims(first_rows([out_row]), up_ref[...], 1, 1)[:1]
    dspread = dot_dims(grad_rows, hidden_ref[...], 1, 1)[:1].astype(BF).astype(F32)
    first_term = spread * (dspread - jnp.sum(dspread * spread, axis=1, keepdims=True))
    mixed = combine * dcombine
    prob = prob_ref[...]
    top = lax.broadcasted_iota(jnp.int32, prob.shape, 0) == 0
    dlogits = jnp.where(top, mixed + first_term, 0.0) - prob * mixed
    dproduct = dlogits * scale * length
    pull = jnp.sum(dlogits * logits_ref[...], axis=0, keepdims=True) * length * length
    pull_ref[...] = to_column(pull)
    dproduct_bf = dproduct.astype(BF)
    hold_ref[...] = dot_dims(dproduct_bf, columns_ref[...], 0, 0) + dot_dims(
        first_rows([spread]), grad_rows, 0, 0
    )
    router = jnp.dot(dproduct_bf, hidden_ref[...], preferred_element_type=F32)

    def product_rows(index, total):
        window = pl.ds(index * STEP, STEP)
        dhidden = hold_ref[window, :] - hidden_ref[window, :].astype(F32) * pull_ref[window, :1]
        hold_ref[window, :] = dhidden
        product = dhidden * (in_ref[window, :].astype(F32) * inverse_ref[window, :1])
        mean_ref[window, :] = lane_sums(product * gain)
        return total + product[:8] + product[8:]

    gain_sum = lax.fori_loop(
        0, in_ref.shape[0] // STEP, product_rows, jnp.zeros((8, in_ref.shape[1]), F32)
    )
    mean = jnp.sum(mean_ref[...], axis=1, keepdims=True) * (1.0 / in_ref.shape[1])
    mean_ref[...] = jnp.broadcast_to(mean * inverse_ref[...], mean_ref.shape)

    def grad_rows_pass(window):
        inverse = inverse_ref[window, :1]
        through = hold_ref[window, :] * gain
        wide = in_ref[window, :].astype(F32)
        dinput = inverse * (through - wide * mean_ref[window, :1])
        grads_ref[window, :] = (up_ref[window, :].astype(F32) + dinput).astype(BF)

    passes(in_ref, grad_rows_pass)
    return router, gain_sum


def back_late_kernel(
    scale_ref, sums_ref, in_ref, hidden_ref, inverse_ref, logits_ref, prob_ref, rows_ref,
    up_ref, columns_ref, gain_ref, moved_ref,
    grads_ref, mixed_ref, outs_ref, router_ref, gain_out, hold_ref, pull_ref, mean_ref,
):
    chunk = sums_ref.shape[1] // 2
    total = summed(sums_ref)
    outs_ref[...] = total
    router, gain_sum = back_body(
        scale_ref[0], to_row(total[:chunk]), to_row(total[chunk:]), in_ref, hidden_ref,
        inverse_ref, logits_ref, prob_ref, rows_ref, up_ref, columns_ref, gain_ref, grads_ref,
        hold_ref, pull_ref, mean_ref,
    )
    router_ref[...] = router
    gain_out[...] = gain_sum
    combine = to_row(moved_ref[chunk : chunk + 2])
    mixed_ref[...] = to_chunk(mix_rows(combine, grads_ref[...])).astype(BF)


def back_early_kernel(
    scale_ref, flags_ref, sums_ref, packed_ref, in_ref, hidden_ref, inverse_ref, logits_ref,
    prob_ref, rows_ref, columns_ref, gain_ref, router_in_ref, gain_in_ref, cotangent_ref, sent_ref,
    grads_ref, outs_ref, send_ref, up_ref, hold_ref, pull_ref, mean_ref, wide_ref, up_sem,
):
    begin_copy(flags_ref[1], cotangent_ref.at[0, 0], sent_ref, up_ref, up_sem)
    chunk = sums_ref.shape[1]
    total = summed(sums_ref)
    outs_ref[...] = total
    end_copy(sent_ref, up_ref, up_sem)
    router, gain_sum = back_body(
        scale_ref[0], to_row(packed_ref[:chunk]), to_row(total), in_ref, hidden_ref,
        inverse_ref, logits_ref, prob_ref, rows_ref, up_ref, columns_ref, gain_ref, grads_ref,
        hold_ref, pull_ref, mean_ref,
    )
    router = router + router_in_ref[...]
    peers = send_ref.shape[0]
    count = router.shape[0] // peers
    for k in range(count):
        put_rows(wide_ref, k * chunk, router[k * peers : (k + 1) * peers])
    gain_row = jnp.sum(gain_sum + gain_in_ref[...], axis=0, keepdims=True)
    wide_ref[:, count * chunk :, :] = jnp.broadcast_to(
        to_chunk(gain_row)[None], (peers, chunk, LANES)
    )
    send_ref[...] = wide_ref[...].astype(BF)


def final_kernel(chunks_ref, weights_ref, router_ref, gain_ref):
    weights, inverse = scaled_weights(weights_ref)
    total = jnp.sum(chunks_ref[...].astype(F32), axis=0)
    count = weights.shape[0]
    chunk = weights.shape[1] // LANES
    rows = [to_row(total[k * chunk : (k + 1) * chunk]) for k in range(count)]
    pulled = jnp.concatenate(rows, axis=0)
    dots = jnp.sum(pulled * weights, axis=1, keepdims=True)
    router_ref[...] = (inverse * (pulled - weights * (dots * inverse * inverse))).astype(BF)
    gain_ref[...] = to_row(total[count * chunk :])


def shards(
    tokens,
    cotangent,
    inflow,
    backflow,
    norm_gain,
    slot_scale,
    router_weight,
    expert_in,
    expert_back,
):
    section_index = lax.axis_index("section")
    is_first = section_index == 0
    is_last = section_index == lax.axis_size("section") - 1
    flags = jnp.stack([is_first, is_last]).astype(jnp.int32)
    group = lax.axis_size(DP)
    patches = tokens.shape[2]
    width = tokens.shape[3]
    chunk = width // LANES
    local = router_weight.shape[2]
    slots = local * group
    hidden_units = expert_in.shape[2]
    first_weight = expert_in[0]
    second_weight = expert_back[0]
    weights = router_weight[0].T
    token_block = ((patches, width), BF)
    column = ((patches, LANES), F32)
    table = ((slots, patches), F32)
    rows = ((8, patches), F32)
    single = ((group, chunk, LANES), BF)
    double = ((group, 2 * chunk, LANES), BF)
    every_slot = ((group, width), BF)
    every_hidden = ((group, hidden_units), BF)
    copy_sem = pltpu.SemaphoreType.DMA

    columns_block = run(
        columns_kernel, [((group, local * chunk, LANES), BF)], [], 1000000, 1, weights
    )[0]
    (
        send, start_in, columns, hidden_early, inverse_early, logits_early, prob_early,
        rows_early, mixed_last,
    ) = run(
        early_kernel,
        [
            single, token_block, ((slots, width), BF), token_block, column, table, table, rows,
            ((chunk, LANES), BF),
        ],
        [token_block, ((group, local * chunk, LANES), F32), column, copy_sem, copy_sem],
        300000000,
        4,
        slot_scale,
        flags,
        exchange(columns_block, DP),
        norm_gain,
        tokens,
        inflow,
        cotangent,
    )
    sent_in = section_shift(start_in, 1)
    part, slot_early, act_early, slope_early = run(
        expert_early_kernel,
        [single, every_slot, every_hidden, ((group, hidden_units), F32)],
        [((group, chunk, LANES), F32)],
        70000000,
        3,
        exchange(send, DP),
        first_weight,
        second_weight,
    )
    packed = run(
        pack_kernel, [((chunk + 8, LANES), F32)], [], 1000000, 2, exchange(part, DP), rows_early
    )[0]
    moved = section_shift(packed, 1)

    base = jnp.where(is_first, tokens[1, 0], sent_in)
    (
        send, late_in, hidden_late, inverse_late, logits_late, prob_late, rows_late, late_up,
    ) = run(
        late_kernel,
        [double, token_block, token_block, column, table, table, rows, token_block],
        [column, column, copy_sem],
        400000000,
        6,
        slot_scale,
        flags,
        base,
        moved,
        columns,
        norm_gain,
        cotangent,
        backflow,
    )
    parts, slot_late, mixed_late, act_late, pre_grad_late = run(
        expert_late_kernel,
        [double, every_slot, every_slot, every_hidden, every_hidden],
        [((group, 2 * chunk, LANES), F32)],
        140000000,
        3,
        exchange(send, DP),
        first_weight,
        second_weight,
    )
    back_scratch = [((patches, width), F32), column, column]
    grads_late, mixed_before, outs_late, router_late, gain_late = run(
        back_late_kernel,
        [
            token_block, ((chunk, LANES), BF), ((2 * chunk, LANES), F32), ((slots, width), F32),
            ((8, width), F32),
        ],
        back_scratch,
        600000000,
        12,
        slot_scale,
        exchange(parts, DP),
        late_in,
        hidden_late,
        inverse_late,
        logits_late,
        prob_late,
        rows_late,
        late_up,
        columns,
        norm_gain,
        moved,
    )
    moved_back, held_grads = lax.optimization_barrier(
        (section_shift(mixed_before, -1), grads_late)
    )
    sent_grads = section_shift(held_grads, -1)
    send = run(spread_kernel, [single], [], 1000000, 2, moved_back, mixed_last)[0]
    part, mixed_early_all, pre_grad_early = run(
        expert_back_kernel,
        [single, every_slot, every_hidden],
        [((group, chunk, LANES), F32)],
        70000000,
        4,
        exchange(send, DP),
        slope_early,
        first_weight,
        second_weight,
    )
    last_rows = (local + 1) * chunk
    grads_early, outs_early, finals = run(
        back_early_kernel,
        [token_block, ((chunk, LANES), F32), ((group, last_rows, LANES), BF)],
        [token_block] + back_scratch + [((group, last_rows, LANES), F32), copy_sem],
        600000000,
        14,
        slot_scale,
        flags,
        exchange(part, DP),
        packed,
        start_in,
        hidden_early,
        inverse_early,
        logits_early,
        prob_early,
        rows_early,
        columns,
        norm_gain,
        router_late,
        gain_late,
        cotangent,
        sent_grads,
    )
    router_grad, gain_total = run(
        final_kernel,
        [((local, width), BF), ((1, width), F32)],
        [],
        1000000,
        2,
        exchange(finals, DP),
        weights,
    )

    first_grad = dot_dims(
        jnp.concatenate([slot_early, slot_late], axis=0),
        jnp.concatenate([pre_grad_early, pre_grad_late], axis=0),
        0,
        0,
    )
    second_grad = dot_dims(
        jnp.concatenate([act_early, act_late], axis=0),
        jnp.concatenate([mixed_early_all, mixed_late], axis=0),
        0,
        0,
    )
    slot_out = jnp.stack([packed[:chunk].reshape(1, width), outs_late[:chunk].reshape(1, width)])
    slot_grad = jnp.stack([outs_early.reshape(1, width), outs_late[chunk:].reshape(1, width)])
    return (
        jnp.stack([grads_early, grads_late])[None, :, None],
        slot_out.astype(BF)[None],
        slot_grad.astype(BF)[None],
        first_grad.astype(BF)[None],
        second_grad.astype(BF)[None],
        router_grad.T[None],
        gain_total,
    )


def solution(mesh):
    fine = Mesh(mesh.devices.reshape(mesh.shape["section"], 2, 4, 4), AXES)
    in_specs = (
        P(None, DP, None, None),
        P(None, DP, None, None),
        P("section", DP, None, None),
        P("section", DP, None, None),
        P("section", None),
        P("section"),
        P("section", None, DP),
        P("section", None, DP),
        P("section", DP, None),
    )
    out_specs = (
        P("section", None, DP, None, None),
        P("section", None, DP, None),
        P("section", None, DP, None),
        P("section", None, DP),
        P("section", DP, None),
        P("section", None, DP),
        P("section", None),
    )
    return jax.shard_map(shards, mesh=fine, in_specs=in_specs, out_specs=out_specs, check_vma=False)
```

time: 245 us -> 214 us (0.87)
  other arithmetic: 17.6 us -> 2.94 us
  waiting for transfers between devices: 51.4 us -> 39.5 us
  local copies, waits for them, and re-layouts: 14.7 us -> 4.77 us
  blocking collectives: 97.4 us -> 107 us
  starting transfers between devices: 29.4 us -> 26.7 us
    all_to_all x5 -> x6, blocking collectives: 97.4 us -> 107 us  [exchange(): return lax.all_to_all(chunks, axes, 0, 0, tiled=True)]
    select_n x4 -> x0, other arithmetic: 7.38 us -> none  [the longest x1 3.35 us: shards(): late_up = jnp.where(is_last, cotangent[1, 0], backflow[0, 0])]
    all_to_all x3 -> x2, waiting for transfers between devices: 37.6 us -> 30.7 us  [exchange(): return lax.all_to_all(chunks, axes, 0, 0, tiled=True)]
    unnamed x96 -> x24, local copies, waits for them, and re-layouts: 11.6 us -> 4.72 us
    ppermute x4, waiting for transfers between devices: 13.8 us -> 8.81 us  [section_shift(): return lax.ppermute(block, 'section', route)]
    all_to_all x3 -> x2, starting transfers between devices: 21.7 us -> 17 us  [exchange(): return lax.all_to_all(chunks, axes, 0, 0, tiled=True)]
    pallas_call x9 -> x11, Pallas kernels: 28.1 us -> 27.7 us  [run(): pl.pallas_call(body, out_shape=[jax.ShapeDtypeStruct(shape, kind) for sha...]
  transfers between devices with their start and end apart: 7 -> 6, of which waited for: 5 -> 4; matrix products, arithmetic and copies ran while one was open for 7% -> 3% of each run, Pallas kernels for 4% -> 1%
where the time goes in v3:
time: 214 us; the launch traced here: 213 us
  blocking collectives  107 us (50%)
  waiting for transfers between devices  39.5 us (18%)
  Pallas kernels  27.7 us (13%)
  starting transfers between devices  26.7 us (12%)
  local copies, waits for them, and re-layouts  4.77 us (2%)
  other arithmetic  2.94 us (1%)
  matrix products  2.87 us (1%)
    all_to_all x6, blocking collectives, exchange(): return lax.all_to_all(chunks, axes, 0, 0, tiled=True)  107 us
    all_to_all x2, waiting for transfers between devices, exchange(): return lax.all_to_all(chunks, axes, 0, 0, tiled=True)  30.7 us
    pallas_call x11, Pallas kernels, run(): pl.pallas_call(body, out_shape=[jax.ShapeDtypeStruct(shape, kind) for sha...  27.7 us
    all_to_all x2, starting transfers between devices, exchange(): return lax.all_to_all(chunks, axes, 0, 0, tiled=True)  17 us
    ppermute x4, starting transfers between devices, section_shift(): return lax.ppermute(block, 'section', route)  9.71 us
    ppermute x4, waiting for transfers between devices, section_shift(): return lax.ppermute(block, 'section', route)  8.81 us
    unnamed x24, local copies, waits for them, and re-layouts  4.72 us
  transfers between devices with their start and end apart: 6, of which 4 were waited for; matrix products, arithmetic and copies ran while one was open for 3% of the time, Pallas kernels for 1%

profile of v3, /device:TPU:32, one launch (start us, length us, event | category | flops | bytes accessed | tf_op | source)
XLA Modules:
  0.0 213.1 jit_solution(17095406924430778984)
XLA Ops:
  0.6 0.0 copy-start.6
  0.6 0.0 copy-start.10
  0.7 0.8 copy-done.10
  1.4 1.0 shard_map.144
  2.4 13.0 %all-to-all-start = ((bf16[32,64,128]{2,1,0:T(8,128)(2,1)}), bf16[32,64,128]{2,1,0:T(8,128)(2,1)S(1)}, u32[]{:S(2)}, u32[]{:S(2)}) async-start(bf16[32,64,128]{2,1,0:T(8,128)(2,1)} %shard_map.144), calls=%async_computation | async-start | bytes 1048576 | tf_op jit(solution)/shard_map/all_to_all | solution.py:29
  16.1 0.1 add_convert_fusion.flags_ref
  16.2 20.4 %all-to-all-done.chunks_ref = bf16[32,64,128]{2,1,0:T(8,128)(2,1)S(1)} async-done(((bf16[32,64,128]{2,1,0:T(8,128)(2,1)}), bf16[32,64,128]{2,1,0:T(8,128)(2,1)S(1)}, u32[]{:S(2)}, u32[]{:S(2)}) %all-to-all-start) | async-done | bytes 524320 | tf_op jit(solution)/shard_map/all_to_all | solution.py:29
  36.5 0.0 copy-done.6
  36.6 1.6 copy-done
  38.1 1.6 copy-done.4
  39.7 0.7 copy-done.8
  40.4 4.4 %shard_map.145 = (bf16[32,16,128]{2,1,0:T(8,128)(2,1)S(1)}, bf16[256,2048]{1,0:T(8,128)(2,1)S(1)}, bf16[128,2048]{1,0:T(8,128)(2,1)S(1)}, bf16[256,2048]{1,0:T(8...) custom-call(f32[1]{0:T(128)S(6)} %copy.21.scale_ref, ...), custom_call_target="tpu_custom_call" | custom-call | flops 300000000 | bytes 4000000 | tf_op jit(solution)/shard_map/pallas_call | solution.py:44
  44.8 0.0 copy-start.5
  44.8 2.1 collective-permute-start
  46.9 16.8 %all_to_all.40.slots_ref = bf16[32,16,128]{2,1,0:T(8,128)(2,1)S(1)} all-to-all(bf16[32,16,128]{2,1,0:T(8,128)(2,1)S(1)} %get-tuple-element.49), channel_id=1, replica_groups=mesh['section'=8,'zh'=2,'y'=4,'x'=4] {'zh','y','x'}, dimensions={0} | all-to-all | bytes 262144 | tf_op jit(solution)/shard_map/all_to_all | solution.py:29
  63.7 0.0 copy-done.2
  63.7 0.8 shard_map.146
  64.5 0.0 copy-start.1
  64.6 0.0 copy-start.7
  64.6 0.0 copy-start.9
  64.6 16.3 %all_to_all.41.sums_ref = bf16[32,16,128]{2,1,0:T(8,128)(2,1)S(1)} all-to-all(bf16[32,16,128]{2,1,0:T(8,128)(2,1)S(1)} %get-tuple-element.50), channel_id=1, replica_groups=mesh['section'=8,'zh'=2,'y'=4,'x'=4] {'zh','y','x'}, dimensions={0} | all-to-all | bytes 262144 | tf_op jit(solution)/shard_map/all_to_all | solution.py:29
  80.9 1.9 collective-permute-start.1
  82.9 0.0 collective-permute-done
  82.9 0.1 bitcast_select_fusion.base_ref
  83.0 7.5 %collective-permute-done.1.moved_ref = f32[24,128]{1,0:T(8,128)S(1)} collective-permute-done((f32[24,128]{1,0:T(8,128)S(1)}, f32[24,128]{1,0:T(8,128)S(1)}, u32[]{:S(2)}, u32[]{:S(2)}) %collective-permute-start.1) | collective-permute-done | bytes 12320 | tf_op jit(solution)/shard_map/ppermute | solution.py:35
  90.5 0.0 copy-done.1
  90.5 0.0 copy-done.9
  90.5 5.6 %shard_map.148 = (bf16[32,32,128]{2,1,0:T(8,128)(2,1)S(1)}, bf16[256,2048]{1,0:T(8,128)(2,1)S(1)}, bf16[256,2048]{1,0:T(8,128)(2,1)S(1)}, f32[256,128]{1,0:T(8,1...) custom-call(f32[1]{0:T(128)S(6)} %copy.21.scale_ref, ...), custom_call_target="tpu_custom_call" | custom-call | flops 400000000 | bytes 4000000 | tf_op jit(solution)/shard_map/pallas_call | solution.py:44
  96.2 16.6 %all_to_all.42.pairs_ref = bf16[32,32,128]{2,1,0:T(8,128)(2,1)S(1)} all-to-all(bf16[32,32,128]{2,1,0:T(8,128)(2,1)S(1)} %get-tuple-element.53), channel_id=1, replica_groups=mesh['section'=8,'zh'=2,'y'=4,'x'=4] {'zh','y','x'}, dimensions={0} | all-to-all | bytes 524288 | tf_op jit(solution)/shard_map/all_to_all | solution.py:29
  112.8 1.2 shard_map.149
  114.0 17.3 %all_to_all.43.sums_ref = bf16[32,32,128]{2,1,0:T(8,128)(2,1)S(1)} all-to-all(bf16[32,32,128]{2,1,0:T(8,128)(2,1)S(1)} %get-tuple-element.54), channel_id=1, replica_groups=mesh['section'=8,'zh'=2,'y'=4,'x'=4] {'zh','y','x'}, dimensions={0} | all-to-all | bytes 524288 | tf_op jit(solution)/shard_map/all_to_all | solution.py:29
  131.3 5.2 %shard_map.150 = (bf16[256,2048]{1,0:T(8,128)(2,1)S(1)}, bf16[16,128]{1,0:T(8,128)(2,1)S(1)}, f32[32,128]{1,0:T(8,128)S(1)}, f32[128,2048]{1,0:T(8,128)S(1)}, f32[8,2048]{1,0:T(8,128)S(1)}) custom-call(f32[1]{0:T(128)S(6)} %copy.21.scale_ref, bf16[32,32,128]{2,1,0:T(8,128)(2,1)S(1)} %all_to_all.43.sums_ref, bf16[256,2048]{1,0:T(8,128)(2,1)S(1)} %get-tuple-element.55.in_ref, ...), custom_call_target="tpu_custom_call" | custom-call | flops 600000000 | bytes 4000000 | tf_op jit(solution)/shard_map/pallas_call | solution.py:44
  136.5 1.9 collective-permute-start.2
  138.4 1.3 collective-permute-done.2.moved_ref
  139.7 3.8 %collective-permute-start.3 = (bf16[256,2048]{1,0:T(8,128)(2,1)S(1)}, bf16[256,2048]{1,0:T(8,128)(2,1)S(1)}, u32[]{:S(2)}, u32[]{:S(2)}) collective-permute-start(bf16[256,2048]{1,0:T(8,128)(2,1)S(1)} %get-tuple-element.74), channel_id=1, source_target_pairs={{32,0},{64,32},{96,64},{128,96},{160,128},{192,160},{224,192},{33,... | collective-permute-start | bytes 3145736 | tf_op jit(solution)/shard_map/ppermute | solution.py:35
  143.6 17.9 %all_to_all.44.mixed_in_ref = bf16[32,16,128]{2,1,0:T(8,128)(2,1)S(1)} all-to-all(bf16[32,16,128]{2,1,0:T(8,128)(2,1)S(1)} %shard_map.151), channel_id=1, replica_groups=mesh['section'=8,'zh'=2,'y'=4,'x'=4] {'zh','y','x'}, dimensions={0} | all-to-all | bytes 262144 | tf_op jit(solution)/shard_map/all_to_all | solution.py:29
  161.5 1.3 shard_map.152
  162.9 22.1 %all_to_all.45.sums_ref = bf16[32,16,128]{2,1,0:T(8,128)(2,1)S(1)} all-to-all(bf16[32,16,128]{2,1,0:T(8,128)(2,1)S(1)} %get-tuple-element.67), channel_id=1, replica_groups=mesh['section'=8,'zh'=2,'y'=4,'x'=4] {'zh','y','x'}, dimensions={0} | all-to-all | bytes 262144 | tf_op jit(solution)/shard_map/all_to_all | solution.py:29
  185.0 0.0 collective-permute-done.3.sent_ref
  185.0 7.3 %shard_map.153 = (bf16[256,2048]{1,0:T(8,128)(2,1)S(1)}, f32[16,128]{1,0:T(8,128)S(1)}, bf16[32,80,128]{2,1,0:T(8,128)(2,1)}) custom-call(f32[1]{0:T(128)S(6)} %copy.21.scale_ref, s32[2]{0:T(128)S(1)} %add_convert_fusion.flags_ref, bf16[32,16,128]{2,1,0:T(8,128)(2,1)S(1)} %all_to_all.45.sums_ref, f32[24,128]{1,0:T(8,128)S(1)} %shard_map.147.packed_ref, ...), custom_call_target="tpu_custom_call" | custom-call | flops 600000000 | bytes 4000000 | tf_op jit(solution)/shard_map/pallas_call | solution.py:44
  192.3 3.9 %all-to-all-start.7 = ((bf16[32,80,128]{2,1,0:T(8,128)(2,1)}), bf16[32,80,128]{2,1,0:T(8,128)(2,1)S(1)}, u32[]{:S(2)}, u32[]{:S(2)}) async-start(bf16[32,80,128]{2,1,0:T(8,128)(2,1)} %get-tuple-element.86), calls=%async_computation.7 | async-start | bytes 1310720 | tf_op jit(solution)/shard_map/all_to_all | solution.py:29
  196.3 0.6 pad_maximum_fusion
  196.9 1.4 fusion.1
  198.3 1.4 fusion
  199.8 0.6 pad_maximum_fusion.1
  200.4 1.5 maximum_bitcast_fusion
  201.9 10.3 %all-to-all-done.7.chunks_ref = bf16[32,80,128]{2,1,0:T(8,128)(2,1)S(1)} async-done(((bf16[32,80,128]{2,1,0:T(8,128)(2,1)}), bf16[32,80,128]{2,1,0:T(8,128)(2,1)S(1)}, u32[]{:S(2)}, u32[]{:S(2)}) %all-to-all-start.7) | async-done | bytes 655392 | tf_op jit(solution)/shard_map/all_to_all | solution.py:29
  212.2 0.8 shard_map.154
  (20 shorter events, 0.1 us)
Async XLA Ops:
  0.6 35.9 %copy-start.6 = (bf16[1,1,256,2048]{3,2,1,0:T(8,128)(2,1)S(1)}, bf16[1,1,256,2048]{3,2,1,0:T(8,128)(2,1)}, u32[]{:S(2)}) copy-start(bf16[1,1,256,2048]{3,2,1,0:T(8,128)(2,1)} %inflow_ref.1) | copy-start | bytes 3145732
  0.6 0.8 copy-start.10
  2.4 34.1 %all-to-all-start = ((bf16[32,64,128]{2,1,0:T(8,128)(2,1)}), bf16[32,64,128]{2,1,0:T(8,128)(2,1)S(1)}, u32[]{:S(2)}, u32[]{:S(2)}) async-start(bf16[32,64,128]{2,1,0:T(8,128)(2,1)} %shard_map.144), calls=%async_computation | async-start | bytes 1048576 | tf_op jit(solution)/shard_map/all_to_all | solution.py:29
  36.5 1.6 copy-start
  38.1 1.6 copy-start.4
  39.7 0.7 copy-start.8
  40.4 23.3 %copy-start.2 = (bf16[1,2048,256]{2,1,0:T(8,128)(2,1)S(1)}, bf16[1,2048,256]{2,1,0:T(8,128)(2,1)}, u32[]{:S(2)}) copy-start(bf16[1,2048,256]{2,1,0:T(8,128)(2,1)} %param.16) | copy-start | bytes 3145732
  40.4 23.3 %copy-start.3 = (bf16[1,256,2048]{2,1,0:T(8,128)(2,1)S(1)}, bf16[1,256,2048]{2,1,0:T(8,128)(2,1)}, u32[]{:S(2)}) copy-start(bf16[1,256,2048]{2,1,0:T(8,128)(2,1)} %param.17) | copy-start | bytes 3145732
  44.8 38.1 %copy-start.5 = (bf16[2,1,256,2048]{3,2,1,0:T(8,128)(2,1)S(1)}, bf16[2,1,256,2048]{3,2,1,0:T(8,128)(2,1)}, u32[]{:S(2)}) copy-start(bf16[2,1,256,2048]{3,2,1,0:T(8,128)(2,1)} %tokens_ref.1) | copy-start | bytes 6291460
  44.8 38.1 %collective-permute-start = (bf16[256,2048]{1,0:T(8,128)(2,1)S(1)}, bf16[256,2048]{1,0:T(8,128)(2,1)S(1)}, u32[]{:S(2)}, u32[]{:S(2)}) collective-permute-start(bf16[256,2048]{1,0:T(8,128)(2,1)S(1)} %get-tuple-element.48.in_ref), channel_id=1, source_target_pairs={{0,32},{32,64},{64,96},{96,128},{128,160},{160,192},{192,224},{1,3... | collective-permute-start | bytes 3145736 | tf_op jit(solution)/shard_map/ppermute | solution.py:35
  64.5 26.0 %copy-start.1 = (bf16[2,1,256,2048]{3,2,1,0:T(8,128)(2,1)S(1)}, bf16[2,1,256,2048]{3,2,1,0:T(8,128)(2,1)}, u32[]{:S(2)}) copy-start(bf16[2,1,256,2048]{3,2,1,0:T(8,128)(2,1)} %cotangent_ref.5) | copy-start | bytes 6291460
  64.6 26.0 %copy-start.7 = (bf16[1,1,256,2048]{3,2,1,0:T(8,128)(2,1)S(1)}, bf16[1,1,256,2048]{3,2,1,0:T(8,128)(2,1)}, u32[]{:S(2)}) copy-start(bf16[1,1,256,2048]{3,2,1,0:T(8,128)(2,1)} %backflow_ref.1) | copy-start | bytes 3145732
  64.6 25.9 %copy-start.9 = (f32[1,2048]{1,0:T(1,128)S(1)}, f32[1,2048]{1,0:T(1,128)}, u32[]{:S(2)}) copy-start(f32[1,2048]{1,0:T(1,128)} %gain_ref.7) | copy-start | bytes 24580
  80.9 9.6 %collective-permute-start.1 = (f32[24,128]{1,0:T(8,128)S(1)}, f32[24,128]{1,0:T(8,128)S(1)}, u32[]{:S(2)}, u32[]{:S(2)}) collective-permute-start(f32[24,128]{1,0:T(8,128)S(1)} %shard_map.147.packed_ref), channel_id=1, source_target_pairs={{0,32},{32,64},{64,96},{96,128},{128,160},{160,192},{192,224},{1,3... | collective-permute-start | bytes 36872 | tf_op jit(solution)/shard_map/ppermute | solution.py:35
  136.5 3.2 %collective-permute-start.2 = (bf16[16,128]{1,0:T(8,128)(2,1)S(1)}, bf16[16,128]{1,0:T(8,128)(2,1)S(1)}, u32[]{:S(2)}, u32[]{:S(2)}) collective-permute-start(bf16[16,128]{1,0:T(8,128)(2,1)S(1)} %get-tuple-element.62), channel_id=1, source_target_pairs={{32,0},{64,32},{96,64},{128,96},{160,128},{192,160},{224,192},{33,... | collective-permute-start | bytes 12296 | tf_op jit(solution)/shard_map/ppermute | solution.py:35
  139.7 45.3 %collective-permute-start.3 = (bf16[256,2048]{1,0:T(8,128)(2,1)S(1)}, bf16[256,2048]{1,0:T(8,128)(2,1)S(1)}, u32[]{:S(2)}, u32[]{:S(2)}) collective-permute-start(bf16[256,2048]{1,0:T(8,128)(2,1)S(1)} %get-tuple-element.74), channel_id=1, source_target_pairs={{32,0},{64,32},{96,64},{128,96},{160,128},{192,160},{224,192},{33,... | collective-permute-start | bytes 3145736 | tf_op jit(solution)/shard_map/ppermute | solution.py:35
  192.3 19.9 %all-to-all-start.7 = ((bf16[32,80,128]{2,1,0:T(8,128)(2,1)}), bf16[32,80,128]{2,1,0:T(8,128)(2,1)S(1)}, u32[]{:S(2)}, u32[]{:S(2)}) async-start(bf16[32,80,128]{2,1,0:T(8,128)(2,1)} %get-tuple-element.86), calls=%async_computation.7 | async-start | bytes 1310720 | tf_op jit(solution)/shard_map/all_to_all | solution.py:29
  200.4 11.8 %copy-start.11 = (bf16[1,2048,4]{1,2,0:T(4,128)(2,1)S(1)}, bf16[1,2048,4]{1,2,0:T(4,128)(2,1)}, u32[]{:S(2)}) copy-start(bf16[1,2048,4]{1,2,0:T(4,128)(2,1)} %param.15) | copy-start | bytes 49156

commit v4 on v3

--- a/solution.py
+++ b/solution.py
@@ -29,10 +29,9 @@
     return lax.all_to_all(chunks, axes, 0, 0, tiled=True)
 
 
-def section_shift(block, distance):
+def section_ring(block, distance):
     sections = lax.axis_size("section")
-    route = [(i, i + distance) for i in range(sections) if 0 <= i + distance < sections]
-    return lax.ppermute(block, "section", route)
+    return lax.ppermute(block, "section", [(i, (i + distance) % sections) for i in range(sections)])
 
 
 def run(body, outs, scratch, flops, near, *operands):
@@ -43,11 +42,13 @@
 
     return pl.pallas_call(
         body,
-        out_shape=[jax.ShapeDtypeStruct(shape, kind) for shape, kind in outs],
+        out_shape=[jax.ShapeDtypeStruct(item[0], item[1]) for item in outs],
         in_specs=[
             pl.BlockSpec(memory_space=place(index, item)) for index, item in enumerate(operands)
         ],
-        out_specs=[pl.BlockSpec(memory_space=pltpu.VMEM) for _ in outs],
+        out_specs=[
+            pl.BlockSpec(memory_space=pltpu.VMEM if len(item) == 2 else pl.ANY) for item in outs
+        ],
         scratch_shapes=[
             pltpu.VMEM(*item) if isinstance(item, tuple) else item for item in scratch
         ],
@@ -174,62 +175,58 @@
     return mixed[:1] + mixed[1:2]
 
 
+def norm_kernel(
+    flags_ref, aux_ref, tokens_ref, inflow_ref,
+    start_ref, hidden_out, inverse_ref, length_ref,
+    in_ref, hidden_ref, sums_ref, in_sem, out_sem, hidden_sem,
+):
+    begin_copy(flags_ref[0], tokens_ref.at[0, 0], inflow_ref.at[0, 0], in_ref, in_sem)
+    end_copy(inflow_ref.at[0, 0], in_ref, in_sem)
+    pltpu.make_async_copy(in_ref, start_ref, out_sem).start()
+
+    def square_rows(window):
+        wide = in_ref[window, :].astype(F32)
+        sums_ref[window, :] = lane_sums(wide * wide)
+
+    passes(in_ref, square_rows)
+    length = norm_passes(in_ref, aux_ref[:1], hidden_ref, inverse_ref, sums_ref)
+    length_ref[...] = jnp.broadcast_to(length, length_ref.shape)
+    pltpu.make_async_copy(hidden_ref, hidden_out, hidden_sem).start()
+    end_copy(in_ref, start_ref, out_sem)
+    end_copy(hidden_ref, hidden_out, hidden_sem)
+
+
 def early_kernel(
-    scale_ref, flags_ref, chunks_ref, gain_ref, tokens_ref, inflow_ref, cotangent_ref,
-    send_ref, in_ref, columns_ref, hidden_ref, inverse_ref, logits_ref, prob_ref, rows_ref,
-    mixed_ref, up_ref, wide_ref, sums_ref, in_sem, up_sem,
-):
-    begin_copy(flags_ref[0], tokens_ref.at[0, 0], inflow_ref.at[0, 0], in_ref, in_sem)
-    last = flags_ref[1] != 0
-
-    @pl.when(last)
-    def _():
-        pltpu.make_async_copy(cotangent_ref.at[0, 0], up_ref, up_sem).start()
-
+    flags_ref, chunks_ref, length_ref, aux_ref, hidden_in, start_in, tokens_ref,
+    send_ref, columns_ref, logits_ref, prob_ref, rows_ref, base_ref,
+    hidden_ref, wide_ref, hidden_sem, base_sem,
+):
+    pltpu.make_async_copy(hidden_in, hidden_ref, hidden_sem).start()
+    begin_copy(flags_ref[1], tokens_ref.at[1, 0], start_in, base_ref, base_sem)
     peers = chunks_ref.shape[0]
-    chunk = gain_ref.shape[1] // LANES
+    chunk = aux_ref.shape[1] // LANES
     wide_ref[...] = chunks_ref[...].astype(F32)
     for k in range(chunks_ref.shape[1] // chunk):
         columns_ref[k * peers : (k + 1) * peers] = wide_rows(wide_ref, k * chunk, chunk).astype(BF)
-    end_copy(inflow_ref.at[0, 0], in_ref, in_sem)
-
-    def square_rows(window):
-        wide = in_ref[window, :].astype(F32)
-        sums_ref[window, :] = lane_sums(wide * wide)
-
-    passes(in_ref, square_rows)
-    length = norm_passes(in_ref, gain_ref[...], hidden_ref, inverse_ref, sums_ref)
-    combine, slot = slot_front(
-        scale_ref[0], columns_ref, hidden_ref, length, logits_ref, prob_ref, rows_ref
+    end_copy(hidden_in, hidden_ref, hidden_sem)
+    _, slot = slot_front(
+        aux_ref[1:2, :1], columns_ref, hidden_ref, length_ref[:1], logits_ref, prob_ref, rows_ref
     )
     send_ref[...] = jnp.broadcast_to(to_chunk(slot).astype(BF)[None], send_ref.shape)
-    mixed_ref[...] = jnp.zeros_like(mixed_ref)
-
-    @pl.when(last)
-    def _():
-        end_copy(cotangent_ref.at[0, 0], up_ref, up_sem)
-        mixed_ref[...] = to_chunk(mix_rows(combine, up_ref[...])).astype(BF)
-
-
-def pack_kernel(sums_ref, rows_ref, out_ref):
-    total = summed(sums_ref)
-    combine = to_chunk(rows_ref[1:2])
-    count = total.shape[0]
-    out_ref[:count] = total
-    out_ref[count:] = jnp.concatenate(
-        [combine, jnp.zeros((out_ref.shape[0] - count - combine.shape[0], LANES), F32)], axis=0
-    )
+    end_copy(start_in, base_ref, base_sem)
 
 
 def late_kernel(
-    scale_ref, flags_ref, base_ref, moved_ref, columns_ref, gain_ref, cotangent_ref, backflow_ref,
-    send_ref, in_ref, hidden_ref, inverse_ref, logits_ref, prob_ref, rows_ref, up_ref,
+    flags_ref, sums_in, rows_in, base_ref, columns_ref, aux_ref, backflow_ref, cotangent_ref,
+    send_ref, in_ref, hidden_ref, inverse_ref, logits_ref, prob_ref, rows_ref, up_ref, out_ref,
     sums_ref, comb_ref, up_sem,
 ):
-    begin_copy(flags_ref[1], cotangent_ref.at[1, 0], backflow_ref.at[0, 0], up_ref, up_sem)
-    chunk = gain_ref.shape[1] // LANES
-    out_row = to_row(moved_ref[:chunk])
-    comb_ref[...] = to_column(to_row(moved_ref[chunk : chunk + 2]))
+    begin_copy(flags_ref[2], cotangent_ref.at[1, 0], backflow_ref, up_ref, up_sem)
+    total = summed(sums_in)
+    out_ref[...] = total
+    out_row = to_row(total)
+    before = rows_in[1:2]
+    comb_ref[...] = to_column(jnp.where(flags_ref[1] != 0, jnp.zeros_like(before), before))
 
     def add_rows(window):
         base = base_ref[window, :].astype(F32)
@@ -239,11 +236,11 @@
         sums_ref[window, :] = lane_sums(wide * wide)
 
     passes(in_ref, add_rows)
-    length = norm_passes(in_ref, gain_ref[...], hidden_ref, inverse_ref, sums_ref)
+    length = norm_passes(in_ref, aux_ref[:1], hidden_ref, inverse_ref, sums_ref)
     combine, slot = slot_front(
-        scale_ref[0], columns_ref, hidden_ref, length, logits_ref, prob_ref, rows_ref
-    )
-    end_copy(backflow_ref.at[0, 0], up_ref, up_sem)
+        aux_ref[1:2, :1], columns_ref, hidden_ref, length, logits_ref, prob_ref, rows_ref
+    )
+    end_copy(backflow_ref, up_ref, up_sem)
     mixed = mix_rows(combine, up_ref[...])
     both = jnp.concatenate([to_chunk(slot), to_chunk(mixed)], axis=0).astype(BF)
     send_ref[...] = jnp.broadcast_to(both[None], send_ref.shape)
@@ -303,16 +300,12 @@
     send_ref[...] = wide_ref[...].astype(BF)
 
 
-def spread_kernel(moved_ref, own_ref, send_ref):
-    block = (moved_ref[...].astype(F32) + own_ref[...].astype(F32)).astype(BF)
-    send_ref[...] = jnp.broadcast_to(block[None], send_ref.shape)
-
-
 def back_body(
-    scale, out_row, grad_row, in_ref, hidden_ref, inverse_ref, logits_ref, prob_ref, rows_ref,
-    up_ref, columns_ref, gain_ref, grads_ref, hold_ref, pull_ref, mean_ref,
-):
-    gain = gain_ref[...]
+    out_row, grad_row, in_ref, hidden_ref, inverse_ref, logits_ref, prob_ref, rows_ref,
+    up_ref, columns_ref, aux_ref, hold_ref, pull_ref, mean_ref, put_grads,
+):
+    gain = aux_ref[:1]
+    scale = aux_ref[1:2, :1]
     length = rows_ref[0:1]
     combine = rows_ref[1:2]
     spread = rows_ref[2:3]
@@ -352,52 +345,89 @@
         through = hold_ref[window, :] * gain
         wide = in_ref[window, :].astype(F32)
         dinput = inverse * (through - wide * mean_ref[window, :1])
-        grads_ref[window, :] = (up_ref[window, :].astype(F32) + dinput).astype(BF)
+        put_grads(window, (up_ref[window, :].astype(F32) + dinput).astype(BF))
 
     passes(in_ref, grad_rows_pass)
     return router, gain_sum
 
 
 def back_late_kernel(
-    scale_ref, sums_ref, in_ref, hidden_ref, inverse_ref, logits_ref, prob_ref, rows_ref,
-    up_ref, columns_ref, gain_ref, moved_ref,
-    grads_ref, mixed_ref, outs_ref, router_ref, gain_out, hold_ref, pull_ref, mean_ref,
-):
+    flags_ref, sums_ref, in_ref, hidden_ref, inverse_ref, logits_ref, prob_ref, rows_ref,
+    up_ref, columns_ref, aux_ref, before_ref, slot_ref, mixed_ref, act_ref, grad_ref, cotangent_ref,
+    send_ref, pack_ref, next_ref,
+    own_ref, hold_ref, pull_ref, mean_ref, own_sem,
+):
+    last = flags_ref[1] != 0
+
+    @pl.when(last)
+    def _():
+        pltpu.make_async_copy(cotangent_ref.at[0, 0], own_ref, own_sem).start()
+
+    tokens, width = in_ref.shape
     chunk = sums_ref.shape[1] // 2
     total = summed(sums_ref)
-    outs_ref[...] = total
+    out_row = to_row(total[:chunk])
+    grad_row = to_row(total[chunk:])
+
+    @pl.when(last)
+    def _():
+        end_copy(cotangent_ref.at[0, 0], own_ref, own_sem)
+
+    def put_grads(window, value):
+        pack_ref[window, :] = value
+        next_ref[window, :] = jnp.where(last, own_ref[window, :], value)
+
     router, gain_sum = back_body(
-        scale_ref[0], to_row(total[:chunk]), to_row(total[chunk:]), in_ref, hidden_ref,
-        inverse_ref, logits_ref, prob_ref, rows_ref, up_ref, columns_ref, gain_ref, grads_ref,
-        hold_ref, pull_ref, mean_ref,
-    )
-    router_ref[...] = router
-    gain_out[...] = gain_sum
-    combine = to_row(moved_ref[chunk : chunk + 2])
-    mixed_ref[...] = to_chunk(mix_rows(combine, grads_ref[...])).astype(BF)
+        out_row, grad_row, in_ref, hidden_ref, inverse_ref, logits_ref, prob_ref, rows_ref,
+        up_ref, columns_ref, aux_ref, hold_ref, pull_ref, mean_ref, put_grads,
+    )
+    mixed = to_chunk(mix_rows(before_ref[1:2], next_ref[...])).astype(BF)
+    send_ref[...] = jnp.broadcast_to(mixed[None], send_ref.shape)
+    slots = router.shape[0]
+    peers = slot_ref.shape[0]
+    pack_ref[tokens : tokens + slots] = router.astype(BF)
+    gain_row = jnp.sum(gain_sum, axis=0, keepdims=True)
+    place = tokens + slots
+    pack_ref[place : place + STEP] = first_rows([*two_parts(gain_row), out_row, grad_row])
+    place += STEP
+    pack_ref[place : place + peers] = slot_ref[...]
+    pack_ref[place + peers : place + 2 * peers] = mixed_ref[...]
+    place += 2 * peers
+    hidden_units = act_ref.shape[1]
+    pack_ref[place : place + peers, :hidden_units] = act_ref[...]
+    pack_ref[place : place + peers, hidden_units : 2 * hidden_units] = grad_ref[...]
+    rest = jnp.zeros((peers, width - 2 * hidden_units), BF)
+    pack_ref[place : place + peers, 2 * hidden_units :] = rest
 
 
 def back_early_kernel(
-    scale_ref, flags_ref, sums_ref, packed_ref, in_ref, hidden_ref, inverse_ref, logits_ref,
-    prob_ref, rows_ref, columns_ref, gain_ref, router_in_ref, gain_in_ref, cotangent_ref, sent_ref,
-    grads_ref, outs_ref, send_ref, up_ref, hold_ref, pull_ref, mean_ref, wide_ref, up_sem,
-):
-    begin_copy(flags_ref[1], cotangent_ref.at[0, 0], sent_ref, up_ref, up_sem)
+    sums_ref, out_ref, in_ref, hidden_ref, inverse_ref, logits_ref, prob_ref, rows_ref,
+    up_ref, columns_ref, aux_ref, back_ref,
+    grads_ref, outs_ref, send_ref, extra_ref, hold_ref, pull_ref, mean_ref, wide_ref, extra_sem,
+):
+    tokens = in_ref.shape[0]
+    extra = back_ref.at[pl.ds(tokens, extra_ref.shape[0])]
+    pltpu.make_async_copy(extra, extra_ref, extra_sem).start()
     chunk = sums_ref.shape[1]
     total = summed(sums_ref)
     outs_ref[...] = total
-    end_copy(sent_ref, up_ref, up_sem)
+
+    def put_grads(window, value):
+        grads_ref[window, :] = value
+
     router, gain_sum = back_body(
-        scale_ref[0], to_row(packed_ref[:chunk]), to_row(total), in_ref, hidden_ref,
-        inverse_ref, logits_ref, prob_ref, rows_ref, up_ref, columns_ref, gain_ref, grads_ref,
-        hold_ref, pull_ref, mean_ref,
-    )
-    router = router + router_in_ref[...]
+        to_row(out_ref[...]), to_row(total), in_ref, hidden_ref, inverse_ref, logits_ref, prob_ref,
+        rows_ref, up_ref, columns_ref, aux_ref, hold_ref, pull_ref, mean_ref, put_grads,
+    )
+    end_copy(extra, extra_ref, extra_sem)
+    slots = router.shape[0]
+    router = router + extra_ref[:slots].astype(F32)
     peers = send_ref.shape[0]
-    count = router.shape[0] // peers
+    count = slots // peers
     for k in range(count):
         put_rows(wide_ref, k * chunk, router[k * peers : (k + 1) * peers])
-    gain_row = jnp.sum(gain_sum + gain_in_ref[...], axis=0, keepdims=True)
+    late = extra_ref[slots:].astype(F32)
+    gain_row = jnp.sum(gain_sum, axis=0, keepdims=True) + late[:1] + late[1:2]
     wide_ref[:, count * chunk :, :] = jnp.broadcast_to(
         to_chunk(gain_row)[None], (peers, chunk, LANES)
     )
@@ -428,9 +458,9 @@
     expert_back,
 ):
     section_index = lax.axis_index("section")
-    is_first = section_index == 0
-    is_last = section_index == lax.axis_size("section") - 1
-    flags = jnp.stack([is_first, is_last]).astype(jnp.int32)
+    end = lax.axis_size("section") - 1
+    flags = jnp.stack([section_index == 0, section_index == end, section_index == end - 1])
+    flags = flags.astype(jnp.int32)
     group = lax.axis_size(DP)
     patches = tokens.shape[2]
     width = tokens.shape[3]
@@ -454,27 +484,40 @@
     columns_block = run(
         columns_kernel, [((group, local * chunk, LANES), BF)], [], 1000000, 1, weights
     )[0]
-    (
-        send, start_in, columns, hidden_early, inverse_early, logits_early, prob_early,
-        rows_early, mixed_last,
-    ) = run(
+    aux = jnp.concatenate(
+        [norm_gain, jnp.broadcast_to(slot_scale[:, None], (1, width)), jnp.zeros((6, width), F32)]
+    )
+    start_in, hidden_early, inverse_early, length_early = run(
+        norm_kernel,
+        [token_block + ("far",), token_block + ("far",), column, rows],
+        [token_block, token_block, column, copy_sem, copy_sem, copy_sem],
+        30000000,
+        2,
+        flags,
+        aux,
+        tokens,
+        inflow,
+    )
+    ahead = lax.optimization_barrier(
+        (length_early, expert_in[0], expert_back[0], backflow[0, 0], aux)
+    )
+    length_early = ahead[0]
+    first_next, second_next, up_next, aux_next = [section_ring(item, -1) for item in ahead[1:]]
+    send, columns, logits_early, prob_early, rows_early, base = run(
         early_kernel,
-        [
-            single, token_block, ((slots, width), BF), token_block, column, table, table, rows,
-            ((chunk, LANES), BF),
-        ],
-        [token_block, ((group, local * chunk, LANES), F32), column, copy_sem, copy_sem],
+        [single, ((slots, width), BF), table, table, rows, token_block],
+        [token_block, ((group, local * chunk, LANES), F32), copy_sem, copy_sem],
         300000000,
         4,
-        slot_scale,
         flags,
         exchange(columns_block, DP),
-        norm_gain,
+        length_early,
+        aux,
+        hidden_early,
+        start_in,
         tokens,
-        inflow,
-        cotangent,
-    )
-    sent_in = section_shift(start_in, 1)
+    )
+    columns_next = section_ring(columns, -1)
     part, slot_early, act_early, slope_early = run(
         expert_early_kernel,
         [single, every_slot, every_hidden, ((group, hidden_units), F32)],
@@ -485,28 +528,26 @@
         first_weight,
         second_weight,
     )
-    packed = run(
-        pack_kernel, [((chunk + 8, LANES), F32)], [], 1000000, 2, exchange(part, DP), rows_early
-    )[0]
-    moved = section_shift(packed, 1)
-
-    base = jnp.where(is_first, tokens[1, 0], sent_in)
     (
         send, late_in, hidden_late, inverse_late, logits_late, prob_late, rows_late, late_up,
+        out_early,
     ) = run(
         late_kernel,
-        [double, token_block, token_block, column, table, table, rows, token_block],
+        [
+            double, token_block, token_block, column, table, table, rows, token_block,
+            ((chunk, LANES), F32),
+        ],
         [column, column, copy_sem],
         400000000,
         6,
-        slot_scale,
         flags,
+        exchange(part, DP),
+        rows_early,
         base,
-        moved,
-        columns,
-        norm_gain,
+        columns_next,
+        aux_next,
+        up_next,
         cotangent,
-        backflow,
     )
     parts, slot_late, mixed_late, act_late, pre_grad_late = run(
         expert_late_kernel,
@@ -515,20 +556,18 @@
         140000000,
         3,
         exchange(send, DP),
-        first_weight,
-        second_weight,
+        first_next,
+        second_next,
     )
     back_scratch = [((patches, width), F32), column, column]
-    grads_late, mixed_before, outs_late, router_late, gain_late = run(
+    pack_rows = patches + slots + STEP + 3 * group
+    send, pack, early_up = run(
         back_late_kernel,
-        [
-            token_block, ((chunk, LANES), BF), ((2 * chunk, LANES), F32), ((slots, width), F32),
-            ((8, width), F32),
-        ],
-        back_scratch,
+        [single, ((pack_rows, width), BF), token_block],
+        [token_block] + back_scratch + [copy_sem],
         600000000,
-        12,
-        slot_scale,
+        16,
+        flags,
         exchange(parts, DP),
         late_in,
         hidden_late,
@@ -537,15 +576,16 @@
         prob_late,
         rows_late,
         late_up,
-        columns,
-        norm_gain,
-        moved,
-    )
-    moved_back, held_grads = lax.optimization_barrier(
-        (section_shift(mixed_before, -1), grads_late)
-    )
-    sent_grads = section_shift(held_grads, -1)
-    send = run(spread_kernel, [single], [], 1000000, 2, moved_back, mixed_last)[0]
+        columns_next,
+        aux_next,
+        rows_early,
+        slot_late,
+        mixed_late,
+        act_late,
+        pre_grad_late,
+        cotangent,
+    )
+    back = section_ring(pack, 1)
     part, mixed_early_all, pre_grad_early = run(
         expert_back_kernel,
         [single, every_slot, every_hidden],
@@ -561,25 +601,23 @@
     grads_early, outs_early, finals = run(
         back_early_kernel,
         [token_block, ((chunk, LANES), F32), ((group, last_rows, LANES), BF)],
-        [token_block] + back_scratch + [((group, last_rows, LANES), F32), copy_sem],
+        [((slots + STEP, width), BF)]
+        + back_scratch
+        + [((group, last_rows, LANES), F32), copy_sem],
         600000000,
-        14,
-        slot_scale,
-        flags,
+        11,
         exchange(part, DP),
-        packed,
+        out_early,
         start_in,
         hidden_early,
         inverse_early,
         logits_early,
         prob_early,
         rows_early,
+        early_up,
         columns,
-        norm_gain,
-        router_late,
-        gain_late,
-        cotangent,
-        sent_grads,
+        aux,
+        back,
     )
     router_grad, gain_total = run(
         final_kernel,
@@ -591,6 +629,16 @@
         weights,
     )
 
+    place = patches + slots
+    grads_late = back[:patches]
+    out_late = back[place + 2 : place + 3]
+    slot_grad_late = back[place + 3 : place + 4]
+    place += STEP
+    slot_late = back[place : place + group]
+    mixed_late = back[place + group : place + 2 * group]
+    place += 2 * group
+    act_late = back[place:, :hidden_units]
+    pre_grad_late = back[place:, hidden_units : 2 * hidden_units]
     first_grad = dot_dims(
         jnp.concatenate([slot_early, slot_late], axis=0),
         jnp.concatenate([pre_grad_early, pre_grad_late], axis=0),
@@ -603,12 +651,12 @@
         0,
         0,
     )
-    slot_out = jnp.stack([packed[:chunk].reshape(1, width), outs_late[:chunk].reshape(1, width)])
-    slot_grad = jnp.stack([outs_early.reshape(1, width), outs_late[chunk:].reshape(1, width)])
+    slot_out = jnp.stack([out_early.reshape(1, width).astype(BF), out_late])
+    slot_grad = jnp.stack([outs_early.reshape(1, width).astype(BF), slot_grad_late])
     return (
         jnp.stack([grads_early, grads_late])[None, :, None],
-        slot_out.astype(BF)[None],
-        slot_grad.astype(BF)[None],
+        slot_out[None],
+        slot_grad[None],
         first_grad.astype(BF)[None],
         second_grad.astype(BF)[None],
         router_grad.T[None],

time: 214 us -> 241 us (1.13)
  blocking collectives: 107 us -> 44.1 us
  waiting for transfers between devices: 39.5 us -> 77.5 us
  local copies, waits for them, and re-layouts: 4.77 us -> 32.1 us
  starting transfers between devices: 26.7 us -> 43.3 us
  Pallas kernels: 27.7 us -> 34.3 us
    all_to_all x6 -> x2, blocking collectives: 107 us -> 44.1 us  [exchange(): return lax.all_to_all(chunks, axes, 0, 0, tiled=True)]
    all_to_all x2 -> x6, waiting for transfers between devices: 30.7 us -> 69 us  [exchange(): return lax.all_to_all(chunks, axes, 0, 0, tiled=True)]
    unnamed x24 -> x116, local copies, waits for them, and re-layouts: 4.72 us -> 31.8 us
    all_to_all x2 -> x6, starting transfers between devices: 17 us -> 42.8 us  [exchange(): return lax.all_to_all(chunks, axes, 0, 0, tiled=True)]
    ppermute x4 -> x6, starting transfers between devices: 9.71 us -> 0.5 us  [section_ring(): lax.ppermute(block, 'section', [(i, (i + distance) % sections) for i in r...]
    pallas_call x11 -> x10, Pallas kernels: 27.7 us -> 34.3 us  [run(): pl.pallas_call(body, out_shape=[jax.ShapeDtypeStruct(item[0], item[1]) fo...]
    ppermute x4 -> x6, waiting for transfers between devices: 8.81 us -> 8.44 us  [section_ring(): lax.ppermute(block, 'section', [(i, (i + distance) % sections) for i in r...]
  transfers between devices with their start and end apart: 6 -> 12, of which waited for: 4 -> 7; matrix products, arithmetic and copies ran while one was open for 3% -> 3% of each run, Pallas kernels for 1% -> 6%
where the time goes in v4:
time: 241 us; the launch traced here: 239 us
  waiting for transfers between devices  77.5 us (32%)
  blocking collectives  44.1 us (18%)
  starting transfers between devices  43.3 us (18%)
  Pallas kernels  34.3 us (14%)
  local copies, waits for them, and re-layouts  32.1 us (13%)
  other arithmetic  3.6 us (1%)
  matrix products  2.87 us (1%)
    all_to_all x6, waiting for transfers between devices, exchange(): return lax.all_to_all(chunks, axes, 0, 0, tiled=True)  69 us
    all_to_all x2, blocking collectives, exchange(): return lax.all_to_all(chunks, axes, 0, 0, tiled=True)  44.1 us
    all_to_all x6, starting transfers between devices, exchange(): return lax.all_to_all(chunks, axes, 0, 0, tiled=True)  42.8 us
    pallas_call x10, Pallas kernels, run(): pl.pallas_call(body, out_shape=[jax.ShapeDtypeStruct(item[0], item[1]) fo...  34.3 us
    unnamed x116, local copies, waits for them, and re-layouts  31.8 us
    ppermute x6, waiting for transfers between devices, section_ring(): lax.ppermute(block, 'section', [(i, (i + distance) % sections) for i in r...  8.44 us
  transfers between devices with their start and end apart: 12, of which 7 were waited for; matrix products, arithmetic and copies ran while one was open for 3% of the time, Pallas kernels for 6%

profile of v4, /device:TPU:32, one launch (start us, length us, event | category | flops | bytes accessed | tf_op | source)
XLA Modules:
  0.0 239.5 jit_solution(14806509682865234975)
XLA Ops:
  1.4 1.0 shard_map.144
  2.3 13.0 %all-to-all-start = ((bf16[32,64,128]{2,1,0:T(8,128)(2,1)}), bf16[32,64,128]{2,1,0:T(8,128)(2,1)S(1)}, u32[]{:S(2)}, u32[]{:S(2)}) async-start(bf16[32,64,128]{2,1,0:T(8,128)(2,1)} %shard_map.144), calls=%async_computation | async-start | bytes 1048576 | tf_op jit(solution)/shard_map/all_to_all | solution.py:29
  17.0 1.6 copy-done
  18.6 1.2 copy-done.16
  19.9 2.9 %shard_map.145 = (bf16[256,2048]{1,0:T(8,128)(2,1)S(1)}, bf16[256,2048]{1,0:T(8,128)(2,1)S(1)}, f32[256,128]{1,0:T(8,128)S(1)}, f32[8,256]{1,0:T(8,128)S(1)}) custom-call(s32[3]{0:T(128)S(1)} %add_convert_fusion.flags_ref, f32[8,2048]{1,0:T(8,128)S(1)} %maximum_maximum_fusion.aux_ref, bf16[2,1,256,2048]{3,2,1,0:T(8,128)(2,1)S(1)} %copy-done, ...), custom_call_target="tpu_custom_call" | custom-call | flops 30000000 | bytes 4000000 | tf_op jit(solution)/shard_map/pallas_call | solution.py:43
  22.8 1.0 copy-done.6
  23.8 1.0 copy-done.9
  25.6 11.0 %all-to-all-done.chunks_ref = bf16[32,64,128]{2,1,0:T(8,128)(2,1)S(1)} async-done(((bf16[32,64,128]{2,1,0:T(8,128)(2,1)}), bf16[32,64,128]{2,1,0:T(8,128)(2,1)S(1)}, u32[]{:S(2)}, u32[]{:S(2)}) %all-to-all-start) | async-done | bytes 524320 | tf_op jit(solution)/shard_map/all_to_all | solution.py:29
  36.6 0.8 copy-done.12
  37.4 1.2 copy-done.7
  38.6 1.2 copy-done.10
  39.9 1.0 copy-done.13
  40.9 3.3 %shard_map.146 = (bf16[32,16,128]{2,1,0:T(8,128)(2,1)}, bf16[128,2048]{1,0:T(8,128)(2,1)}, f32[128,256]{1,0:T(8,128)S(1)}, f32[128,256]{1,0:T(8,128)S(1)}, f32[8...) custom-call(s32[3]{0:T(128)S(1)} %add_convert_fusion.flags_ref, bf16[32,64,128]{2,1,0:T(8,128)(2,1)S(1)} %copy-done.13, ...), custom_call_target="tpu_custom_call" | custom-call | flops 300000000 | bytes 4000000 | tf_op jit(solution)/shard_map/pallas_call | solution.py:43
  44.2 1.0 copy-done.14
  46.4 4.1 %all-to-all-start.1 = ((bf16[32,16,128]{2,1,0:T(8,128)(2,1)}), bf16[32,16,128]{2,1,0:T(8,128)(2,1)S(1)}, u32[]{:S(2)}, u32[]{:S(2)}) async-start(bf16[32,16,128]{2,1,0:T(8,128)(2,1)} %get-tuple-element.55), calls=%async_computation.1 | async-start | bytes 262144 | tf_op jit(solution)/shard_map/all_to_all | solution.py:29
  50.8 13.1 %all-to-all-done.1.slots_ref = bf16[32,16,128]{2,1,0:T(8,128)(2,1)S(1)} async-done(((bf16[32,16,128]{2,1,0:T(8,128)(2,1)}), bf16[32,16,128]{2,1,0:T(8,128)(2,1)S(1)}, u32[]{:S(2)}, u32[]{:S(2)}) %all-to-all-start.1) | async-done | bytes 131104 | tf_op jit(solution)/shard_map/all_to_all | solution.py:29
  63.8 1.2 copy-done.4
  65.1 1.5 shard_map.147
  68.4 5.3 %all-to-all-start.2 = ((bf16[32,16,128]{2,1,0:T(8,128)(2,1)}), bf16[32,16,128]{2,1,0:T(8,128)(2,1)S(1)}, u32[]{:S(2)}, u32[]{:S(2)}) async-start(bf16[32,16,128]{2,1,0:T(8,128)(2,1)} %get-tuple-element.56), calls=%async_computation.2 | async-start | bytes 262144 | tf_op jit(solution)/shard_map/all_to_all | solution.py:29
  73.7 8.4 %collective-permute-done.1.aux_ref = f32[8,2048]{1,0:T(8,128)S(1)} collective-permute-done((f32[8,2048]{1,0:T(8,128)S(1)}, f32[8,2048]{1,0:T(8,128)S(1)}, u32[]{:S(2)}, u32[]{:S(2)}) %collective-permute-start.1) | collective-permute-done | bytes 65568 | tf_op jit(solution)/shard_map/ppermute | solution.py:34
  82.2 6.1 %all-to-all-done.2.sums_in = bf16[32,16,128]{2,1,0:T(8,128)(2,1)S(1)} async-done(((bf16[32,16,128]{2,1,0:T(8,128)(2,1)}), bf16[32,16,128]{2,1,0:T(8,128)(2,1)S(1)}, u32[]{:S(2)}, u32[]{:S(2)}) %all-to-all-start.2) | async-done | bytes 131104 | tf_op jit(solution)/shard_map/all_to_all | solution.py:29
  88.3 1.2 copy-done.15
  89.5 6.1 %shard_map.148 = (bf16[32,32,128]{2,1,0:T(8,128)(2,1)S(1)}, bf16[256,2048]{1,0:T(8,128)(2,1)S(1)}, bf16[256,2048]{1,0:T(8,128)(2,1)S(1)}, f32[256,128]{1,0:T(8,1...) custom-call(s32[3]{0:T(128)S(1)} %add_convert_fusion.flags_ref, ...), custom_call_target="tpu_custom_call" | custom-call | flops 400000000 | bytes 4000000 | tf_op jit(solution)/shard_map/pallas_call | solution.py:43
  95.6 1.0 copy-done.21
  96.5 1.0 copy-done.23
  97.5 1.0 copy-done.25
  101.7 6.0 %all-to-all-start.3 = ((bf16[32,32,128]{2,1,0:T(8,128)(2,1)}), bf16[32,32,128]{2,1,0:T(8,128)(2,1)S(1)}, u32[]{:S(2)}, u32[]{:S(2)}) async-start(bf16[32,32,128]{2,1,0:T(8,128)(2,1)} %copy-done.28), calls=%async_computation.3 | async-start | bytes 524288 | tf_op jit(solution)/shard_map/all_to_all | solution.py:29
  107.7 14.8 %all-to-all-done.3.pairs_ref = bf16[32,32,128]{2,1,0:T(8,128)(2,1)S(1)} async-done(((bf16[32,32,128]{2,1,0:T(8,128)(2,1)}), bf16[32,32,128]{2,1,0:T(8,128)(2,1)S(1)}, u32[]{:S(2)}, u32[]{:S(2)}) %all-to-all-start.3) | async-done | bytes 262176 | tf_op jit(solution)/shard_map/all_to_all | solution.py:29
  122.6 2.8 %shard_map.149 = (bf16[32,32,128]{2,1,0:T(8,128)(2,1)S(1)}, bf16[32,2048]{1,0:T(8,128)(2,1)S(1)}, bf16[32,2048]{1,0:T(8,128)(2,1)S(1)}, bf16[32,256]{1,0:T(8,128)(2,1)S(1)}, bf16[32,256]{1,0:T(8,128)(2,1)S(1)}) custom-call(bf16[32,32,128]{2,1,0:T(8,128)(2,1)S(1)} %all-to-all-done.3.pairs_ref, bf16[2048,256]{1,0:T(8,128)(2,1)} %collective-permute-done.3.first_ref, ...), custom_call_target="tpu_custom_call" | custom-call | flops 140000000 | bytes 4000000 | tf_op jit(solution)/shard_map/pallas_call | solution.py:43
  125.5 17.6 %all_to_all.40.sums_ref = bf16[32,32,128]{2,1,0:T(8,128)(2,1)S(1)} all-to-all(bf16[32,32,128]{2,1,0:T(8,128)(2,1)S(1)} %get-tuple-element.65), channel_id=1, replica_groups=mesh['section'=8,'zh'=2,'y'=4,'x'=4] {'zh','y','x'}, dimensions={0} | all-to-all | bytes 524288 | tf_op jit(solution)/shard_map/all_to_all | solution.py:29
  143.1 1.2 copy-done.26
  144.3 7.8 %shard_map.150 = (bf16[32,16,128]{2,1,0:T(8,128)(2,1)S(1)}, bf16[496,2048]{1,0:T(8,128)(2,1)}, bf16[256,2048]{1,0:T(8,128)(2,1)S(1)}) custom-call(s32[3]{0:T(128)S(1)} %copy-done.55, bf16[32,32,128]{2,1,0:T(8,128)(2,1)S(1)} %all_to_all.40.sums_ref, bf16[256,2048]{1,0:T(8,128)(2,1)S(1)} %copy-done.22, bf16[256,2048]{1,0:T(8,128)(2,1)S(1)} %copy-done.24, ...), custom_call_target="tpu_custom_call" | custom-call | flops 600000000 | bytes 4000000 | tf_op jit(solution)/shard_map/pallas_call | solution.py:43
  152.3 26.6 %all_to_all.41.mixed_in_ref = bf16[32,16,128]{2,1,0:T(8,128)(2,1)S(1)} all-to-all(bf16[32,16,128]{2,1,0:T(8,128)(2,1)S(1)} %get-tuple-element.77), channel_id=1, replica_groups=mesh['section'=8,'zh'=2,'y'=4,'x'=4] {'zh','y','x'}, dimensions={0} | all-to-all | bytes 262144 | tf_op jit(solution)/shard_map/all_to_all | solution.py:29
  178.9 1.3 shard_map.151
  182.1 10.3 %all-to-all-start.6 = ((bf16[32,16,128]{2,1,0:T(8,128)(2,1)}), bf16[32,16,128]{2,1,0:T(8,128)(2,1)S(1)}, u32[]{:S(2)}, u32[]{:S(2)}) async-start(bf16[32,16,128]{2,1,0:T(8,128)(2,1)} %copy-done.41), calls=%async_computation.6 | async-start | bytes 262144 | tf_op jit(solution)/shard_map/all_to_all | solution.py:29
  192.4 12.4 %all-to-all-done.6.sums_ref = bf16[32,16,128]{2,1,0:T(8,128)(2,1)S(1)} async-done(((bf16[32,16,128]{2,1,0:T(8,128)(2,1)}), bf16[32,16,128]{2,1,0:T(8,128)(2,1)S(1)}, u32[]{:S(2)}, u32[]{:S(2)}) %all-to-all-start.6) | async-done | bytes 131104 | tf_op jit(solution)/shard_map/all_to_all | solution.py:29
  204.9 1.2 copy-done.8
  206.1 1.2 copy-done.11
  207.3 1.2 copy-done.18
  208.6 6.8 %shard_map.152 = (bf16[256,2048]{1,0:T(8,128)(2,1)S(1)}, f32[16,128]{1,0:T(8,128)S(1)}, bf16[32,80,128]{2,1,0:T(8,128)(2,1)S(1)}) custom-call(bf16[32,16,128]{2,1,0:T(8,128)(2,1)S(1)} %all-to-all-done.6.sums_ref, f32[16,128]{1,0:T(8,128)S(1)} %get-tuple-element.80.out_ref, bf16[256,2048]{1,0:T(8,128)(2,1)S(1)} %copy-done.8, ...), custom_call_target="tpu_custom_call" | custom-call | flops 600000000 | bytes 4000000 | tf_op jit(solution)/shard_map/pallas_call | solution.py:43
  215.4 1.0 copy-done.19
  216.3 0.9 copy-done.27
  217.2 4.0 %all-to-all-start.7 = ((bf16[32,80,128]{2,1,0:T(8,128)(2,1)}), bf16[32,80,128]{2,1,0:T(8,128)(2,1)S(1)}, u32[]{:S(2)}, u32[]{:S(2)}) async-start(bf16[32,80,128]{2,1,0:T(8,128)(2,1)} %copy-done.27), calls=%async_computation.7 | async-start | bytes 1310720 | tf_op jit(solution)/shard_map/all_to_all | solution.py:29
  221.4 1.4 fusion.1
  222.8 1.4 fusion
  225.6 1.5 maximum_bitcast_fusion
  227.1 11.6 %all-to-all-done.7.chunks_ref = bf16[32,80,128]{2,1,0:T(8,128)(2,1)S(1)} async-done(((bf16[32,80,128]{2,1,0:T(8,128)(2,1)}), bf16[32,80,128]{2,1,0:T(8,128)(2,1)S(1)}, u32[]{:S(2)}, u32[]{:S(2)}) %all-to-all-start.7) | async-done | bytes 655392 | tf_op jit(solution)/shard_map/all_to_all | solution.py:29
  238.7 0.8 shard_map.153
  (122 shorter events, 12.7 us)
Async XLA Ops:
  2.3 34.3 %all-to-all-start = ((bf16[32,64,128]{2,1,0:T(8,128)(2,1)}), bf16[32,64,128]{2,1,0:T(8,128)(2,1)S(1)}, u32[]{:S(2)}, u32[]{:S(2)}) async-start(bf16[32,64,128]{2,1,0:T(8,128)(2,1)} %shard_map.144), calls=%async_computation | async-start | bytes 1048576 | tf_op jit(solution)/shard_map/all_to_all | solution.py:29
  16.3 72.0 %copy-start.54 = (s32[3]{0:T(128)}, s32[3]{0:T(128)S(1)}, u32[]{:S(2)}) copy-start(s32[3]{0:T(128)S(1)} %add_convert_fusion.flags_ref) | copy-start | bytes 40
  17.0 1.6 copy-start
  18.6 1.2 copy-start.16
  19.8 17.6 %copy-start.1 = (bf16[2,1,256,2048]{3,2,1,0:T(8,128)(2,1)S(1)}, bf16[2,1,256,2048]{3,2,1,0:T(8,128)(2,1)}, u32[]{:S(2)}) copy-start(bf16[2,1,256,2048]{3,2,1,0:T(8,128)(2,1)} %tokens_ref.3) | copy-start | bytes 6291460
  22.8 1.0 copy-start.6
  25.4 56.8 %collective-permute-start.2 = (bf16[256,2048]{1,0:T(8,128)(2,1)}, bf16[256,2048]{1,0:T(8,128)(2,1)}, u32[]{:S(2)}, u32[]{:S(2)}) collective-permute-start(bf16[256,2048]{1,0:T(8,128)(2,1)} %bitcast.45), channel_id=1, source_target_pairs={{0,224},{32,0},{64,32},{96,64},{128,96},{160,128},{192,160},{224,1... | collective-permute-start | bytes 3145736 | tf_op jit(solution)/shard_map/ppermute | solution.py:34
  37.4 1.2 copy-start.7
  38.6 1.2 copy-start.10
  39.9 1.0 copy-start.13
  40.9 9.7 %copy-start.3 = (bf16[1,2048,256]{2,1,0:T(8,128)(2,1)S(1)}, bf16[1,2048,256]{2,1,0:T(8,128)(2,1)}, u32[]{:S(2)}) copy-start(bf16[1,2048,256]{2,1,0:T(8,128)(2,1)} %param.16) | copy-start | bytes 3145732
  46.4 41.8 %copy-start.2 = (bf16[2,1,256,2048]{3,2,1,0:T(8,128)(2,1)S(1)}, bf16[2,1,256,2048]{3,2,1,0:T(8,128)(2,1)}, u32[]{:S(2)}) copy-start(bf16[2,1,256,2048]{3,2,1,0:T(8,128)(2,1)} %cotangent_ref.3) | copy-start | bytes 6291460
  46.4 41.8 %collective-permute-start = (bf16[128,2048]{1,0:T(8,128)(2,1)}, bf16[128,2048]{1,0:T(8,128)(2,1)}, u32[]{:S(2)}, u32[]{:S(2)}) collective-permute-start(bf16[128,2048]{1,0:T(8,128)(2,1)} %get-tuple-element.59.columns_ref), channel_id=1, source_target_pairs={{0,224},{32,0},{64,32},{96,64},{128,96},{160,128},{192,160},{224,1... | collective-permute-start | bytes 1572872 | tf_op jit(solution)/shard_map/ppermute | solution.py:34
  46.4 17.4 %all-to-all-start.1 = ((bf16[32,16,128]{2,1,0:T(8,128)(2,1)}), bf16[32,16,128]{2,1,0:T(8,128)(2,1)S(1)}, u32[]{:S(2)}, u32[]{:S(2)}) async-start(bf16[32,16,128]{2,1,0:T(8,128)(2,1)} %get-tuple-element.55), calls=%async_computation.1 | async-start | bytes 262144 | tf_op jit(solution)/shard_map/all_to_all | solution.py:29
  50.6 57.1 %collective-permute-start.3 = (bf16[2048,256]{1,0:T(8,128)(2,1)S(1)}, bf16[2048,256]{1,0:T(8,128)(2,1)}, u32[]{:S(2)}, u32[]{:S(2)}) collective-permute-start(bf16[2048,256]{1,0:T(8,128)(2,1)S(1)} %bitcast.34), channel_id=1, source_target_pairs={{0,224},{32,0},{64,32},{96,64},{128,96},{160,128},{192,160},{224,1... | collective-permute-start | bytes 3145736 | tf_op jit(solution)/shard_map/ppermute | solution.py:34
  50.7 57.1 %collective-permute-start.4 = (bf16[256,2048]{1,0:T(8,128)(2,1)}, bf16[256,2048]{1,0:T(8,128)(2,1)}, u32[]{:S(2)}, u32[]{:S(2)}) collective-permute-start(bf16[256,2048]{1,0:T(8,128)(2,1)} %bitcast.37), channel_id=1, source_target_pairs={{0,224},{32,0},{64,32},{96,64},{128,96},{160,128},{192,160},{224,1... | collective-permute-start | bytes 3145736 | tf_op jit(solution)/shard_map/ppermute | solution.py:34
  63.8 1.2 copy-start.4
  68.4 19.9 %all-to-all-start.2 = ((bf16[32,16,128]{2,1,0:T(8,128)(2,1)}), bf16[32,16,128]{2,1,0:T(8,128)(2,1)S(1)}, u32[]{:S(2)}, u32[]{:S(2)}) async-start(bf16[32,16,128]{2,1,0:T(8,128)(2,1)} %get-tuple-element.56), calls=%async_computation.2 | async-start | bytes 262144 | tf_op jit(solution)/shard_map/all_to_all | solution.py:29
  73.6 8.5 %collective-permute-start.1 = (f32[8,2048]{1,0:T(8,128)S(1)}, f32[8,2048]{1,0:T(8,128)S(1)}, u32[]{:S(2)}, u32[]{:S(2)}) collective-permute-start(f32[8,2048]{1,0:T(8,128)S(1)} %maximum_maximum_fusion.aux_ref), channel_id=1, source_target_pairs={{0,224},{32,0},{64,32},{96,64},{128,96},{160,128},{192,160},{224,1... | collective-permute-start | bytes 196616 | tf_op jit(solution)/shard_map/ppermute | solution.py:34
  88.3 1.2 copy-start.15
  96.5 1.0 copy-start.23
  101.7 20.9 %all-to-all-start.3 = ((bf16[32,32,128]{2,1,0:T(8,128)(2,1)}), bf16[32,32,128]{2,1,0:T(8,128)(2,1)S(1)}, u32[]{:S(2)}, u32[]{:S(2)}) async-start(bf16[32,32,128]{2,1,0:T(8,128)(2,1)} %copy-done.28), calls=%async_computation.3 | async-start | bytes 524288 | tf_op jit(solution)/shard_map/all_to_all | solution.py:29
  122.6 20.5 %copy-start.22 = (bf16[256,2048]{1,0:T(8,128)(2,1)S(1)}, bf16[256,2048]{1,0:T(8,128)(2,1)}, u32[]{:S(2)}) copy-start(bf16[256,2048]{1,0:T(8,128)(2,1)} %copy-done.21) | copy-start | bytes 3145732
  122.6 20.5 %copy-start.24 = (bf16[256,2048]{1,0:T(8,128)(2,1)S(1)}, bf16[256,2048]{1,0:T(8,128)(2,1)}, u32[]{:S(2)}) copy-start(bf16[256,2048]{1,0:T(8,128)(2,1)} %copy-done.23) | copy-start | bytes 3145732
  122.6 20.5 %copy-start.36 = (f32[256,128]{1,0:T(8,128)S(1)}, f32[256,128]{1,0:T(8,128)}, u32[]{:S(2)}) copy-start(f32[256,128]{1,0:T(8,128)} %copy-done.35) | copy-start | bytes 393220
  122.6 20.5 %copy-start.38 = (f32[128,256]{1,0:T(8,128)S(1)}, f32[128,256]{1,0:T(8,128)}, u32[]{:S(2)}) copy-start(f32[128,256]{1,0:T(8,128)} %copy-done.37) | copy-start | bytes 393220
  122.6 20.5 %copy-start.40 = (f32[128,256]{1,0:T(8,128)S(1)}, f32[128,256]{1,0:T(8,128)}, u32[]{:S(2)}) copy-start(f32[128,256]{1,0:T(8,128)} %copy-done.39) | copy-start | bytes 393220
  122.6 20.5 %copy-start.55 = (s32[3]{0:T(128)S(1)}, s32[3]{0:T(128)}, u32[]{:S(2)}) copy-start(s32[3]{0:T(128)} %copy-done.54) | copy-start | bytes 40
  122.6 20.5 %copy-start.57 = (f32[8,256]{1,0:T(8,128)S(1)}, f32[8,256]{1,0:T(8,128)}, u32[]{:S(2)}) copy-start(f32[8,256]{1,0:T(8,128)} %copy-done.56) | copy-start | bytes 24580
  143.1 1.2 copy-start.26
  144.3 34.5 %copy-start.5 = (bf16[1,256,2048]{2,1,0:T(8,128)(2,1)S(1)}, bf16[1,256,2048]{2,1,0:T(8,128)(2,1)}, u32[]{:S(2)}) copy-start(bf16[1,256,2048]{2,1,0:T(8,128)(2,1)} %param.17) | copy-start | bytes 3145732
  144.3 34.5 %copy-start.49 = (f32[32,256]{1,0:T(8,128)S(1)}, f32[32,256]{1,0:T(8,128)}, u32[]{:S(2)}) copy-start(f32[32,256]{1,0:T(8,128)} %copy-done.48) | copy-start | bytes 98308
  152.2 28.0 %copy-start.17 = (bf16[256,2048]{1,0:T(8,128)(2,1)}, bf16[256,2048]{1,0:T(8,128)(2,1)S(1)}, u32[]{:S(2)}) copy-start(bf16[256,2048]{1,0:T(8,128)(2,1)S(1)} %get-tuple-element.84.up_ref) | copy-start | bytes 3145732
  152.2 52.7 %copy-start.30 = (f32[256,128]{1,0:T(8,128)S(1)}, f32[256,128]{1,0:T(8,128)}, u32[]{:S(2)}) copy-start(f32[256,128]{1,0:T(8,128)} %copy-done.29) | copy-start | bytes 393220
  152.2 52.7 %copy-start.32 = (f32[128,256]{1,0:T(8,128)S(1)}, f32[128,256]{1,0:T(8,128)}, u32[]{:S(2)}) copy-start(f32[128,256]{1,0:T(8,128)} %copy-done.31) | copy-start | bytes 393220
  152.2 52.7 %copy-start.34 = (f32[128,256]{1,0:T(8,128)S(1)}, f32[128,256]{1,0:T(8,128)}, u32[]{:S(2)}) copy-start(f32[128,256]{1,0:T(8,128)} %copy-done.33) | copy-start | bytes 393220
  152.2 52.6 %collective-permute-start.5 = (bf16[496,2048]{1,0:T(8,128)(2,1)}, bf16[496,2048]{1,0:T(8,128)(2,1)S(1)}, u32[]{:S(2)}, u32[]{:S(2)}) collective-permute-start(bf16[496,2048]{1,0:T(8,128)(2,1)} %get-tuple-element.85), channel_id=1, source_target_pairs={{0,32},{32,64},{64,96},{96,128},{128,160},{160,192},{192,224},{224... | collective-permute-start | bytes 6094856 | tf_op jit(solution)/shard_map/ppermute | solution.py:34
  182.1 22.8 %all-to-all-start.6 = ((bf16[32,16,128]{2,1,0:T(8,128)(2,1)}), bf16[32,16,128]{2,1,0:T(8,128)(2,1)S(1)}, u32[]{:S(2)}, u32[]{:S(2)}) async-start(bf16[32,16,128]{2,1,0:T(8,128)(2,1)} %copy-done.41), calls=%async_computation.6 | async-start | bytes 262144 | tf_op jit(solution)/shard_map/all_to_all | solution.py:29
  204.9 1.2 copy-start.8
  206.1 1.2 copy-start.11
  207.3 1.2 copy-start.18
  208.5 12.8 %copy-start.45 = (bf16[32,2048]{1,0:T(8,128)(2,1)S(1)}, bf16[32,2048]{1,0:T(8,128)(2,1)}, u32[]{:S(2)}) copy-start(bf16[32,2048]{1,0:T(8,128)(2,1)} %copy-done.44) | copy-start | bytes 393220
  208.6 12.8 %copy-start.51 = (bf16[32,256]{1,0:T(8,128)(2,1)S(1)}, bf16[32,256]{1,0:T(8,128)(2,1)}, u32[]{:S(2)}) copy-start(bf16[32,256]{1,0:T(8,128)(2,1)} %copy-done.50) | copy-start | bytes 49156
  217.2 5.6 %copy-start.43 = (bf16[32,2048]{1,0:T(8,128)(2,1)S(1)}, bf16[32,2048]{1,0:T(8,128)(2,1)}, u32[]{:S(2)}) copy-start(bf16[32,2048]{1,0:T(8,128)(2,1)} %copy-done.42) | copy-start | bytes 393220
  217.2 5.6 %copy-start.53 = (bf16[32,256]{1,0:T(8,128)(2,1)S(1)}, bf16[32,256]{1,0:T(8,128)(2,1)}, u32[]{:S(2)}) copy-start(bf16[32,256]{1,0:T(8,128)(2,1)} %copy-done.52) | copy-start | bytes 49156
  217.2 21.4 %all-to-all-start.7 = ((bf16[32,80,128]{2,1,0:T(8,128)(2,1)}), bf16[32,80,128]{2,1,0:T(8,128)(2,1)S(1)}, u32[]{:S(2)}, u32[]{:S(2)}) async-start(bf16[32,80,128]{2,1,0:T(8,128)(2,1)} %copy-done.27), calls=%async_computation.7 | async-start | bytes 1310720 | tf_op jit(solution)/shard_map/all_to_all | solution.py:29
  221.4 4.2 %copy-start.20 = (bf16[256,2048]{1,0:T(8,128)(2,1)S(1)}, bf16[256,2048]{1,0:T(8,128)(2,1)}, u32[]{:S(2)}) copy-start(bf16[256,2048]{1,0:T(8,128)(2,1)} %copy-done.19) | copy-start | bytes 3145732
  225.6 13.1 %copy-start.47 = (bf16[1,2048,4]{1,2,0:T(4,128)(2,1)S(1)}, bf16[1,2048,4]{1,2,0:T(4,128)(2,1)}, u32[]{:S(2)}) copy-start(bf16[1,2048,4]{1,2,0:T(4,128)(2,1)} %param.15) | copy-start | bytes 49156
  (22 other events, 16.2 us)

commit v5 on v3

--- a/solution.py
+++ b/solution.py
@@ -14,6 +14,7 @@
 LANES = 128
 STEP = 16
 VMEM_BYTES = 24 * 1024 * 1024
+VMEM_MOST = 58 * 1024 * 1024
 
 
 def dot_dims(left_side, right_side, left_dim, right_dim):
@@ -35,7 +36,12 @@
     return lax.ppermute(block, "section", route)
 
 
-def run(body, outs, scratch, flops, near, *operands):
+def section_ring(block, distance):
+    sections = lax.axis_size("section")
+    return lax.ppermute(block, "section", [(i, (i + distance) % sections) for i in range(sections)])
+
+
+def run(body, outs, scratch, flops, near, *operands, vmem=VMEM_BYTES):
     def place(index, item):
         if item.ndim == 1:
             return pltpu.SMEM
@@ -43,15 +49,17 @@
 
     return pl.pallas_call(
         body,
-        out_shape=[jax.ShapeDtypeStruct(shape, kind) for shape, kind in outs],
+        out_shape=[jax.ShapeDtypeStruct(item[0], item[1]) for item in outs],
         in_specs=[
             pl.BlockSpec(memory_space=place(index, item)) for index, item in enumerate(operands)
         ],
-        out_specs=[pl.BlockSpec(memory_space=pltpu.VMEM) for _ in outs],
+        out_specs=[
+            pl.BlockSpec(memory_space=pltpu.VMEM if len(item) == 2 else pl.ANY) for item in outs
+        ],
         scratch_shapes=[
             pltpu.VMEM(*item) if isinstance(item, tuple) else item for item in scratch
         ],
-        compiler_params=pltpu.CompilerParams(vmem_limit_bytes=VMEM_BYTES),
+        compiler_params=pltpu.CompilerParams(vmem_limit_bytes=vmem),
         cost_estimate=pl.CostEstimate(flops=flops, bytes_accessed=4000000, transcendentals=0),
     )(*operands)
 
@@ -104,7 +112,7 @@
 
 
 def passes(ref, body):
-    @pl.loop(0, ref.shape[0] // STEP)
+    @pl.loop(0, ref.shape[0] // STEP, unroll=8)
     def _(index):
         body(pl.ds(index * STEP, STEP))
 
@@ -174,51 +182,53 @@
     return mixed[:1] + mixed[1:2]
 
 
+def norm_kernel(
+    flags_ref, gain_ref, tokens_ref, inflow_ref,
+    start_ref, hidden_out, inverse_ref, length_ref,
+    in_ref, hidden_ref, sums_ref, in_sem, out_sem, hidden_sem,
+):
+    begin_copy(flags_ref[0], tokens_ref.at[0, 0], inflow_ref.at[0, 0], in_ref, in_sem)
+    end_copy(inflow_ref.at[0, 0], in_ref, in_sem)
+    pltpu.make_async_copy(in_ref, start_ref, out_sem).start()
+
+    def square_rows(window):
+        wide = in_ref[window, :].astype(F32)
+        sums_ref[window, :] = lane_sums(wide * wide)
+
+    passes(in_ref, square_rows)
+    length = norm_passes(in_ref, gain_ref[...], hidden_ref, inverse_ref, sums_ref)
+    length_ref[...] = jnp.broadcast_to(length, length_ref.shape)
+    pltpu.make_async_copy(hidden_ref, hidden_out, hidden_sem).start()
+    end_copy(in_ref, start_ref, out_sem)
+    end_copy(hidden_ref, hidden_out, hidden_sem)
+
+
 def early_kernel(
-    scale_ref, flags_ref, chunks_ref, gain_ref, tokens_ref, inflow_ref, cotangent_ref,
-    send_ref, in_ref, columns_ref, hidden_ref, inverse_ref, logits_ref, prob_ref, rows_ref,
-    mixed_ref, up_ref, wide_ref, sums_ref, in_sem, up_sem,
-):
-    begin_copy(flags_ref[0], tokens_ref.at[0, 0], inflow_ref.at[0, 0], in_ref, in_sem)
-    last = flags_ref[1] != 0
-
-    @pl.when(last)
-    def _():
-        pltpu.make_async_copy(cotangent_ref.at[0, 0], up_ref, up_sem).start()
-
+    scale_ref, chunks_ref, length_ref, hidden_in,
+    send_ref, columns_ref, logits_ref, prob_ref, rows_ref,
+    hidden_ref, wide_ref, hidden_sem,
+):
+    pltpu.make_async_copy(hidden_in, hidden_ref, hidden_sem).start()
     peers = chunks_ref.shape[0]
-    chunk = gain_ref.shape[1] // LANES
+    chunk = hidden_ref.shape[1] // LANES
     wide_ref[...] = chunks_ref[...].astype(F32)
     for k in range(chunks_ref.shape[1] // chunk):
         columns_ref[k * peers : (k + 1) * peers] = wide_rows(wide_ref, k * chunk, chunk).astype(BF)
-    end_copy(inflow_ref.at[0, 0], in_ref, in_sem)
-
-    def square_rows(window):
-        wide = in_ref[window, :].astype(F32)
-        sums_ref[window, :] = lane_sums(wide * wide)
-
-    passes(in_ref, square_rows)
-    length = norm_passes(in_ref, gain_ref[...], hidden_ref, inverse_ref, sums_ref)
-    combine, slot = slot_front(
-        scale_ref[0], columns_ref, hidden_ref, length, logits_ref, prob_ref, rows_ref
+    end_copy(hidden_in, hidden_ref, hidden_sem)
+    _, slot = slot_front(
+        scale_ref[0], columns_ref, hidden_ref, length_ref[:1], logits_ref, prob_ref, rows_ref
     )
     send_ref[...] = jnp.broadcast_to(to_chunk(slot).astype(BF)[None], send_ref.shape)
-    mixed_ref[...] = jnp.zeros_like(mixed_ref)
-
-    @pl.when(last)
-    def _():
-        end_copy(cotangent_ref.at[0, 0], up_ref, up_sem)
-        mixed_ref[...] = to_chunk(mix_rows(combine, up_ref[...])).astype(BF)
+
+
+def join_rows(parts, out_ref):
+    count = sum(part.shape[0] for part in parts)
+    filler = jnp.zeros((out_ref.shape[0] - count, LANES), F32)
+    out_ref[...] = jnp.concatenate([*parts, filler], axis=0)
 
 
 def pack_kernel(sums_ref, rows_ref, out_ref):
-    total = summed(sums_ref)
-    combine = to_chunk(rows_ref[1:2])
-    count = total.shape[0]
-    out_ref[:count] = total
-    out_ref[count:] = jnp.concatenate(
-        [combine, jnp.zeros((out_ref.shape[0] - count - combine.shape[0], LANES), F32)], axis=0
-    )
+    join_rows([summed(sums_ref), to_chunk(rows_ref[1:2])], out_ref)
 
 
 def late_kernel(
@@ -229,7 +239,8 @@
     begin_copy(flags_ref[1], cotangent_ref.at[1, 0], backflow_ref.at[0, 0], up_ref, up_sem)
     chunk = gain_ref.shape[1] // LANES
     out_row = to_row(moved_ref[:chunk])
-    comb_ref[...] = to_column(to_row(moved_ref[chunk : chunk + 2]))
+    before = to_row(moved_ref[chunk : chunk + 2])
+    comb_ref[...] = to_column(jnp.where(flags_ref[0] != 0, jnp.zeros_like(before), before))
 
     def add_rows(window):
         base = base_ref[window, :].astype(F32)
@@ -303,22 +314,31 @@
     send_ref[...] = wide_ref[...].astype(BF)
 
 
-def spread_kernel(moved_ref, own_ref, send_ref):
-    block = (moved_ref[...].astype(F32) + own_ref[...].astype(F32)).astype(BF)
-    send_ref[...] = jnp.broadcast_to(block[None], send_ref.shape)
+def spread_kernel(flags_ref, moved_ref, own_ref, send_ref, kept_ref):
+    block = jnp.where(flags_ref[1] != 0, own_ref[...], moved_ref[...])
+    kept_ref[...] = block
+    send_ref[...] = jnp.broadcast_to(block[: send_ref.shape[1]].astype(BF)[None], send_ref.shape)
+
+
+def row_dots(pairs):
+    def body(window):
+        for ref, row, sums_ref in pairs:
+            sums_ref[window, :] = lane_sums(ref[window, :].astype(F32) * row)
+
+    passes(pairs[0][0], body)
+    return [jnp.sum(jnp.transpose(sums_ref[...]), axis=0, keepdims=True) for _, _, sums_ref in pairs]
 
 
 def back_body(
-    scale, out_row, grad_row, in_ref, hidden_ref, inverse_ref, logits_ref, prob_ref, rows_ref,
-    up_ref, columns_ref, gain_ref, grads_ref, hold_ref, pull_ref, mean_ref,
+    scale, dcombine, dspread, grad_row, in_ref, hidden_ref, inverse_ref, logits_ref, prob_ref, rows_ref,
+    columns_ref, gain_ref, hold_ref, pull_ref, mean_ref, put_grads,
 ):
     gain = gain_ref[...]
     length = rows_ref[0:1]
     combine = rows_ref[1:2]
     spread = rows_ref[2:3]
     grad_rows = first_rows([grad_row])
-    dcombine = dot_dims(first_rows([out_row]), up_ref[...], 1, 1)[:1]
-    dspread = dot_dims(grad_rows, hidden_ref[...], 1, 1)[:1].astype(BF).astype(F32)
+    dspread = dspread.astype(BF).astype(F32)
     first_term = spread * (dspread - jnp.sum(dspread * spread, axis=1, keepdims=True))
     mixed = combine * dcombine
     prob = prob_ref[...]
@@ -342,7 +362,7 @@
         return total + product[:8] + product[8:]
 
     gain_sum = lax.fori_loop(
-        0, in_ref.shape[0] // STEP, product_rows, jnp.zeros((8, in_ref.shape[1]), F32)
+        0, in_ref.shape[0] // STEP, product_rows, jnp.zeros((8, in_ref.shape[1]), F32), unroll=4
     )
     mean = jnp.sum(mean_ref[...], axis=1, keepdims=True) * (1.0 / in_ref.shape[1])
     mean_ref[...] = jnp.broadcast_to(mean * inverse_ref[...], mean_ref.shape)
@@ -352,56 +372,85 @@
         through = hold_ref[window, :] * gain
         wide = in_ref[window, :].astype(F32)
         dinput = inverse * (through - wide * mean_ref[window, :1])
-        grads_ref[window, :] = (up_ref[window, :].astype(F32) + dinput).astype(BF)
+        put_grads(window, dinput)
 
     passes(in_ref, grad_rows_pass)
     return router, gain_sum
 
 
 def back_late_kernel(
-    scale_ref, sums_ref, in_ref, hidden_ref, inverse_ref, logits_ref, prob_ref, rows_ref,
-    up_ref, columns_ref, gain_ref, moved_ref,
-    grads_ref, mixed_ref, outs_ref, router_ref, gain_out, hold_ref, pull_ref, mean_ref,
-):
+    scale_ref, flags_ref, sums_ref, in_ref, hidden_ref, inverse_ref, logits_ref, prob_ref,
+    rows_ref, up_ref, columns_ref, gain_ref, moved_ref, rows_own_ref, packed_ref, cotangent_ref,
+    grads_ref, moved_out, own_out, outs_ref, router_ref, gain_out,
+    own_ref, hold_ref, pull_ref, mean_ref, own_sem,
+):
+    last = flags_ref[1] != 0
+
+    @pl.when(last)
+    def _():
+        pltpu.make_async_copy(cotangent_ref.at[0, 0], own_ref, own_sem).start()
+
     chunk = sums_ref.shape[1] // 2
     total = summed(sums_ref)
     outs_ref[...] = total
+
+    def put_grads(window, dinput):
+        grads_ref[window, :] = (up_ref[window, :].astype(F32) + dinput).astype(BF)
+
+    grad_row = to_row(total[chunk:])
+    dcombine, dspread = row_dots(
+        [(up_ref, to_row(total[:chunk]), pull_ref), (hidden_ref, grad_row, mean_ref)]
+    )
     router, gain_sum = back_body(
-        scale_ref[0], to_row(total[:chunk]), to_row(total[chunk:]), in_ref, hidden_ref,
-        inverse_ref, logits_ref, prob_ref, rows_ref, up_ref, columns_ref, gain_ref, grads_ref,
-        hold_ref, pull_ref, mean_ref,
-    )
+        scale_ref[0], dcombine, dspread, grad_row, in_ref, hidden_ref, inverse_ref, logits_ref,
+        prob_ref, rows_ref, columns_ref, gain_ref, hold_ref, pull_ref, mean_ref, put_grads,
+    )
+
+    def message(combine, out_row, ref, out):
+        mixed = to_chunk(mix_rows(combine, ref[...]).astype(BF).astype(F32))
+        join_rows([mixed, to_chunk(row_dots([(ref, out_row, mean_ref)])[0])], out)
+
+    combine = to_row(moved_ref[chunk : chunk + 2])
+    message(combine, to_row(moved_ref[:chunk]), grads_ref, moved_out)
     router_ref[...] = router
     gain_out[...] = gain_sum
-    combine = to_row(moved_ref[chunk : chunk + 2])
-    mixed_ref[...] = to_chunk(mix_rows(combine, grads_ref[...])).astype(BF)
+    own_out[...] = jnp.zeros_like(own_out)
+
+    @pl.when(last)
+    def _():
+        end_copy(cotangent_ref.at[0, 0], own_ref, own_sem)
+        message(rows_own_ref[1:2], to_row(packed_ref[:chunk]), own_ref, own_out)
 
 
 def back_early_kernel(
-    scale_ref, flags_ref, sums_ref, packed_ref, in_ref, hidden_ref, inverse_ref, logits_ref,
-    prob_ref, rows_ref, columns_ref, gain_ref, router_in_ref, gain_in_ref, cotangent_ref, sent_ref,
-    grads_ref, outs_ref, send_ref, up_ref, hold_ref, pull_ref, mean_ref, wide_ref, up_sem,
-):
-    begin_copy(flags_ref[1], cotangent_ref.at[0, 0], sent_ref, up_ref, up_sem)
+    scale_ref, sums_ref, kept_ref, in_ref, hidden_ref, inverse_ref, logits_ref, prob_ref,
+    rows_ref, columns_ref, gain_ref, router_in_ref, gain_in_ref,
+    dinput_ref, outs_ref, send_ref, hold_ref, pull_ref, mean_ref, wide_ref,
+):
     chunk = sums_ref.shape[1]
     total = summed(sums_ref)
     outs_ref[...] = total
-    end_copy(sent_ref, up_ref, up_sem)
+
+    def put_grads(window, dinput):
+        dinput_ref[window, :] = dinput.astype(BF)
+
+    grad_row = to_row(total)
+    (dspread,) = row_dots([(hidden_ref, grad_row, mean_ref)])
     router, gain_sum = back_body(
-        scale_ref[0], to_row(packed_ref[:chunk]), to_row(total), in_ref, hidden_ref,
-        inverse_ref, logits_ref, prob_ref, rows_ref, up_ref, columns_ref, gain_ref, grads_ref,
-        hold_ref, pull_ref, mean_ref,
+        scale_ref[0], to_row(kept_ref[chunk : chunk + 2]), dspread, grad_row, in_ref, hidden_ref,
+        inverse_ref, logits_ref, prob_ref, rows_ref, columns_ref, gain_ref, hold_ref, pull_ref,
+        mean_ref, put_grads,
     )
     router = router + router_in_ref[...]
     peers = send_ref.shape[0]
     count = router.shape[0] // peers
     for k in range(count):
         put_rows(wide_ref, k * chunk, router[k * peers : (k + 1) * peers])
+    send_ref[:, : count * chunk, :] = wide_ref[...].astype(BF)
     gain_row = jnp.sum(gain_sum + gain_in_ref[...], axis=0, keepdims=True)
-    wide_ref[:, count * chunk :, :] = jnp.broadcast_to(
-        to_chunk(gain_row)[None], (peers, chunk, LANES)
-    )
-    send_ref[...] = wide_ref[...].astype(BF)
+    send_ref[:, count * chunk :, :] = jnp.broadcast_to(
+        to_chunk(gain_row).astype(BF)[None], (peers, chunk, LANES)
+    )
 
 
 def final_kernel(chunks_ref, weights_ref, router_ref, gain_ref):
@@ -454,27 +503,30 @@
     columns_block = run(
         columns_kernel, [((group, local * chunk, LANES), BF)], [], 1000000, 1, weights
     )[0]
-    (
-        send, start_in, columns, hidden_early, inverse_early, logits_early, prob_early,
-        rows_early, mixed_last,
-    ) = run(
-        early_kernel,
-        [
-            single, token_block, ((slots, width), BF), token_block, column, table, table, rows,
-            ((chunk, LANES), BF),
-        ],
-        [token_block, ((group, local * chunk, LANES), F32), column, copy_sem, copy_sem],
-        300000000,
-        4,
-        slot_scale,
+    start_in, hidden_early, inverse_early, length_early = run(
+        norm_kernel,
+        [token_block + ("far",), token_block + ("far",), column, rows],
+        [token_block, token_block, column, copy_sem, copy_sem, copy_sem],
+        30000000,
+        2,
         flags,
-        exchange(columns_block, DP),
         norm_gain,
         tokens,
         inflow,
-        cotangent,
+        vmem=VMEM_MOST,
     )
     sent_in = section_shift(start_in, 1)
+    send, columns, logits_early, prob_early, rows_early = run(
+        early_kernel,
+        [single, ((slots, width), BF), table, table, rows],
+        [token_block, ((group, local * chunk, LANES), F32), copy_sem],
+        300000000,
+        3,
+        slot_scale,
+        exchange(columns_block, DP),
+        length_early,
+        hidden_early,
+    )
     part, slot_early, act_early, slope_early = run(
         expert_early_kernel,
         [single, every_slot, every_hidden, ((group, hidden_units), F32)],
@@ -488,7 +540,7 @@
     packed = run(
         pack_kernel, [((chunk + 8, LANES), F32)], [], 1000000, 2, exchange(part, DP), rows_early
     )[0]
-    moved = section_shift(packed, 1)
+    moved = section_ring(packed, 1)
 
     base = jnp.where(is_first, tokens[1, 0], sent_in)
     (
@@ -519,16 +571,18 @@
         second_weight,
     )
     back_scratch = [((patches, width), F32), column, column]
-    grads_late, mixed_before, outs_late, router_late, gain_late = run(
+    message = ((chunk + 8, LANES), F32)
+    grads_late, moved_back, own_back, outs_late, router_late, gain_late = run(
         back_late_kernel,
         [
-            token_block, ((chunk, LANES), BF), ((2 * chunk, LANES), F32), ((slots, width), F32),
+            token_block, message, message, ((2 * chunk, LANES), F32), ((slots, width), F32),
             ((8, width), F32),
         ],
-        back_scratch,
+        [token_block] + back_scratch + [copy_sem],
         600000000,
-        12,
+        15,
         slot_scale,
+        flags,
         exchange(parts, DP),
         late_in,
         hidden_late,
@@ -540,12 +594,13 @@
         columns,
         norm_gain,
         moved,
-    )
-    moved_back, held_grads = lax.optimization_barrier(
-        (section_shift(mixed_before, -1), grads_late)
-    )
-    sent_grads = section_shift(held_grads, -1)
-    send = run(spread_kernel, [single], [], 1000000, 2, moved_back, mixed_last)[0]
+        rows_early,
+        packed,
+        cotangent,
+    )
+    send, kept = run(
+        spread_kernel, [single, message], [], 1000000, 3, flags, section_ring(moved_back, -1), own_back
+    )
     part, mixed_early_all, pre_grad_early = run(
         expert_back_kernel,
         [single, every_slot, every_hidden],
@@ -558,16 +613,17 @@
         second_weight,
     )
     last_rows = (local + 1) * chunk
-    grads_early, outs_early, finals = run(
+    slot_sums, held_grads = lax.optimization_barrier((exchange(part, DP), grads_late))
+    sent_grads = section_shift(held_grads, -1)
+    dinput, outs_early, finals = run(
         back_early_kernel,
         [token_block, ((chunk, LANES), F32), ((group, last_rows, LANES), BF)],
-        [token_block] + back_scratch + [((group, last_rows, LANES), F32), copy_sem],
+        back_scratch + [((group, local * chunk, LANES), F32)],
         600000000,
-        14,
+        13,
         slot_scale,
-        flags,
-        exchange(part, DP),
-        packed,
+        slot_sums,
+        kept,
         start_in,
         hidden_early,
         inverse_early,
@@ -578,8 +634,6 @@
         norm_gain,
         router_late,
         gain_late,
-        cotangent,
-        sent_grads,
     )
     router_grad, gain_total = run(
         final_kernel,
@@ -591,6 +645,17 @@
         weights,
     )
 
+    (
+        dinput, outs_early, outs_late, packed, slot_early, slot_late, pre_grad_early, pre_grad_late,
+        act_early, act_late, mixed_early_all, mixed_late,
+    ) = lax.optimization_barrier(
+        (
+            dinput, outs_early, outs_late, packed, slot_early, slot_late, pre_grad_early,
+            pre_grad_late, act_early, act_late, mixed_early_all, mixed_late,
+        )
+    )
+    early_up = jnp.where(is_last, cotangent[0, 0], sent_grads).astype(F32)
+    grads_early = (early_up + dinput.astype(F32)).astype(BF)
     first_grad = dot_dims(
         jnp.concatenate([slot_early, slot_late], axis=0),
         jnp.concatenate([pre_grad_early, pre_grad_late], axis=0),

time: 214 us -> 196 us (0.916)
  the two profiles are of different devices: /device:TPU:32 before, /device:TPU:33 now
where the time goes in v5:
time: 196 us; the launch traced here: 195 us
  blocking collectives  90.9 us (46%)
  waiting for transfers between devices  30.7 us (16%)
  starting transfers between devices  30.6 us (16%)
  Pallas kernels  25.5 us (13%)
  other arithmetic  7.8 us (4%)
  matrix products  3.86 us (2%)
  local copies, waits for them, and re-layouts  3.76 us (2%)
    all_to_all x6, blocking collectives, exchange(): return lax.all_to_all(chunks, axes, 0, 0, tiled=True)  90.9 us
    pallas_call x12, Pallas kernels, run(): pl.pallas_call(body, out_shape=[jax.ShapeDtypeStruct(item[0], item[1]) fo...  25.5 us
    all_to_all x2, starting transfers between devices, exchange(): return lax.all_to_all(chunks, axes, 0, 0, tiled=True)  16.7 us
    ppermute x2, waiting for transfers between devices, section_shift(): return lax.ppermute(block, 'section', route)  15.4 us
    all_to_all x2, waiting for transfers between devices, exchange(): return lax.all_to_all(chunks, axes, 0, 0, tiled=True)  10.4 us
    ppermute x2, starting transfers between devices, section_ring(): lax.ppermute(block, 'section', [(i, (i + distance) % sections) for i in r...  8.56 us
    ppermute x2, starting transfers between devices, section_shift(): return lax.ppermute(block, 'section', route)  5.4 us
    ppermute x2, waiting for transfers between devices, section_ring(): lax.ppermute(block, 'section', [(i, (i + distance) % sections) for i in r...  4.93 us
  transfers between devices with their start and end apart: 6, of which 3 were waited for; matrix products, arithmetic and copies ran while one was open for 6% of the time, Pallas kernels for 6%

profile of v5, /device:TPU:33, one launch (start us, length us, event | category | flops | bytes accessed | tf_op | source)
XLA Modules:
  0.0 194.8 jit_solution(316868319498001022)
XLA Ops:
  0.6 0.0 copy-start.13
  0.6 0.7 copy-done.13
  1.4 1.0 shard_map.145
  2.3 12.8 %all-to-all-start = ((bf16[32,64,128]{2,1,0:T(8,128)(2,1)}), bf16[32,64,128]{2,1,0:T(8,128)(2,1)S(1)}, u32[]{:S(2)}, u32[]{:S(2)}) async-start(bf16[32,64,128]{2,1,0:T(8,128)(2,1)} %shard_map.145), calls=%async_computation | async-start | bytes 1048576 | tf_op jit(solution)/shard_map/all_to_all | solution.py:30
  15.1 0.6 add_convert_fusion.1.flags_ref
  15.7 4.6 %shard_map.144 = (bf16[256,2048]{1,0:T(8,128)(2,1)}, bf16[256,2048]{1,0:T(8,128)(2,1)}, f32[256,128]{1,0:T(8,128)}, f32[8,256]{1,0:T(8,128)}) custom-call(s32[2]{0:T(128)} %add_convert_fusion.1.flags_ref, f32[1,2048]{1,0:T(1,128)} %gain_ref.7, bf16[2,1,256,2048]{3,2,1,0:T(8,128)(2,1)} %tokens_ref.1, bf16[1,1,256,2048]{3,2,1,0:T(8,128)(2,1)} %inflow_ref.1), custom_call_target="tpu_custom_call" | custom-call | flops 30000000 | bytes 4000000 | tf_op jit(solution)/shard_map/pallas_call | solution.py:50
  20.3 3.5 %collective-permute-start = (bf16[256,2048]{1,0:T(8,128)(2,1)}, bf16[256,2048]{1,0:T(8,128)(2,1)}, u32[]{:S(2)}, u32[]{:S(2)}) collective-permute-start(bf16[256,2048]{1,0:T(8,128)(2,1)} %get-tuple-element.63.in_ref), channel_id=1, source_target_pairs={{0,32},{32,64},{64,96},{96,128},{128,160},{160,192},{192,224},{1,3... | collective-permute-start | bytes 3145736 | tf_op jit(solution)/shard_map/ppermute | solution.py:36
  24.5 10.4 %all-to-all-done.chunks_ref = bf16[32,64,128]{2,1,0:T(8,128)(2,1)S(1)} async-done(((bf16[32,64,128]{2,1,0:T(8,128)(2,1)}), bf16[32,64,128]{2,1,0:T(8,128)(2,1)S(1)}, u32[]{:S(2)}, u32[]{:S(2)}) %all-to-all-start) | async-done | bytes 524320 | tf_op jit(solution)/shard_map/all_to_all | solution.py:30
  34.9 1.2 copy-done.4
  36.1 0.7 copy-done.22
  36.8 1.8 shard_map.146
  38.6 15.2 %all_to_all.40.slots_ref = bf16[32,16,128]{2,1,0:T(8,128)(2,1)S(1)} all-to-all(bf16[32,16,128]{2,1,0:T(8,128)(2,1)S(1)} %get-tuple-element.66), channel_id=1, replica_groups=mesh['section'=8,'zh'=2,'y'=4,'x'=4] {'zh','y','x'}, dimensions={0} | all-to-all | bytes 262144 | tf_op jit(solution)/shard_map/all_to_all | solution.py:30
  53.7 0.8 shard_map.147
  54.6 0.0 copy-start
  54.6 0.0 copy-start.8
  54.6 0.0 copy-start.10
  54.6 0.0 copy-start.23
  54.6 14.9 %all_to_all.41.sums_ref = bf16[32,16,128]{2,1,0:T(8,128)(2,1)S(1)} all-to-all(bf16[32,16,128]{2,1,0:T(8,128)(2,1)S(1)} %get-tuple-element.67), channel_id=1, replica_groups=mesh['section'=8,'zh'=2,'y'=4,'x'=4] {'zh','y','x'}, dimensions={0} | all-to-all | bytes 262144 | tf_op jit(solution)/shard_map/all_to_all | solution.py:30
  69.5 6.2 %collective-permute-start.1 = (f32[24,128]{1,0:T(8,128)S(1)}, f32[24,128]{1,0:T(8,128)S(1)}, u32[]{:S(2)}, u32[]{:S(2)}) collective-permute-start(f32[24,128]{1,0:T(8,128)S(1)} %shard_map.148.packed_ref), channel_id=1, source_target_pairs={{0,32},{32,64},{64,96},{96,128},{128,160},{160,192},{192,224},{224... | collective-permute-start | bytes 36872 | tf_op jit(solution)/shard_map/ppermute | solution.py:41
  75.7 1.4 bitcast_select_fusion.base_ref
  77.1 0.0 copy-start.3
  77.1 3.6 %shard_map.149 = (bf16[32,32,128]{2,1,0:T(8,128)(2,1)S(1)}, bf16[256,2048]{1,0:T(8,128)(2,1)S(1)}, bf16[256,2048]{1,0:T(8,128)(2,1)S(1)}, f32[256,128]{1,0:T(8,1...) custom-call(f32[1]{0:T(128)S(6)} %copy.21.scale_ref, ...), custom_call_target="tpu_custom_call" | custom-call | flops 400000000 | bytes 4000000 | tf_op jit(solution)/shard_map/pallas_call | solution.py:50
  80.8 15.1 %all_to_all.42.pairs_ref = bf16[32,32,128]{2,1,0:T(8,128)(2,1)S(1)} all-to-all(bf16[32,32,128]{2,1,0:T(8,128)(2,1)S(1)} %get-tuple-element.70), channel_id=1, replica_groups=mesh['section'=8,'zh'=2,'y'=4,'x'=4] {'zh','y','x'}, dimensions={0} | all-to-all | bytes 524288 | tf_op jit(solution)/shard_map/all_to_all | solution.py:30
  95.9 1.2 shard_map.150
  97.1 16.4 %all_to_all.43.sums_ref = bf16[32,32,128]{2,1,0:T(8,128)(2,1)S(1)} all-to-all(bf16[32,32,128]{2,1,0:T(8,128)(2,1)S(1)} %get-tuple-element.71), channel_id=1, replica_groups=mesh['section'=8,'zh'=2,'y'=4,'x'=4] {'zh','y','x'}, dimensions={0} | all-to-all | bytes 524288 | tf_op jit(solution)/shard_map/all_to_all | solution.py:30
  113.5 5.4 %shard_map.151 = (bf16[256,2048]{1,0:T(8,128)(2,1)}, f32[24,128]{1,0:T(8,128)S(1)}, f32[24,128]{1,0:T(8,128)S(1)}, f32[32,128]{1,0:T(8,128)S(1)}, f32[128,2048]{1,0:T(8,128)S(1)}, /*index=5*/f32[8,2048]{1,0:T(8,128)S(1)}) custom-call(f32[1]{0:T(128)S(6)} %copy.21.scale_ref, s32[2]{0:T(128)S(1)} %copy-done.23, bf16[32,32,128]{2,1,0:T(8,128)(2,1)S(1)} %all_to_all.43.sums_ref, ...), custom_call_target="tpu_custom_call" | custom-call | flops 600000000 | bytes 4000000 | tf_op jit(solution)/shard_map/pallas_call | solution.py:50
  118.9 0.0 copy-start.21
  118.9 0.0 copy-start.5
  118.9 0.0 copy-start.9
  118.9 2.4 %collective-permute-start.2 = (f32[24,128]{1,0:T(8,128)S(1)}, f32[24,128]{1,0:T(8,128)S(1)}, u32[]{:S(2)}, u32[]{:S(2)}) collective-permute-start(f32[24,128]{1,0:T(8,128)S(1)} %get-tuple-element.79), channel_id=1, source_target_pairs={{0,224},{32,0},{64,32},{96,64},{128,96},{160,128},{192,160},{224,1... | collective-permute-start | bytes 36872 | tf_op jit(solution)/shard_map/ppermute | solution.py:41
  121.4 4.9 %collective-permute-done.2.moved_ref = f32[24,128]{1,0:T(8,128)S(1)} collective-permute-done((f32[24,128]{1,0:T(8,128)S(1)}, f32[24,128]{1,0:T(8,128)S(1)}, u32[]{:S(2)}, u32[]{:S(2)}) %collective-permute-start.2) | collective-permute-done | bytes 12320 | tf_op jit(solution)/shard_map/ppermute | solution.py:41
  126.3 0.6 shard_map.152
  126.9 14.7 %all_to_all.44.mixed_in_ref = bf16[32,16,128]{2,1,0:T(8,128)(2,1)S(1)} all-to-all(bf16[32,16,128]{2,1,0:T(8,128)(2,1)S(1)} %get-tuple-element.81), channel_id=1, replica_groups=mesh['section'=8,'zh'=2,'y'=4,'x'=4] {'zh','y','x'}, dimensions={0} | all-to-all | bytes 262144 | tf_op jit(solution)/shard_map/all_to_all | solution.py:30
  141.6 1.3 shard_map.153
  142.9 14.6 %all_to_all.45.sums_ref = bf16[32,16,128]{2,1,0:T(8,128)(2,1)S(1)} all-to-all(bf16[32,16,128]{2,1,0:T(8,128)(2,1)S(1)} %get-tuple-element.83), channel_id=1, replica_groups=mesh['section'=8,'zh'=2,'y'=4,'x'=4] {'zh','y','x'}, dimensions={0} | all-to-all | bytes 262144 | tf_op jit(solution)/shard_map/all_to_all | solution.py:30
  157.5 1.9 collective-permute-start.3
  159.5 4.4 %shard_map.154 = (bf16[256,2048]{1,0:T(8,128)(2,1)S(1)}, f32[16,128]{1,0:T(8,128)S(1)}, bf16[32,80,128]{2,1,0:T(8,128)(2,1)}) custom-call(f32[1]{0:T(128)S(6)} %copy.21.scale_ref, bf16[32,16,128]{2,1,0:T(8,128)(2,1)S(1)} %all_to_all.45.sums_ref, f32[24,128]{1,0:T(8,128)S(1)} %get-tuple-element.87.kept_ref, bf16[256,2048]{1,0:T(8,128)(2,1)S(1)} %copy-done.9, ...), custom_call_target="tpu_custom_call" | custom-call | flops 600000000 | bytes 4000000 | tf_op jit(solution)/shard_map/pallas_call | solution.py:50
  163.9 1.0 copy-done.6
  164.9 0.7 convert.18
  165.6 3.9 %all-to-all-start.7 = ((bf16[32,80,128]{2,1,0:T(8,128)(2,1)}), bf16[32,80,128]{2,1,0:T(8,128)(2,1)S(1)}, u32[]{:S(2)}, u32[]{:S(2)}) async-start(bf16[32,80,128]{2,1,0:T(8,128)(2,1)} %get-tuple-element.116), calls=%async_computation.7 | async-start | bytes 1310720 | tf_op jit(solution)/shard_map/all_to_all | solution.py:30
  169.6 2.4 %fusion.1 = bf16[1,256,2048]{2,1,0:T(8,128)(2,1)} fusion(bf16[32,2048]{1,0:T(8,128)(2,1)S(1)} %get-tuple-element.115, bf16[32,2048]{1,0:T(8,128)(2,1)} %copy-done.11, bf16[32,256]{1,0:T(8,128)(2,1)S(1)} %copy-done.18, bf16[32,256]{1,0:T(8,128)(2,1)S(1)} %get-tuple-element.112), kind=kOutput, calls=%fused_computation.3 | convolution fusion | flops 68222976 | bytes 1343488 | tf_op jit(solution)/shard_map/dot_general | solution.py:21
  172.0 1.4 fusion
  173.5 0.6 pad_maximum_fusion
  174.1 15.4 %collective-permute-done.3 = bf16[256,2048]{1,0:T(8,128)(2,1)} collective-permute-done((bf16[256,2048]{1,0:T(8,128)(2,1)}, bf16[256,2048]{1,0:T(8,128)(2,1)}, u32[]{:S(2)}, u32[]{:S(2)}) %collective-permute-start.3) | collective-permute-done | bytes 1048608 | tf_op jit(solution)/shard_map/ppermute | solution.py:36
  189.5 1.7 fusion.2
  191.2 0.0 copy-start.14
  191.3 2.7 %maximum_bitcast_fusion = bf16[1,2,1,256,2048]{4,3,2,1,0:T(8,128)(2,1)} fusion(bf16[1,256,2048]{2,1,0:T(8,128)(2,1)} %bitcast.9, bf16[1,256,2048]{2,1,0:T(8,128)(2,1)S(1)} %fusion.2), kind=kLoop, calls=%fused_computation.4 | loop fusion | flops 1048576 | bytes 4194304
  194.0 0.8 shard_map.155
  (47 shorter events, 0.2 us)
Async XLA Ops:
  0.6 0.7 copy-start.13
  2.3 32.6 %all-to-all-start = ((bf16[32,64,128]{2,1,0:T(8,128)(2,1)}), bf16[32,64,128]{2,1,0:T(8,128)(2,1)S(1)}, u32[]{:S(2)}, u32[]{:S(2)}) async-start(bf16[32,64,128]{2,1,0:T(8,128)(2,1)} %shard_map.145), calls=%async_computation | async-start | bytes 1048576 | tf_op jit(solution)/shard_map/all_to_all | solution.py:30
  15.7 38.1 %copy-start.1 = (bf16[1,2048,256]{2,1,0:T(8,128)(2,1)S(1)}, bf16[1,2048,256]{2,1,0:T(8,128)(2,1)}, u32[]{:S(2)}) copy-start(bf16[1,2048,256]{2,1,0:T(8,128)(2,1)} %param.16) | copy-start | bytes 3145732
  15.7 38.1 %copy-start.2 = (bf16[1,256,2048]{2,1,0:T(8,128)(2,1)S(1)}, bf16[1,256,2048]{2,1,0:T(8,128)(2,1)}, u32[]{:S(2)}) copy-start(bf16[1,256,2048]{2,1,0:T(8,128)(2,1)} %param.17) | copy-start | bytes 3145732
  20.3 55.4 %collective-permute-start = (bf16[256,2048]{1,0:T(8,128)(2,1)}, bf16[256,2048]{1,0:T(8,128)(2,1)}, u32[]{:S(2)}, u32[]{:S(2)}) collective-permute-start(bf16[256,2048]{1,0:T(8,128)(2,1)} %get-tuple-element.63.in_ref), channel_id=1, source_target_pairs={{0,32},{32,64},{64,96},{96,128},{128,160},{160,192},{192,224},{1,3... | collective-permute-start | bytes 3145736 | tf_op jit(solution)/shard_map/ppermute | solution.py:36
  34.9 1.2 copy-start.4
  36.1 0.7 copy-start.22
  36.8 38.9 %copy-start.24 = (bf16[2,1,256,2048]{3,2,1,0:T(8,128)(2,1)S(1)}, bf16[2,1,256,2048]{3,2,1,0:T(8,128)(2,1)}, u32[]{:S(2)}) copy-start(bf16[2,1,256,2048]{3,2,1,0:T(8,128)(2,1)} %tokens_ref.1) | copy-start | bytes 6291460
  54.6 22.5 %copy-start = (bf16[2,1,256,2048]{3,2,1,0:T(8,128)(2,1)S(1)}, bf16[2,1,256,2048]{3,2,1,0:T(8,128)(2,1)}, u32[]{:S(2)}) copy-start(bf16[2,1,256,2048]{3,2,1,0:T(8,128)(2,1)} %cotangent_ref.3) | copy-start | bytes 6291460
  54.6 22.5 %copy-start.8 = (bf16[1,1,256,2048]{3,2,1,0:T(8,128)(2,1)S(1)}, bf16[1,1,256,2048]{3,2,1,0:T(8,128)(2,1)}, u32[]{:S(2)}) copy-start(bf16[1,1,256,2048]{3,2,1,0:T(8,128)(2,1)} %backflow_ref.1) | copy-start | bytes 3145732
  54.6 22.5 %copy-start.10 = (f32[1,2048]{1,0:T(1,128)S(1)}, f32[1,2048]{1,0:T(1,128)}, u32[]{:S(2)}) copy-start(f32[1,2048]{1,0:T(1,128)} %gain_ref.7) | copy-start | bytes 24580
  54.6 22.5 %copy-start.23 = (s32[2]{0:T(128)S(1)}, s32[2]{0:T(128)}, u32[]{:S(2)}) copy-start(s32[2]{0:T(128)} %add_convert_fusion.1.flags_ref) | copy-start | bytes 28
  69.5 7.5 %collective-permute-start.1 = (f32[24,128]{1,0:T(8,128)S(1)}, f32[24,128]{1,0:T(8,128)S(1)}, u32[]{:S(2)}, u32[]{:S(2)}) collective-permute-start(f32[24,128]{1,0:T(8,128)S(1)} %shard_map.148.packed_ref), channel_id=1, source_target_pairs={{0,32},{32,64},{64,96},{96,128},{128,160},{160,192},{192,224},{224... | collective-permute-start | bytes 36872 | tf_op jit(solution)/shard_map/ppermute | solution.py:41
  77.1 18.8 %copy-start.3 = (bf16[1,256,2048]{2,1,0:T(8,128)(2,1)S(1)}, bf16[1,256,2048]{2,1,0:T(8,128)(2,1)}, u32[]{:S(2)}) copy-start(bf16[1,256,2048]{2,1,0:T(8,128)(2,1)} %param.17) | copy-start | bytes 3145732
  97.1 21.8 %copy-start.15 = (bf16[32,256]{1,0:T(8,128)(2,1)}, bf16[32,256]{1,0:T(8,128)(2,1)S(1)}, u32[]{:S(2)}) copy-start(bf16[32,256]{1,0:T(8,128)(2,1)S(1)} %get-tuple-element.111) | copy-start | bytes 49156
  97.1 21.8 %copy-start.17 = (bf16[32,256]{1,0:T(8,128)(2,1)}, bf16[32,256]{1,0:T(8,128)(2,1)S(1)}, u32[]{:S(2)}) copy-start(bf16[32,256]{1,0:T(8,128)(2,1)S(1)} %get-tuple-element.113) | copy-start | bytes 49156
  118.9 45.0 %copy-start.21 = (f32[32,128]{1,0:T(8,128)}, f32[32,128]{1,0:T(8,128)S(1)}, u32[]{:S(2)}) copy-start(f32[32,128]{1,0:T(8,128)S(1)} %get-tuple-element.106) | copy-start | bytes 49156
  118.9 40.5 %copy-start.5 = (bf16[256,2048]{1,0:T(8,128)(2,1)S(1)}, bf16[256,2048]{1,0:T(8,128)(2,1)}, u32[]{:S(2)}) copy-start(bf16[256,2048]{1,0:T(8,128)(2,1)} %get-tuple-element.65.hidden_in.hidden_ref) | copy-start | bytes 3145732
  118.9 40.5 %copy-start.9 = (bf16[256,2048]{1,0:T(8,128)(2,1)S(1)}, bf16[256,2048]{1,0:T(8,128)(2,1)}, u32[]{:S(2)}) copy-start(bf16[256,2048]{1,0:T(8,128)(2,1)} %get-tuple-element.63.in_ref) | copy-start | bytes 3145732
  118.9 40.5 %copy-start.12 = (f32[256,128]{1,0:T(8,128)S(1)}, f32[256,128]{1,0:T(8,128)}, u32[]{:S(2)}) copy-start(f32[256,128]{1,0:T(8,128)} %get-tuple-element.88.inverse_ref) | copy-start | bytes 393220
  118.9 7.3 %collective-permute-start.2 = (f32[24,128]{1,0:T(8,128)S(1)}, f32[24,128]{1,0:T(8,128)S(1)}, u32[]{:S(2)}, u32[]{:S(2)}) collective-permute-start(f32[24,128]{1,0:T(8,128)S(1)} %get-tuple-element.79), channel_id=1, source_target_pairs={{0,224},{32,0},{64,32},{96,64},{128,96},{160,128},{192,160},{224,1... | collective-permute-start | bytes 36872 | tf_op jit(solution)/shard_map/ppermute | solution.py:41
  142.9 21.0 %copy-start.11 = (bf16[32,2048]{1,0:T(8,128)(2,1)}, bf16[32,2048]{1,0:T(8,128)(2,1)S(1)}, u32[]{:S(2)}) copy-start(bf16[32,2048]{1,0:T(8,128)(2,1)S(1)} %get-tuple-element.114) | copy-start | bytes 393220
  142.9 21.0 %copy-start.19 = (bf16[32,256]{1,0:T(8,128)(2,1)}, bf16[32,256]{1,0:T(8,128)(2,1)S(1)}, u32[]{:S(2)}) copy-start(bf16[32,256]{1,0:T(8,128)(2,1)S(1)} %get-tuple-element.110) | copy-start | bytes 49156
  157.5 32.0 %collective-permute-start.3 = (bf16[256,2048]{1,0:T(8,128)(2,1)}, bf16[256,2048]{1,0:T(8,128)(2,1)}, u32[]{:S(2)}, u32[]{:S(2)}) collective-permute-start(bf16[256,2048]{1,0:T(8,128)(2,1)} %get-tuple-element.85), channel_id=1, source_target_pairs={{32,0},{64,32},{96,64},{128,96},{160,128},{192,160},{224,192},{33,... | collective-permute-start | bytes 3145736 | tf_op jit(solution)/shard_map/ppermute | solution.py:36
  159.5 10.1 %copy-start.18 = (bf16[32,256]{1,0:T(8,128)(2,1)S(1)}, bf16[32,256]{1,0:T(8,128)(2,1)}, u32[]{:S(2)}) copy-start(bf16[32,256]{1,0:T(8,128)(2,1)} %copy-done.17) | copy-start | bytes 49156
  163.9 1.0 copy-start.6
  164.9 7.1 %copy-start.16 = (bf16[32,256]{1,0:T(8,128)(2,1)S(1)}, bf16[32,256]{1,0:T(8,128)(2,1)}, u32[]{:S(2)}) copy-start(bf16[32,256]{1,0:T(8,128)(2,1)} %copy-done.15) | copy-start | bytes 49156
  164.9 7.1 %copy-start.20 = (bf16[32,256]{1,0:T(8,128)(2,1)S(1)}, bf16[32,256]{1,0:T(8,128)(2,1)}, u32[]{:S(2)}) copy-start(bf16[32,256]{1,0:T(8,128)(2,1)} %copy-done.19) | copy-start | bytes 49156
  165.6 28.4 %all-to-all-start.7 = ((bf16[32,80,128]{2,1,0:T(8,128)(2,1)}), bf16[32,80,128]{2,1,0:T(8,128)(2,1)S(1)}, u32[]{:S(2)}, u32[]{:S(2)}) async-start(bf16[32,80,128]{2,1,0:T(8,128)(2,1)} %get-tuple-element.116), calls=%async_computation.7 | async-start | bytes 1310720 | tf_op jit(solution)/shard_map/all_to_all | solution.py:30
  169.6 19.9 %copy-start.7 = (bf16[256,2048]{1,0:T(8,128)(2,1)S(1)}, bf16[256,2048]{1,0:T(8,128)(2,1)}, u32[]{:S(2)}) copy-start(bf16[256,2048]{1,0:T(8,128)(2,1)} %copy-done.6) | copy-start | bytes 3145732
  191.2 2.8 %copy-start.14 = (bf16[1,2048,4]{1,2,0:T(4,128)(2,1)S(1)}, bf16[1,2048,4]{1,2,0:T(4,128)(2,1)}, u32[]{:S(2)}) copy-start(bf16[1,2048,4]{1,2,0:T(4,128)(2,1)} %param.15) | copy-start | bytes 49156

commit v6 on v5

--- a/solution.py
+++ b/solution.py
@@ -11,10 +11,11 @@
 F32 = jnp.float32
 AXES = ("section", "zh", "y", "x")
 DP = ("zh", "y", "x")
+PLANE = ("y", "x")
 LANES = 128
 STEP = 16
 VMEM_BYTES = 24 * 1024 * 1024
-VMEM_MOST = 58 * 1024 * 1024
+VMEM_NORM = VMEM_BYTES
 
 
 def dot_dims(left_side, right_side, left_dim, right_dim):
@@ -34,6 +35,10 @@
     sections = lax.axis_size("section")
     route = [(i, i + distance) for i in range(sections) if 0 <= i + distance < sections]
     return lax.ppermute(block, "section", route)
+
+
+def other_half(block):
+    return lax.ppermute(block, "zh", [(0, 1), (1, 0)])
 
 
 def section_ring(block, distance):
@@ -141,7 +146,15 @@
     weights, inverse = scaled_weights(weights_ref)
     columns = weights * inverse
     rows = [to_chunk(columns[k : k + 1]) for k in range(columns.shape[0])]
-    block = jnp.concatenate(rows, axis=0).astype(BF)
+    send_ref[...] = jnp.concatenate(rows, axis=0).astype(BF)
+
+
+def order_kernel(flags_ref, own_ref, other_ref, send_ref):
+    own = own_ref[...].astype(F32)
+    other = other_ref[...].astype(F32)
+    upper = flags_ref[2] != 0
+    pair = [jnp.where(upper, other, own), jnp.where(upper, own, other)]
+    block = jnp.concatenate(pair, axis=0).astype(BF)
     send_ref[...] = jnp.broadcast_to(block[None], send_ref.shape)
 
 
@@ -162,9 +175,9 @@
     return lax.rsqrt(total + EPSILON)
 
 
-def slot_front(scale, columns_ref, hidden_ref, length, logits_ref, prob_ref, rows_ref):
+def slot_front(scaled, columns_ref, hidden_ref, length, logits_ref, prob_ref, rows_ref):
     product = dot_dims(columns_ref[...], hidden_ref[...], 1, 1)
-    logits = scale * product * length
+    logits = product * scaled
     expo = jnp.exp(logits)
     first = expo[:1]
     norm = jnp.sum(expo, axis=0, keepdims=True)
@@ -183,13 +196,11 @@
 
 
 def norm_kernel(
-    flags_ref, gain_ref, tokens_ref, inflow_ref,
-    start_ref, hidden_out, inverse_ref, length_ref,
-    in_ref, hidden_ref, sums_ref, in_sem, out_sem, hidden_sem,
+    scale_ref, flags_ref, gain_ref, tokens_ref, inflow_ref,
+    in_ref, hidden_ref, inverse_ref, length_ref, sums_ref, in_sem,
 ):
     begin_copy(flags_ref[0], tokens_ref.at[0, 0], inflow_ref.at[0, 0], in_ref, in_sem)
     end_copy(inflow_ref.at[0, 0], in_ref, in_sem)
-    pltpu.make_async_copy(in_ref, start_ref, out_sem).start()
 
     def square_rows(window):
         wide = in_ref[window, :].astype(F32)
@@ -197,26 +208,24 @@
 
     passes(in_ref, square_rows)
     length = norm_passes(in_ref, gain_ref[...], hidden_ref, inverse_ref, sums_ref)
-    length_ref[...] = jnp.broadcast_to(length, length_ref.shape)
-    pltpu.make_async_copy(hidden_ref, hidden_out, hidden_sem).start()
-    end_copy(in_ref, start_ref, out_sem)
-    end_copy(hidden_ref, hidden_out, hidden_sem)
+    length_ref[...] = stack_rows([length, length * scale_ref[0]], 8, F32)
 
 
 def early_kernel(
-    scale_ref, chunks_ref, length_ref, hidden_in,
-    send_ref, columns_ref, logits_ref, prob_ref, rows_ref,
-    hidden_ref, wide_ref, hidden_sem,
-):
-    pltpu.make_async_copy(hidden_in, hidden_ref, hidden_sem).start()
+    chunks_ref, length_ref, hidden_ref,
+    send_ref, columns_ref, logits_ref, prob_ref, rows_ref, wide_ref,
+):
     peers = chunks_ref.shape[0]
     chunk = hidden_ref.shape[1] // LANES
     wide_ref[...] = chunks_ref[...].astype(F32)
-    for k in range(chunks_ref.shape[1] // chunk):
-        columns_ref[k * peers : (k + 1) * peers] = wide_rows(wide_ref, k * chunk, chunk).astype(BF)
-    end_copy(hidden_in, hidden_ref, hidden_sem)
+    local = chunks_ref.shape[1] // (2 * chunk)
+    for k in range(local):
+        for z in range(2):
+            place = (2 * k + z) * peers
+            values = wide_rows(wide_ref, (z * local + k) * chunk, chunk)
+            columns_ref[place : place + peers] = values.astype(BF)
     _, slot = slot_front(
-        scale_ref[0], columns_ref, hidden_ref, length_ref[:1], logits_ref, prob_ref, rows_ref
+        length_ref[1:2], columns_ref, hidden_ref, length_ref[:1], logits_ref, prob_ref, rows_ref
     )
     send_ref[...] = jnp.broadcast_to(to_chunk(slot).astype(BF)[None], send_ref.shape)
 
@@ -252,7 +261,7 @@
     passes(in_ref, add_rows)
     length = norm_passes(in_ref, gain_ref[...], hidden_ref, inverse_ref, sums_ref)
     combine, slot = slot_front(
-        scale_ref[0], columns_ref, hidden_ref, length, logits_ref, prob_ref, rows_ref
+        scale_ref[0] * length, columns_ref, hidden_ref, length, logits_ref, prob_ref, rows_ref
     )
     end_copy(backflow_ref.at[0, 0], up_ref, up_sem)
     mixed = mix_rows(combine, up_ref[...])
@@ -453,7 +462,10 @@
     )
 
 
-def final_kernel(chunks_ref, weights_ref, router_ref, gain_ref):
+def final_kernel(
+    chunks_ref, weights_ref, packed_ref, outs_late_ref, outs_early_ref,
+    router_ref, gain_ref, slot_out_ref, slot_grad_ref,
+):
     weights, inverse = scaled_weights(weights_ref)
     total = jnp.sum(chunks_ref[...].astype(F32), axis=0)
     count = weights.shape[0]
@@ -463,6 +475,11 @@
     dots = jnp.sum(pulled * weights, axis=1, keepdims=True)
     router_ref[...] = (inverse * (pulled - weights * (dots * inverse * inverse))).astype(BF)
     gain_ref[...] = to_row(total[count * chunk :])
+    late = outs_late_ref[...]
+    outs = [to_row(packed_ref[:chunk]), to_row(late[:chunk])]
+    grads = [to_row(outs_early_ref[...]), to_row(late[chunk:])]
+    slot_out_ref[...] = jnp.concatenate(outs, axis=0).astype(BF)
+    slot_grad_ref[...] = jnp.concatenate(grads, axis=0).astype(BF)
 
 
 def shards(
@@ -479,7 +496,7 @@
     section_index = lax.axis_index("section")
     is_first = section_index == 0
     is_last = section_index == lax.axis_size("section") - 1
-    flags = jnp.stack([is_first, is_last]).astype(jnp.int32)
+    flags = jnp.stack([is_first, is_last, lax.axis_index("zh") == 1]).astype(jnp.int32)
     group = lax.axis_size(DP)
     patches = tokens.shape[2]
     width = tokens.shape[3]
@@ -500,30 +517,40 @@
     every_hidden = ((group, hidden_units), BF)
     copy_sem = pltpu.SemaphoreType.DMA
 
-    columns_block = run(
-        columns_kernel, [((group, local * chunk, LANES), BF)], [], 1000000, 1, weights
-    )[0]
+    plane = group // 2
+    block = run(columns_kernel, [((local * chunk, LANES), BF)], [], 1000000, 1, weights)[0]
     start_in, hidden_early, inverse_early, length_early = run(
         norm_kernel,
-        [token_block + ("far",), token_block + ("far",), column, rows],
-        [token_block, token_block, column, copy_sem, copy_sem, copy_sem],
+        [token_block, token_block, column, rows],
+        [column, copy_sem],
         30000000,
-        2,
+        3,
+        slot_scale,
         flags,
         norm_gain,
         tokens,
         inflow,
-        vmem=VMEM_MOST,
-    )
-    sent_in = section_shift(start_in, 1)
+        vmem=VMEM_NORM,
+    )
+    other, length_early = lax.optimization_barrier((other_half(block), length_early))
+    send = run(
+        order_kernel,
+        [((plane, 2 * local * chunk, LANES), BF)],
+        [],
+        1000000,
+        3,
+        flags,
+        block,
+        other,
+    )[0]
+    sent_in = section_ring(start_in, 1)
     send, columns, logits_early, prob_early, rows_early = run(
         early_kernel,
         [single, ((slots, width), BF), table, table, rows],
-        [token_block, ((group, local * chunk, LANES), F32), copy_sem],
+        [((plane, 2 * local * chunk, LANES), F32)],
         300000000,
         3,
-        slot_scale,
-        exchange(columns_block, DP),
+        exchange(send, PLANE),
         length_early,
         hidden_early,
     )
@@ -614,7 +641,7 @@
     )
     last_rows = (local + 1) * chunk
     slot_sums, held_grads = lax.optimization_barrier((exchange(part, DP), grads_late))
-    sent_grads = section_shift(held_grads, -1)
+    sent_grads = section_ring(held_grads, -1)
     dinput, outs_early, finals = run(
         back_early_kernel,
         [token_block, ((chunk, LANES), F32), ((group, last_rows, LANES), BF)],
@@ -635,23 +662,26 @@
         router_late,
         gain_late,
     )
-    router_grad, gain_total = run(
+    router_grad, gain_total, slot_out, slot_grad = run(
         final_kernel,
-        [((local, width), BF), ((1, width), F32)],
+        [((local, width), BF), ((1, width), F32), ((2, width), BF), ((2, width), BF)],
         [],
         1000000,
-        2,
+        5,
         exchange(finals, DP),
         weights,
+        packed,
+        outs_late,
+        outs_early,
     )
 
     (
-        dinput, outs_early, outs_late, packed, slot_early, slot_late, pre_grad_early, pre_grad_late,
-        act_early, act_late, mixed_early_all, mixed_late,
+        dinput, slot_early, slot_late, pre_grad_early, pre_grad_late, act_early, act_late,
+        mixed_early_all, mixed_late, grads_late,
     ) = lax.optimization_barrier(
         (
-            dinput, outs_early, outs_late, packed, slot_early, slot_late, pre_grad_early,
-            pre_grad_late, act_early, act_late, mixed_early_all, mixed_late,
+            dinput, slot_early, slot_late, pre_grad_early, pre_grad_late, act_early, act_late,
+            mixed_early_all, mixed_late, grads_late,
         )
     )
     early_up = jnp.where(is_last, cotangent[0, 0], sent_grads).astype(F32)
@@ -668,12 +698,10 @@
         0,
         0,
     )
-    slot_out = jnp.stack([packed[:chunk].reshape(1, width), outs_late[:chunk].reshape(1, width)])
-    slot_grad = jnp.stack([outs_early.reshape(1, width), outs_late[chunk:].reshape(1, width)])
     return (
         jnp.stack([grads_early, grads_late])[None, :, None],
-        slot_out.astype(BF)[None],
-        slot_grad.astype(BF)[None],
+        slot_out[None, :, None],
+        slot_grad[None, :, None],
         first_grad.astype(BF)[None],
         second_grad.astype(BF)[None],
         router_grad.T[None],

time: 196 us -> 189 us (0.964)
  the two profiles are of different devices: /device:TPU:33 before, /device:TPU:32 now
where the time goes in v6:
time: 189 us; the launch traced here: 188 us
  blocking collectives  122 us (65%)
  Pallas kernels  21.9 us (12%)
  waiting for transfers between devices  19.9 us (11%)
  starting transfers between devices  10.7 us (6%)
  local copies, waits for them, and re-layouts  5.24 us (3%)
  other arithmetic  4.66 us (2%)
  matrix products  2.87 us (2%)
    all_to_all x7, blocking collectives, exchange(): return lax.all_to_all(chunks, axes, 0, 0, tiled=True)  122 us
    pallas_call x13, Pallas kernels, run(): pl.pallas_call(body, out_shape=[jax.ShapeDtypeStruct(item[0], item[1]) fo...  21.9 us
    ppermute x4, waiting for transfers between devices, section_ring(): lax.ppermute(block, 'section', [(i, (i + distance) % sections) for i in r...  14.7 us
    ppermute x1, starting transfers between devices, other_half(): return lax.ppermute(block, 'zh', [(0, 1), (1, 0)])  6.38 us
    unnamed x26, local copies, waits for them, and re-layouts  5.24 us
    all_to_all x1, waiting for transfers between devices, exchange(): return lax.all_to_all(chunks, axes, 0, 0, tiled=True)  5.15 us
    all_to_all x1, starting transfers between devices, exchange(): return lax.all_to_all(chunks, axes, 0, 0, tiled=True)  3.9 us
  transfers between devices with their start and end apart: 6, of which 4 were waited for; matrix products, arithmetic and copies ran while one was open for 4% of the time, Pallas kernels for 5%

profile of v6, /device:TPU:32, one launch (start us, length us, event | category | flops | bytes accessed | tf_op | source)
XLA Modules:
  0.0 188.4 jit_solution(13695331968186709370)
XLA Ops:
  0.6 0.0 copy-start.11
  0.6 0.7 copy-done.11
  1.4 0.1 shard_map.145.own_ref
  1.5 6.4 %collective-permute-start.1 = (bf16[64,128]{1,0:T(8,128)(2,1)S(1)}, bf16[64,128]{1,0:T(8,128)(2,1)S(1)}, u32[]{:S(2)}, u32[]{:S(2)}) collective-permute-start(bf16[64,128]{1,0:T(8,128)(2,1)S(1)} %shard_map.145.own_ref), channel_id=1, source_target_pairs={{0,16},{16,0},{1,17},{17,1},{2,18},{18,2},{3,19},{19,3},{4,20},{20... | collective-permute-start | bytes 49160 | tf_op jit(solution)/shard_map/ppermute | solution.py:41
  8.5 0.1 add_convert_fusion.1.flags_ref
  8.6 1.6 copy-done.3
  10.2 1.2 copy-done.7
  11.4 0.7 copy-done.9
  12.1 1.7 shard_map.144
  13.8 0.0 copy-start.1
  13.8 0.0 copy-start.2
  13.8 0.1 collective-permute-start
  13.9 0.6 shard_map.146
  14.5 19.9 %all_to_all.40.chunks_ref = bf16[16,128,128]{2,1,0:T(8,128)(2,1)S(1)} all-to-all(bf16[16,128,128]{2,1,0:T(8,128)(2,1)S(1)} %shard_map.146), channel_id=1, replica_groups=mesh['section'=8,'zh'=2,'y'=4,'x'=4] {'y','x'}, dimensions={0} | all-to-all | bytes 1048576 | tf_op jit(solution)/shard_map/all_to_all | solution.py:31
  34.4 1.3 shard_map.147
  35.7 15.8 %all_to_all.41.slots_ref = bf16[32,16,128]{2,1,0:T(8,128)(2,1)S(1)} all-to-all(bf16[32,16,128]{2,1,0:T(8,128)(2,1)S(1)} %get-tuple-element.70), channel_id=1, replica_groups=mesh['section'=8,'zh'=2,'y'=4,'x'=4] {'zh','y','x'}, dimensions={0} | all-to-all | bytes 262144 | tf_op jit(solution)/shard_map/all_to_all | solution.py:31
  51.6 0.8 shard_map.148
  52.4 0.0 copy-start
  52.4 0.0 copy-start.8
  52.4 0.0 copy-start.10
  52.4 16.3 %all_to_all.42.sums_ref = bf16[32,16,128]{2,1,0:T(8,128)(2,1)S(1)} all-to-all(bf16[32,16,128]{2,1,0:T(8,128)(2,1)S(1)} %get-tuple-element.71), channel_id=1, replica_groups=mesh['section'=8,'zh'=2,'y'=4,'x'=4] {'zh','y','x'}, dimensions={0} | all-to-all | bytes 262144 | tf_op jit(solution)/shard_map/all_to_all | solution.py:31
  68.7 0.1 collective-permute-start.2
  68.8 0.0 collective-permute-done
  68.8 0.1 bitcast_select_fusion.base_ref
  69.0 3.0 %collective-permute-done.2.moved_ref = f32[24,128]{1,0:T(8,128)S(1)} collective-permute-done((f32[24,128]{1,0:T(8,128)S(1)}, f32[24,128]{1,0:T(8,128)S(1)}, u32[]{:S(2)}, u32[]{:S(2)}) %collective-permute-start.2) | collective-permute-done | bytes 12320 | tf_op jit(solution)/shard_map/ppermute | solution.py:46
  71.9 3.6 %shard_map.150 = (bf16[32,32,128]{2,1,0:T(8,128)(2,1)S(1)}, bf16[256,2048]{1,0:T(8,128)(2,1)S(1)}, bf16[256,2048]{1,0:T(8,128)(2,1)S(1)}, f32[256,128]{1,0:T(8,1...) custom-call(f32[1]{0:T(128)S(6)} %copy.17.scale_ref, ...), custom_call_target="tpu_custom_call" | custom-call | flops 400000000 | bytes 4000000 | tf_op jit(solution)/shard_map/pallas_call | solution.py:55
  75.6 20.0 %all_to_all.43.pairs_ref = bf16[32,32,128]{2,1,0:T(8,128)(2,1)S(1)} all-to-all(bf16[32,32,128]{2,1,0:T(8,128)(2,1)S(1)} %get-tuple-element.74), channel_id=1, replica_groups=mesh['section'=8,'zh'=2,'y'=4,'x'=4] {'zh','y','x'}, dimensions={0} | all-to-all | bytes 524288 | tf_op jit(solution)/shard_map/all_to_all | solution.py:31
  95.5 1.2 shard_map.151
  96.7 17.1 %all_to_all.44.sums_ref = bf16[32,32,128]{2,1,0:T(8,128)(2,1)S(1)} all-to-all(bf16[32,32,128]{2,1,0:T(8,128)(2,1)S(1)} %get-tuple-element.75), channel_id=1, replica_groups=mesh['section'=8,'zh'=2,'y'=4,'x'=4] {'zh','y','x'}, dimensions={0} | all-to-all | bytes 524288 | tf_op jit(solution)/shard_map/all_to_all | solution.py:31
  113.8 5.4 %shard_map.152 = (bf16[256,2048]{1,0:T(8,128)(2,1)}, f32[24,128]{1,0:T(8,128)S(1)}, f32[24,128]{1,0:T(8,128)S(1)}, f32[32,128]{1,0:T(8,128)S(1)}, f32[128,2048]{1,0:T(8,128)S(1)}, /*index=5*/f32[8,2048]{1,0:T(8,128)S(1)}) custom-call(f32[1]{0:T(128)S(6)} %copy.17.scale_ref, s32[3]{0:T(128)S(1)} %add_convert_fusion.1.flags_ref, ...), custom_call_target="tpu_custom_call" | custom-call | flops 600000000 | bytes 4000000 | tf_op jit(solution)/shard_map/pallas_call | solution.py:55
  119.2 0.3 collective-permute-start.3
  119.4 1.4 collective-permute-done.3.moved_ref
  120.8 0.6 shard_map.153
  121.4 16.3 %all_to_all.45.mixed_in_ref = bf16[32,16,128]{2,1,0:T(8,128)(2,1)S(1)} all-to-all(bf16[32,16,128]{2,1,0:T(8,128)(2,1)S(1)} %get-tuple-element.85), channel_id=1, replica_groups=mesh['section'=8,'zh'=2,'y'=4,'x'=4] {'zh','y','x'}, dimensions={0} | all-to-all | bytes 262144 | tf_op jit(solution)/shard_map/all_to_all | solution.py:31
  137.7 1.3 shard_map.154
  139.0 16.4 %all_to_all.46.sums_ref = bf16[32,16,128]{2,1,0:T(8,128)(2,1)S(1)} all-to-all(bf16[32,16,128]{2,1,0:T(8,128)(2,1)S(1)} %get-tuple-element.87), channel_id=1, replica_groups=mesh['section'=8,'zh'=2,'y'=4,'x'=4] {'zh','y','x'}, dimensions={0} | all-to-all | bytes 262144 | tf_op jit(solution)/shard_map/all_to_all | solution.py:31
  155.4 4.4 %shard_map.155 = (bf16[256,2048]{1,0:T(8,128)(2,1)S(1)}, f32[16,128]{1,0:T(8,128)S(1)}, bf16[32,80,128]{2,1,0:T(8,128)(2,1)}) custom-call(f32[1]{0:T(128)S(6)} %copy.17.scale_ref, bf16[32,16,128]{2,1,0:T(8,128)(2,1)S(1)} %all_to_all.46.sums_ref, f32[24,128]{1,0:T(8,128)S(1)} %get-tuple-element.91.kept_ref, bf16[256,2048]{1,0:T(8,128)(2,1)S(1)} %get-tuple-element.65.in_ref, ...), custom_call_target="tpu_custom_call" | custom-call | flops 600000000 | bytes 4000000 | tf_op jit(solution)/shard_map/pallas_call | solution.py:55
  159.8 1.0 copy-done.5
  160.8 3.9 %all-to-all-start.7 = ((bf16[32,80,128]{2,1,0:T(8,128)(2,1)}), bf16[32,80,128]{2,1,0:T(8,128)(2,1)S(1)}, u32[]{:S(2)}, u32[]{:S(2)}) async-start(bf16[32,80,128]{2,1,0:T(8,128)(2,1)} %get-tuple-element.108), calls=%async_computation.7 | async-start | bytes 1310720 | tf_op jit(solution)/shard_map/all_to_all | solution.py:31
  164.7 0.0 copy-start.6
  164.7 1.4 fusion.1
  166.1 1.4 fusion
  167.6 10.4 %collective-permute-done.4 = bf16[256,2048]{1,0:T(8,128)(2,1)} collective-permute-done((bf16[256,2048]{1,0:T(8,128)(2,1)}, bf16[256,2048]{1,0:T(8,128)(2,1)}, u32[]{:S(2)}, u32[]{:S(2)}) %collective-permute-start.4) | collective-permute-done | bytes 1048608 | tf_op jit(solution)/shard_map/ppermute | solution.py:46
  177.9 1.7 fusion.2
  179.7 0.0 copy-start.12
  179.7 2.7 %maximum_bitcast_fusion = bf16[1,2,1,256,2048]{4,3,2,1,0:T(8,128)(2,1)} fusion(bf16[1,256,2048]{2,1,0:T(8,128)(2,1)} %bitcast.10, bf16[1,256,2048]{2,1,0:T(8,128)(2,1)S(1)} %fusion.2), kind=kLoop, calls=%fused_computation.4 | loop fusion | flops 1048576 | bytes 4194304
  182.4 5.2 %all-to-all-done.7.chunks_ref = bf16[32,80,128]{2,1,0:T(8,128)(2,1)S(1)} async-done(((bf16[32,80,128]{2,1,0:T(8,128)(2,1)}), bf16[32,80,128]{2,1,0:T(8,128)(2,1)S(1)}, u32[]{:S(2)}, u32[]{:S(2)}) %all-to-all-start.7) | async-done | bytes 655392 | tf_op jit(solution)/shard_map/all_to_all | solution.py:31
  187.6 0.8 shard_map.156
  (16 shorter events, 0.1 us)
Async XLA Ops:
  0.6 0.7 copy-start.11
  1.5 12.4 %collective-permute-start.1 = (bf16[64,128]{1,0:T(8,128)(2,1)S(1)}, bf16[64,128]{1,0:T(8,128)(2,1)S(1)}, u32[]{:S(2)}, u32[]{:S(2)}) collective-permute-start(bf16[64,128]{1,0:T(8,128)(2,1)S(1)} %shard_map.145.own_ref), channel_id=1, source_target_pairs={{0,16},{16,0},{1,17},{17,1},{2,18},{18,2},{3,19},{19,3},{4,20},{20... | collective-permute-start | bytes 49160 | tf_op jit(solution)/shard_map/ppermute | solution.py:41
  8.6 1.6 copy-start.3
  10.2 1.2 copy-start.7
  11.4 0.7 copy-start.9
  13.8 37.7 %copy-start.1 = (bf16[1,2048,256]{2,1,0:T(8,128)(2,1)S(1)}, bf16[1,2048,256]{2,1,0:T(8,128)(2,1)}, u32[]{:S(2)}) copy-start(bf16[1,2048,256]{2,1,0:T(8,128)(2,1)} %param.16) | copy-start | bytes 3145732
  13.8 37.7 %copy-start.2 = (bf16[1,256,2048]{2,1,0:T(8,128)(2,1)S(1)}, bf16[1,256,2048]{2,1,0:T(8,128)(2,1)}, u32[]{:S(2)}) copy-start(bf16[1,256,2048]{2,1,0:T(8,128)(2,1)} %param.17) | copy-start | bytes 3145732
  13.8 55.0 %collective-permute-start = (bf16[256,2048]{1,0:T(8,128)(2,1)S(1)}, bf16[256,2048]{1,0:T(8,128)(2,1)S(1)}, u32[]{:S(2)}, u32[]{:S(2)}) collective-permute-start(bf16[256,2048]{1,0:T(8,128)(2,1)S(1)} %get-tuple-element.65.in_ref), channel_id=1, source_target_pairs={{0,32},{32,64},{64,96},{96,128},{128,160},{160,192},{192,224},{224... | collective-permute-start | bytes 3145736 | tf_op jit(solution)/shard_map/ppermute | solution.py:46
  34.4 34.4 %copy-start.4 = (bf16[2,1,256,2048]{3,2,1,0:T(8,128)(2,1)S(1)}, bf16[2,1,256,2048]{3,2,1,0:T(8,128)(2,1)}, u32[]{:S(2)}) copy-start(bf16[2,1,256,2048]{3,2,1,0:T(8,128)(2,1)} %tokens_ref.1) | copy-start | bytes 6291460
  52.4 19.5 %copy-start = (bf16[2,1,256,2048]{3,2,1,0:T(8,128)(2,1)S(1)}, bf16[2,1,256,2048]{3,2,1,0:T(8,128)(2,1)}, u32[]{:S(2)}) copy-start(bf16[2,1,256,2048]{3,2,1,0:T(8,128)(2,1)} %cotangent_ref.3) | copy-start | bytes 6291460
  52.4 19.5 %copy-start.8 = (bf16[1,1,256,2048]{3,2,1,0:T(8,128)(2,1)S(1)}, bf16[1,1,256,2048]{3,2,1,0:T(8,128)(2,1)}, u32[]{:S(2)}) copy-start(bf16[1,1,256,2048]{3,2,1,0:T(8,128)(2,1)} %backflow_ref.1) | copy-start | bytes 3145732
  52.4 19.5 %copy-start.10 = (f32[1,2048]{1,0:T(1,128)S(1)}, f32[1,2048]{1,0:T(1,128)}, u32[]{:S(2)}) copy-start(f32[1,2048]{1,0:T(1,128)} %gain_ref.7) | copy-start | bytes 24580
  68.7 3.2 %collective-permute-start.2 = (f32[24,128]{1,0:T(8,128)S(1)}, f32[24,128]{1,0:T(8,128)S(1)}, u32[]{:S(2)}, u32[]{:S(2)}) collective-permute-start(f32[24,128]{1,0:T(8,128)S(1)} %shard_map.149.packed_ref), channel_id=1, source_target_pairs={{0,32},{32,64},{64,96},{96,128},{128,160},{160,192},{192,224},{224... | collective-permute-start | bytes 36872 | tf_op jit(solution)/shard_map/ppermute | solution.py:46
  119.2 1.7 collective-permute-start.3
  155.4 22.6 %collective-permute-start.4 = (bf16[256,2048]{1,0:T(8,128)(2,1)}, bf16[256,2048]{1,0:T(8,128)(2,1)}, u32[]{:S(2)}, u32[]{:S(2)}) collective-permute-start(bf16[256,2048]{1,0:T(8,128)(2,1)} %get-tuple-element.89), channel_id=1, source_target_pairs={{0,224},{32,0},{64,32},{96,64},{128,96},{160,128},{192,160},{224,1... | collective-permute-start | bytes 3145736 | tf_op jit(solution)/shard_map/ppermute | solution.py:46
  159.8 1.0 copy-start.5
  160.8 26.8 %all-to-all-start.7 = ((bf16[32,80,128]{2,1,0:T(8,128)(2,1)}), bf16[32,80,128]{2,1,0:T(8,128)(2,1)S(1)}, u32[]{:S(2)}, u32[]{:S(2)}) async-start(bf16[32,80,128]{2,1,0:T(8,128)(2,1)} %get-tuple-element.108), calls=%async_computation.7 | async-start | bytes 1310720 | tf_op jit(solution)/shard_map/all_to_all | solution.py:31
  164.7 13.3 %copy-start.6 = (bf16[256,2048]{1,0:T(8,128)(2,1)S(1)}, bf16[256,2048]{1,0:T(8,128)(2,1)}, u32[]{:S(2)}) copy-start(bf16[256,2048]{1,0:T(8,128)(2,1)} %copy-done.5) | copy-start | bytes 3145732
  179.7 7.9 %copy-start.12 = (bf16[1,2048,4]{1,2,0:T(4,128)(2,1)S(1)}, bf16[1,2048,4]{1,2,0:T(4,128)(2,1)}, u32[]{:S(2)}) copy-start(bf16[1,2048,4]{1,2,0:T(4,128)(2,1)} %param.15) | copy-start | bytes 49156

commit v7 on v6

--- a/solution.py
+++ b/solution.py
@@ -15,7 +15,6 @@
 LANES = 128
 STEP = 16
 VMEM_BYTES = 24 * 1024 * 1024
-VMEM_NORM = VMEM_BYTES
 
 
 def dot_dims(left_side, right_side, left_dim, right_dim):
@@ -196,12 +195,8 @@
 
 
 def norm_kernel(
-    scale_ref, flags_ref, gain_ref, tokens_ref, inflow_ref,
-    in_ref, hidden_ref, inverse_ref, length_ref, sums_ref, in_sem,
-):
-    begin_copy(flags_ref[0], tokens_ref.at[0, 0], inflow_ref.at[0, 0], in_ref, in_sem)
-    end_copy(inflow_ref.at[0, 0], in_ref, in_sem)
-
+    scale_ref, gain_ref, in_ref, hidden_ref, inverse_ref, length_ref, sums_ref
+):
     def square_rows(window):
         wide = in_ref[window, :].astype(F32)
         sums_ref[window, :] = lane_sums(wide * wide)
@@ -357,8 +352,11 @@
     pull = jnp.sum(dlogits * logits_ref[...], axis=0, keepdims=True) * length * length
     pull_ref[...] = to_column(pull)
     dproduct_bf = dproduct.astype(BF)
-    hold_ref[...] = dot_dims(dproduct_bf, columns_ref[...], 0, 0) + dot_dims(
-        first_rows([spread]), grad_rows, 0, 0
+    hold_ref[...] = dot_dims(
+        jnp.concatenate([dproduct_bf, first_rows([spread])], axis=0),
+        jnp.concatenate([columns_ref[...], grad_rows], axis=0),
+        0,
+        0,
     )
     router = jnp.dot(dproduct_bf, hidden_ref[...], preferred_element_type=F32)
 
@@ -390,8 +388,8 @@
 def back_late_kernel(
     scale_ref, flags_ref, sums_ref, in_ref, hidden_ref, inverse_ref, logits_ref, prob_ref,
     rows_ref, up_ref, columns_ref, gain_ref, moved_ref, rows_own_ref, packed_ref, cotangent_ref,
-    grads_ref, moved_out, own_out, outs_ref, router_ref, gain_out,
-    own_ref, hold_ref, pull_ref, mean_ref, own_sem,
+    grads_out, moved_out, own_out, outs_ref, router_ref, gain_out,
+    own_ref, grads_ref, hold_ref, pull_ref, mean_ref, own_sem, grads_sem,
 ):
     last = flags_ref[1] != 0
 
@@ -414,6 +412,9 @@
         scale_ref[0], dcombine, dspread, grad_row, in_ref, hidden_ref, inverse_ref, logits_ref,
         prob_ref, rows_ref, columns_ref, gain_ref, hold_ref, pull_ref, mean_ref, put_grads,
     )
+
+    leave = pltpu.make_async_copy(grads_ref, grads_out, grads_sem)
+    leave.start()
 
     def message(combine, out_row, ref, out):
         mixed = to_chunk(mix_rows(combine, ref[...]).astype(BF).astype(F32))
@@ -429,6 +430,8 @@
     def _():
         end_copy(cotangent_ref.at[0, 0], own_ref, own_sem)
         message(rows_own_ref[1:2], to_row(packed_ref[:chunk]), own_ref, own_out)
+
+    leave.wait()
 
 
 def back_early_kernel(
@@ -454,7 +457,8 @@
     peers = send_ref.shape[0]
     count = router.shape[0] // peers
     for k in range(count):
-        put_rows(wide_ref, k * chunk, router[k * peers : (k + 1) * peers])
+        place = (k % 2) * (count // 2) + k // 2
+        put_rows(wide_ref, place * chunk, router[k * peers : (k + 1) * peers])
     send_ref[:, : count * chunk, :] = wide_ref[...].astype(BF)
     gain_row = jnp.sum(gain_sum + gain_in_ref[...], axis=0, keepdims=True)
     send_ref[:, count * chunk :, :] = jnp.broadcast_to(
@@ -462,12 +466,21 @@
     )
 
 
+def plane_kernel(flags_ref, chunks_ref, kept_ref, given_ref):
+    total = jnp.sum(chunks_ref[...].astype(F32), axis=0)
+    count = chunks_ref.shape[1] - kept_ref.shape[0]
+    low, high, gain = total[:count], total[count : 2 * count], total[2 * count :]
+    upper = flags_ref[2] != 0
+    kept_ref[...] = jnp.concatenate([jnp.where(upper, high, low), gain], axis=0)
+    given_ref[...] = jnp.concatenate([jnp.where(upper, low, high), gain], axis=0)
+
+
 def final_kernel(
-    chunks_ref, weights_ref, packed_ref, outs_late_ref, outs_early_ref,
+    kept_ref, taken_ref, weights_ref, packed_ref, outs_late_ref, outs_early_ref,
     router_ref, gain_ref, slot_out_ref, slot_grad_ref,
 ):
     weights, inverse = scaled_weights(weights_ref)
-    total = jnp.sum(chunks_ref[...].astype(F32), axis=0)
+    total = kept_ref[...] + taken_ref[...]
     count = weights.shape[0]
     chunk = weights.shape[1] // LANES
     rows = [to_row(total[k * chunk : (k + 1) * chunk]) for k in range(count)]
@@ -519,18 +532,16 @@
 
     plane = group // 2
     block = run(columns_kernel, [((local * chunk, LANES), BF)], [], 1000000, 1, weights)[0]
-    start_in, hidden_early, inverse_early, length_early = run(
+    start_in = jnp.where(is_first, tokens[0, 0], inflow[0, 0])
+    hidden_early, inverse_early, length_early = run(
         norm_kernel,
-        [token_block, token_block, column, rows],
-        [column, copy_sem],
+        [token_block, column, rows],
+        [column],
         30000000,
         3,
         slot_scale,
-        flags,
         norm_gain,
-        tokens,
-        inflow,
-        vmem=VMEM_NORM,
+        start_in,
     )
     other, length_early = lax.optimization_barrier((other_half(block), length_early))
     send = run(
@@ -602,10 +613,10 @@
     grads_late, moved_back, own_back, outs_late, router_late, gain_late = run(
         back_late_kernel,
         [
-            token_block, message, message, ((2 * chunk, LANES), F32), ((slots, width), F32),
-            ((8, width), F32),
+            token_block + ("far",), message, message, ((2 * chunk, LANES), F32),
+            ((slots, width), F32), ((8, width), F32),
         ],
-        [token_block] + back_scratch + [copy_sem],
+        [token_block, token_block] + back_scratch + [copy_sem, copy_sem],
         600000000,
         15,
         slot_scale,
@@ -639,13 +650,13 @@
         first_weight,
         second_weight,
     )
-    last_rows = (local + 1) * chunk
+    last_rows = (2 * local + 1) * chunk
     slot_sums, held_grads = lax.optimization_barrier((exchange(part, DP), grads_late))
     sent_grads = section_ring(held_grads, -1)
     dinput, outs_early, finals = run(
         back_early_kernel,
-        [token_block, ((chunk, LANES), F32), ((group, last_rows, LANES), BF)],
-        back_scratch + [((group, local * chunk, LANES), F32)],
+        [token_block, ((chunk, LANES), F32), ((plane, last_rows, LANES), BF)],
+        back_scratch + [((plane, 2 * local * chunk, LANES), F32)],
         600000000,
         13,
         slot_scale,
@@ -662,25 +673,16 @@
         router_late,
         gain_late,
     )
-    router_grad, gain_total, slot_out, slot_grad = run(
-        final_kernel,
-        [((local, width), BF), ((1, width), F32), ((2, width), BF), ((2, width), BF)],
-        [],
-        1000000,
-        5,
-        exchange(finals, DP),
-        weights,
-        packed,
-        outs_late,
-        outs_early,
-    )
-
+    half_rows = (((local + 1) * chunk, LANES), F32)
+    kept_sums, given_sums = run(
+        plane_kernel, [half_rows, half_rows], [], 1000000, 2, flags, exchange(finals, PLANE)
+    )
     (
-        dinput, slot_early, slot_late, pre_grad_early, pre_grad_late, act_early, act_late,
+        given_sums, dinput, slot_early, slot_late, pre_grad_early, pre_grad_late, act_early, act_late,
         mixed_early_all, mixed_late, grads_late,
     ) = lax.optimization_barrier(
         (
-            dinput, slot_early, slot_late, pre_grad_early, pre_grad_late, act_early, act_late,
+            given_sums, dinput, slot_early, slot_late, pre_grad_early, pre_grad_late, act_early, act_late,
             mixed_early_all, mixed_late, grads_late,
         )
     )
@@ -698,12 +700,32 @@
         0,
         0,
     )
+    taken_sums, section_grads, first_grad, second_grad = lax.optimization_barrier(
+        (
+            other_half(given_sums), jnp.stack([grads_early, grads_late]), first_grad.astype(BF),
+            second_grad.astype(BF),
+        )
+    )
+    router_grad, gain_total, slot_out, slot_grad = run(
+        final_kernel,
+        [((local, width), BF), ((1, width), F32), ((2, width), BF), ((2, width), BF)],
+        [],
+        1000000,
+        6,
+        kept_sums,
+        taken_sums,
+        weights,
+        packed,
+        outs_late,
+        outs_early,
+    )
+
     return (
-        jnp.stack([grads_early, grads_late])[None, :, None],
+        section_grads[None, :, None],
         slot_out[None, :, None],
         slot_grad[None, :, None],
-        first_grad.astype(BF)[None],
-        second_grad.astype(BF)[None],
+        first_grad[None],
+        second_grad[None],
         router_grad.T[None],
         gain_total,
     )

time: 189 us -> 184 us (0.974); the launches traced: 188 us -> 180 us
  blocking collectives: 122 us -> 136 us
  waiting for transfers between devices: 19.9 us -> 6.51 us
  local copies, waits for them, and re-layouts: 5.24 us -> 0.76 us
  Pallas kernels: 21.9 us -> 19.8 us
    all_to_all x7 -> x8, blocking collectives: 122 us -> 136 us  [exchange(): return lax.all_to_all(chunks, axes, 0, 0, tiled=True)]
    ppermute x4, waiting for transfers between devices: 14.7 us -> 4.37 us  [section_ring(): lax.ppermute(block, 'section', [(i, (i + distance) % sections) for i in r...]
    all_to_all x1 -> x0, waiting for transfers between devices: 5.15 us -> none  [exchange(): return lax.all_to_all(chunks, axes, 0, 0, tiled=True)]
    unnamed x26 -> x16, local copies, waits for them, and re-layouts: 5.24 us -> 0.76 us
    all_to_all x1 -> x0, starting transfers between devices: 3.9 us -> none  [exchange(): return lax.all_to_all(chunks, axes, 0, 0, tiled=True)]
    unnamed x1 -> x0, other arithmetic: 2.74 us -> none
    ppermute x1 -> x2, waiting for transfers between devices: 0.01 us -> 2.14 us  [other_half(): return lax.ppermute(block, 'zh', [(0, 1), (1, 0)])]
    pallas_call x13 -> x14, Pallas kernels: 21.9 us -> 19.8 us  [run(): pl.pallas_call(body, out_shape=[jax.ShapeDtypeStruct(item[0], item[1]) fo...]
  transfers between devices with their start and end apart: 6 -> 6, of which waited for: 4 -> 3; matrix products, arithmetic and copies ran while one was open for 4% -> 4% of each run, Pallas kernels for 5% -> 4%
where the time goes in v7:
time: 184 us; the launch traced here: 180 us
  blocking collectives  136 us (74%)
  Pallas kernels  19.8 us (11%)
  starting transfers between devices  9.02 us (5%)
  waiting for transfers between devices  6.51 us (4%)
  other arithmetic  3.92 us (2%)
  matrix products  2.87 us (2%)
    all_to_all x8, blocking collectives, exchange(): return lax.all_to_all(chunks, axes, 0, 0, tiled=True)  136 us
    pallas_call x14, Pallas kernels, run(): pl.pallas_call(body, out_shape=[jax.ShapeDtypeStruct(item[0], item[1]) fo...  19.8 us
    ppermute x2, starting transfers between devices, other_half(): return lax.ppermute(block, 'zh', [(0, 1), (1, 0)])  7.27 us
    ppermute x4, waiting for transfers between devices, section_ring(): lax.ppermute(block, 'section', [(i, (i + distance) % sections) for i in r...  4.37 us
  transfers between devices with their start and end apart: 6, of which 3 were waited for; matrix products, arithmetic and copies ran while one was open for 4% of the time, Pallas kernels for 4%

profile of v7, /device:TPU:32, one launch (start us, length us, event | category | flops | bytes accessed | tf_op | source)
XLA Modules:
  0.0 180.5 jit_solution(16756642475285250813)
XLA Ops:
  0.6 0.0 copy-start.5
  0.7 0.7 copy-done.5
  1.4 0.1 shard_map.144.own_ref
  1.5 6.4 %collective-permute-start.1 = (bf16[64,128]{1,0:T(8,128)(2,1)S(1)}, bf16[64,128]{1,0:T(8,128)(2,1)S(1)}, u32[]{:S(2)}, u32[]{:S(2)}) collective-permute-start(bf16[64,128]{1,0:T(8,128)(2,1)S(1)} %shard_map.144.own_ref), channel_id=1, source_target_pairs={{0,16},{16,0},{1,17},{17,1},{2,18},{18,2},{3,19},{19,3},{4,20},{20... | collective-permute-start | bytes 49160 | tf_op jit(solution)/shard_map/ppermute | solution.py:40
  7.9 1.7 select_bitcast_fusion.in_ref
  9.5 0.1 collective-permute-start
  9.6 0.1 add_convert_fusion.1.flags_ref
  10.4 0.0 copy-done.4
  10.4 0.0 copy-start.1
  10.4 0.0 copy-start.2
  10.4 1.1 shard_map.145
  11.5 0.0 collective-permute-done.1.other_ref
  11.5 0.6 shard_map.146
  12.1 19.9 %all_to_all.40.chunks_ref = bf16[16,128,128]{2,1,0:T(8,128)(2,1)S(1)} all-to-all(bf16[16,128,128]{2,1,0:T(8,128)(2,1)S(1)} %shard_map.146), channel_id=1, replica_groups=mesh['section'=8,'zh'=2,'y'=4,'x'=4] {'y','x'}, dimensions={0} | all-to-all | bytes 1048576 | tf_op jit(solution)/shard_map/all_to_all | solution.py:30
  32.0 1.3 shard_map.147
  33.3 16.6 %all_to_all.41.slots_ref = bf16[32,16,128]{2,1,0:T(8,128)(2,1)S(1)} all-to-all(bf16[32,16,128]{2,1,0:T(8,128)(2,1)S(1)} %get-tuple-element.75), channel_id=1, replica_groups=mesh['section'=8,'zh'=2,'y'=4,'x'=4] {'zh','y','x'}, dimensions={0} | all-to-all | bytes 262144 | tf_op jit(solution)/shard_map/all_to_all | solution.py:30
  49.8 0.8 shard_map.148
  50.7 0.0 copy-start
  50.7 0.0 copy-start.3
  50.7 16.3 %all_to_all.42.sums_ref = bf16[32,16,128]{2,1,0:T(8,128)(2,1)S(1)} all-to-all(bf16[32,16,128]{2,1,0:T(8,128)(2,1)S(1)} %get-tuple-element.76), channel_id=1, replica_groups=mesh['section'=8,'zh'=2,'y'=4,'x'=4] {'zh','y','x'}, dimensions={0} | all-to-all | bytes 262144 | tf_op jit(solution)/shard_map/all_to_all | solution.py:30
  67.0 0.1 collective-permute-start.2
  67.1 0.0 collective-permute-done
  67.1 0.1 bitcast_select_fusion.1.base_ref
  67.2 3.0 %collective-permute-done.2.moved_ref = f32[24,128]{1,0:T(8,128)S(1)} collective-permute-done((f32[24,128]{1,0:T(8,128)S(1)}, f32[24,128]{1,0:T(8,128)S(1)}, u32[]{:S(2)}, u32[]{:S(2)}) %collective-permute-start.2) | collective-permute-done | bytes 12320 | tf_op jit(solution)/shard_map/ppermute | solution.py:45
  70.2 3.6 %shard_map.150 = (bf16[32,32,128]{2,1,0:T(8,128)(2,1)S(1)}, bf16[256,2048]{1,0:T(8,128)(2,1)S(1)}, bf16[256,2048]{1,0:T(8,128)(2,1)S(1)}, f32[256,128]{1,0:T(8,1...) custom-call(f32[1]{0:T(128)S(6)} %copy.17.scale_ref, ...), custom_call_target="tpu_custom_call" | custom-call | flops 400000000 | bytes 4000000 | tf_op jit(solution)/shard_map/pallas_call | solution.py:54
  73.8 18.6 %all_to_all.43.pairs_ref = bf16[32,32,128]{2,1,0:T(8,128)(2,1)S(1)} all-to-all(bf16[32,32,128]{2,1,0:T(8,128)(2,1)S(1)} %get-tuple-element.79), channel_id=1, replica_groups=mesh['section'=8,'zh'=2,'y'=4,'x'=4] {'zh','y','x'}, dimensions={0} | all-to-all | bytes 524288 | tf_op jit(solution)/shard_map/all_to_all | solution.py:30
  92.5 1.2 shard_map.151
  93.7 16.8 %all_to_all.44.sums_ref = bf16[32,32,128]{2,1,0:T(8,128)(2,1)S(1)} all-to-all(bf16[32,32,128]{2,1,0:T(8,128)(2,1)S(1)} %get-tuple-element.80), channel_id=1, replica_groups=mesh['section'=8,'zh'=2,'y'=4,'x'=4] {'zh','y','x'}, dimensions={0} | all-to-all | bytes 524288 | tf_op jit(solution)/shard_map/all_to_all | solution.py:30
  110.4 4.4 %shard_map.152 = (bf16[256,2048]{1,0:T(8,128)(2,1)S(1)}, f32[24,128]{1,0:T(8,128)S(1)}, f32[24,128]{1,0:T(8,128)S(1)}, f32[32,128]{1,0:T(8,128)S(1)}, f32[128,2048]{1,0:T(8,128)S(1)}, /*index=5*/f32[8,2048]{1,0:T(8,128)S(1)}) custom-call(f32[1]{0:T(128)S(6)} %copy.17.scale_ref, s32[3]{0:T(128)S(1)} %add_convert_fusion.1.flags_ref, ...), custom_call_target="tpu_custom_call" | custom-call | flops 600000000 | bytes 4000000 | tf_op jit(solution)/shard_map/pallas_call | solution.py:54
  114.8 0.3 collective-permute-start.3
  115.1 1.4 collective-permute-done.3.moved_ref
  116.5 0.6 shard_map.153
  117.1 16.9 %all_to_all.45.mixed_in_ref = bf16[32,16,128]{2,1,0:T(8,128)(2,1)S(1)} all-to-all(bf16[32,16,128]{2,1,0:T(8,128)(2,1)S(1)} %get-tuple-element.90), channel_id=1, replica_groups=mesh['section'=8,'zh'=2,'y'=4,'x'=4] {'zh','y','x'}, dimensions={0} | all-to-all | bytes 262144 | tf_op jit(solution)/shard_map/all_to_all | solution.py:30
  134.0 1.3 shard_map.154
  135.3 16.0 %all_to_all.46.sums_ref = bf16[32,16,128]{2,1,0:T(8,128)(2,1)S(1)} all-to-all(bf16[32,16,128]{2,1,0:T(8,128)(2,1)S(1)} %get-tuple-element.92), channel_id=1, replica_groups=mesh['section'=8,'zh'=2,'y'=4,'x'=4] {'zh','y','x'}, dimensions={0} | all-to-all | bytes 262144 | tf_op jit(solution)/shard_map/all_to_all | solution.py:30
  151.4 1.3 collective-permute-start.5
  152.7 3.5 %shard_map.155 = (bf16[256,2048]{1,0:T(8,128)(2,1)S(1)}, f32[16,128]{1,0:T(8,128)S(1)}, bf16[16,144,128]{2,1,0:T(8,128)(2,1)S(1)}) custom-call(f32[1]{0:T(128)S(6)} %copy.17.scale_ref, bf16[32,16,128]{2,1,0:T(8,128)(2,1)S(1)} %all_to_all.46.sums_ref, f32[24,128]{1,0:T(8,128)S(1)} %get-tuple-element.95.kept_ref, ...), custom_call_target="tpu_custom_call" | custom-call | flops 600000000 | bytes 4000000 | tf_op jit(solution)/shard_map/pallas_call | solution.py:54
  156.2 14.9 %all_to_all.47.chunks_ref = bf16[16,144,128]{2,1,0:T(8,128)(2,1)S(1)} all-to-all(bf16[16,144,128]{2,1,0:T(8,128)(2,1)S(1)} %get-tuple-element.101), channel_id=1, replica_groups=mesh['section'=8,'zh'=2,'y'=4,'x'=4] {'y','x'}, dimensions={0} | all-to-all | bytes 1179648 | tf_op jit(solution)/shard_map/all_to_all | solution.py:30
  171.1 0.6 shard_map.156
  171.7 0.9 collective-permute-start.4
  172.6 1.4 convolution_convert_fusion.1
  174.1 1.4 convolution_convert_fusion
  175.5 0.0 collective-permute-done.5
  175.5 0.6 fusion
  176.1 0.0 copy-start.6
  176.1 1.5 pad_maximum_fusion
  177.6 2.1 %collective-permute-done.4.taken_ref = f32[80,128]{1,0:T(8,128)S(1)} collective-permute-done((f32[80,128]{1,0:T(8,128)S(1)}, f32[80,128]{1,0:T(8,128)S(1)}, u32[]{:S(2)}, u32[]{:S(2)}) %collective-permute-start.4) | collective-permute-done | bytes 40992 | tf_op jit(solution)/shard_map/ppermute | solution.py:40
  179.7 0.7 shard_map.157
  (9 shorter events, 0.1 us)
Async XLA Ops:
  0.6 9.7 %copy-start.4 = (f32[1,2048]{1,0:T(1,128)S(1)}, f32[1,2048]{1,0:T(1,128)}, u32[]{:S(2)}) copy-start(f32[1,2048]{1,0:T(1,128)} %gain_ref.7) | copy-start | bytes 24580
  0.6 0.7 copy-start.5
  1.5 10.0 %collective-permute-start.1 = (bf16[64,128]{1,0:T(8,128)(2,1)S(1)}, bf16[64,128]{1,0:T(8,128)(2,1)S(1)}, u32[]{:S(2)}, u32[]{:S(2)}) collective-permute-start(bf16[64,128]{1,0:T(8,128)(2,1)S(1)} %shard_map.144.own_ref), channel_id=1, source_target_pairs={{0,16},{16,0},{1,17},{17,1},{2,18},{18,2},{3,19},{19,3},{4,20},{20... | collective-permute-start | bytes 49160 | tf_op jit(solution)/shard_map/ppermute | solution.py:40
  9.5 57.6 %collective-permute-start = (bf16[256,2048]{1,0:T(8,128)(2,1)S(1)}, bf16[256,2048]{1,0:T(8,128)(2,1)S(1)}, u32[]{:S(2)}, u32[]{:S(2)}) collective-permute-start(bf16[256,2048]{1,0:T(8,128)(2,1)S(1)} %select_bitcast_fusion.in_ref), channel_id=1, source_target_pairs={{0,32},{32,64},{64,96},{96,128},{128,160},{160,192},{192,224},{224... | collective-permute-start | bytes 3145736 | tf_op jit(solution)/shard_map/ppermute | solution.py:45
  10.4 39.5 %copy-start.1 = (bf16[1,2048,256]{2,1,0:T(8,128)(2,1)S(1)}, bf16[1,2048,256]{2,1,0:T(8,128)(2,1)}, u32[]{:S(2)}) copy-start(bf16[1,2048,256]{2,1,0:T(8,128)(2,1)} %param.16) | copy-start | bytes 3145732
  10.4 39.5 %copy-start.2 = (bf16[1,256,2048]{2,1,0:T(8,128)(2,1)S(1)}, bf16[1,256,2048]{2,1,0:T(8,128)(2,1)}, u32[]{:S(2)}) copy-start(bf16[1,256,2048]{2,1,0:T(8,128)(2,1)} %param.17) | copy-start | bytes 3145732
  32.0 35.1 %copy-start.7 = (bf16[2,1,256,2048]{3,2,1,0:T(8,128)(2,1)S(1)}, bf16[2,1,256,2048]{3,2,1,0:T(8,128)(2,1)}, u32[]{:S(2)}) copy-start(bf16[2,1,256,2048]{3,2,1,0:T(8,128)(2,1)} %param.9) | copy-start | bytes 6291460
  50.7 19.5 %copy-start = (bf16[2,1,256,2048]{3,2,1,0:T(8,128)(2,1)S(1)}, bf16[2,1,256,2048]{3,2,1,0:T(8,128)(2,1)}, u32[]{:S(2)}) copy-start(bf16[2,1,256,2048]{3,2,1,0:T(8,128)(2,1)} %cotangent_ref.3) | copy-start | bytes 6291460
  50.7 19.5 %copy-start.3 = (bf16[1,1,256,2048]{3,2,1,0:T(8,128)(2,1)S(1)}, bf16[1,1,256,2048]{3,2,1,0:T(8,128)(2,1)}, u32[]{:S(2)}) copy-start(bf16[1,1,256,2048]{3,2,1,0:T(8,128)(2,1)} %backflow_ref.1) | copy-start | bytes 3145732
  67.0 3.2 %collective-permute-start.2 = (f32[24,128]{1,0:T(8,128)S(1)}, f32[24,128]{1,0:T(8,128)S(1)}, u32[]{:S(2)}, u32[]{:S(2)}) collective-permute-start(f32[24,128]{1,0:T(8,128)S(1)} %shard_map.149.packed_ref), channel_id=1, source_target_pairs={{0,32},{32,64},{64,96},{96,128},{128,160},{160,192},{192,224},{224... | collective-permute-start | bytes 36872 | tf_op jit(solution)/shard_map/ppermute | solution.py:45
  114.8 1.7 collective-permute-start.3
  151.4 24.1 %collective-permute-start.5 = (bf16[256,2048]{1,0:T(8,128)(2,1)S(1)}, bf16[256,2048]{1,0:T(8,128)(2,1)S(1)}, u32[]{:S(2)}, u32[]{:S(2)}) collective-permute-start(bf16[256,2048]{1,0:T(8,128)(2,1)S(1)} %get-tuple-element.113), channel_id=1, source_target_pairs={{0,224},{32,0},{64,32},{96,64},{128,96},{160,128},{192,160},{224,1... | collective-permute-start | bytes 3145736 | tf_op jit(solution)/shard_map/ppermute | solution.py:45
  171.7 8.0 %collective-permute-start.4 = (f32[80,128]{1,0:T(8,128)S(1)}, f32[80,128]{1,0:T(8,128)S(1)}, u32[]{:S(2)}, u32[]{:S(2)}) collective-permute-start(f32[80,128]{1,0:T(8,128)S(1)} %get-tuple-element.112), channel_id=1, source_target_pairs={{0,16},{16,0},{1,17},{17,1},{2,18},{18,2},{3,19},{19,3},{4,20},{20... | collective-permute-start | bytes 122888 | tf_op jit(solution)/shard_map/ppermute | solution.py:40
  176.1 3.7 %copy-start.6 = (bf16[1,2048,4]{1,2,0:T(4,128)(2,1)S(1)}, bf16[1,2048,4]{1,2,0:T(4,128)(2,1)}, u32[]{:S(2)}) copy-start(bf16[1,2048,4]{1,2,0:T(4,128)(2,1)} %param.15) | copy-start | bytes 49156

commit v8 on v7

--- a/solution.py
+++ b/solution.py
@@ -116,7 +116,7 @@
 
 
 def passes(ref, body):
-    @pl.loop(0, ref.shape[0] // STEP, unroll=8)
+    @pl.loop(0, ref.shape[0] // STEP, unroll=16)
     def _(index):
         body(pl.ds(index * STEP, STEP))
 
@@ -369,7 +369,7 @@
         return total + product[:8] + product[8:]
 
     gain_sum = lax.fori_loop(
-        0, in_ref.shape[0] // STEP, product_rows, jnp.zeros((8, in_ref.shape[1]), F32), unroll=4
+        0, in_ref.shape[0] // STEP, product_rows, jnp.zeros((8, in_ref.shape[1]), F32), unroll=8
     )
     mean = jnp.sum(mean_ref[...], axis=1, keepdims=True) * (1.0 / in_ref.shape[1])
     mean_ref[...] = jnp.broadcast_to(mean * inverse_ref[...], mean_ref.shape)
@@ -578,7 +578,7 @@
     packed = run(
         pack_kernel, [((chunk + 8, LANES), F32)], [], 1000000, 2, exchange(part, DP), rows_early
     )[0]
-    moved = section_ring(packed, 1)
+    moved = section_shift(packed, 1)
 
     base = jnp.where(is_first, tokens[1, 0], sent_in)
     (

time: 184 us -> 183 us (level); the launches traced: 180 us -> 183 us
  blocking collectives: 136 us -> 139 us
    all_to_all x8, blocking collectives: 136 us -> 139 us  [exchange(): return lax.all_to_all(chunks, axes, 0, 0, tiled=True)]
    ppermute x4 -> x3, waiting for transfers between devices: 4.37 us -> 1.4 us  [section_ring(): lax.ppermute(block, 'section', [(i, (i + distance) % sections) for i in r...]
    ppermute x0 -> x1, waiting for transfers between devices: none -> 2.95 us  [section_shift(): return lax.ppermute(block, 'section', route)]
    ppermute x0 -> x1, starting transfers between devices: none -> 1.91 us  [section_shift(): return lax.ppermute(block, 'section', route)]
where the time goes in v8:
time: 183 us
  blocking collectives  139 us (76%)
  Pallas kernels  18.6 us (10%)
  starting transfers between devices  9.1 us (5%)
  waiting for transfers between devices  6.74 us (4%)
  other arithmetic  3.92 us (2%)
  matrix products  2.87 us (2%)
    all_to_all x8, blocking collectives, exchange(): return lax.all_to_all(chunks, axes, 0, 0, tiled=True)  139 us
    pallas_call x14, Pallas kernels, run(): pl.pallas_call(body, out_shape=[jax.ShapeDtypeStruct(item[0], item[1]) fo...  18.6 us
    ppermute x2, starting transfers between devices, other_half(): return lax.ppermute(block, 'zh', [(0, 1), (1, 0)])  7.02 us
  transfers between devices with their start and end apart: 6, of which 3 were waited for; matrix products, arithmetic and copies ran while one was open for 4% of the time, Pallas kernels for 4%

profile of v8, /device:TPU:32, one launch (start us, length us, event | category | flops | bytes accessed | tf_op | source)
XLA Modules:
  0.0 182.7 jit_solution(7380073030713708327)
XLA Ops:
  0.6 0.0 copy-start.5
  0.7 0.7 copy-done.5
  1.4 0.1 shard_map.144.own_ref
  1.5 6.4 %collective-permute-start.1 = (bf16[64,128]{1,0:T(8,128)(2,1)S(1)}, bf16[64,128]{1,0:T(8,128)(2,1)S(1)}, u32[]{:S(2)}, u32[]{:S(2)}) collective-permute-start(bf16[64,128]{1,0:T(8,128)(2,1)S(1)} %shard_map.144.own_ref), channel_id=1, source_target_pairs={{0,16},{16,0},{1,17},{17,1},{2,18},{18,2},{3,19},{19,3},{4,20},{20... | collective-permute-start | bytes 49160 | tf_op jit(solution)/shard_map/ppermute | solution.py:40
  7.9 1.7 select_bitcast_fusion.in_ref
  9.5 0.1 collective-permute-start
  9.6 0.1 add_convert_fusion.1.flags_ref
  10.4 0.0 copy-done.4
  10.4 0.0 copy-start.1
  10.4 0.0 copy-start.2
  10.4 0.8 shard_map.145
  11.2 0.0 collective-permute-done.1.other_ref
  11.3 0.6 shard_map.146
  11.9 19.9 %all_to_all.40.chunks_ref = bf16[16,128,128]{2,1,0:T(8,128)(2,1)S(1)} all-to-all(bf16[16,128,128]{2,1,0:T(8,128)(2,1)S(1)} %shard_map.146), channel_id=1, replica_groups=mesh['section'=8,'zh'=2,'y'=4,'x'=4] {'y','x'}, dimensions={0} | all-to-all | bytes 1048576 | tf_op jit(solution)/shard_map/all_to_all | solution.py:30
  31.8 1.3 shard_map.147
  33.0 16.8 %all_to_all.41.slots_ref = bf16[32,16,128]{2,1,0:T(8,128)(2,1)S(1)} all-to-all(bf16[32,16,128]{2,1,0:T(8,128)(2,1)S(1)} %get-tuple-element.75), channel_id=1, replica_groups=mesh['section'=8,'zh'=2,'y'=4,'x'=4] {'zh','y','x'}, dimensions={0} | all-to-all | bytes 262144 | tf_op jit(solution)/shard_map/all_to_all | solution.py:30
  49.8 0.8 shard_map.148
  50.7 0.0 copy-start
  50.7 0.0 copy-start.3
  50.7 16.3 %all_to_all.42.sums_ref = bf16[32,16,128]{2,1,0:T(8,128)(2,1)S(1)} all-to-all(bf16[32,16,128]{2,1,0:T(8,128)(2,1)S(1)} %get-tuple-element.76), channel_id=1, replica_groups=mesh['section'=8,'zh'=2,'y'=4,'x'=4] {'zh','y','x'}, dimensions={0} | all-to-all | bytes 262144 | tf_op jit(solution)/shard_map/all_to_all | solution.py:30
  67.0 1.9 %collective-permute-start.2 = (f32[24,128]{1,0:T(8,128)S(1)}, f32[24,128]{1,0:T(8,128)S(1)}, u32[]{:S(2)}, u32[]{:S(2)}) collective-permute-start(f32[24,128]{1,0:T(8,128)S(1)} %shard_map.149.packed_ref), channel_id=1, source_target_pairs={{0,32},{32,64},{64,96},{96,128},{128,160},{160,192},{192,224},{1,3... | collective-permute-start | bytes 36872 | tf_op jit(solution)/shard_map/ppermute | solution.py:36
  68.9 0.0 collective-permute-done
  69.0 0.1 bitcast_select_fusion.1.base_ref
  69.1 2.9 %collective-permute-done.2.moved_ref = f32[24,128]{1,0:T(8,128)S(1)} collective-permute-done((f32[24,128]{1,0:T(8,128)S(1)}, f32[24,128]{1,0:T(8,128)S(1)}, u32[]{:S(2)}, u32[]{:S(2)}) %collective-permute-start.2) | collective-permute-done | bytes 12320 | tf_op jit(solution)/shard_map/ppermute | solution.py:36
  72.0 3.2 %shard_map.150 = (bf16[32,32,128]{2,1,0:T(8,128)(2,1)S(1)}, bf16[256,2048]{1,0:T(8,128)(2,1)S(1)}, bf16[256,2048]{1,0:T(8,128)(2,1)S(1)}, f32[256,128]{1,0:T(8,1...) custom-call(f32[1]{0:T(128)S(6)} %copy.17.scale_ref, ...), custom_call_target="tpu_custom_call" | custom-call | flops 400000000 | bytes 4000000 | tf_op jit(solution)/shard_map/pallas_call | solution.py:54
  75.3 17.0 %all_to_all.43.pairs_ref = bf16[32,32,128]{2,1,0:T(8,128)(2,1)S(1)} all-to-all(bf16[32,32,128]{2,1,0:T(8,128)(2,1)S(1)} %get-tuple-element.79), channel_id=1, replica_groups=mesh['section'=8,'zh'=2,'y'=4,'x'=4] {'zh','y','x'}, dimensions={0} | all-to-all | bytes 524288 | tf_op jit(solution)/shard_map/all_to_all | solution.py:30
  92.3 1.2 shard_map.151
  93.5 18.8 %all_to_all.44.sums_ref = bf16[32,32,128]{2,1,0:T(8,128)(2,1)S(1)} all-to-all(bf16[32,32,128]{2,1,0:T(8,128)(2,1)S(1)} %get-tuple-element.80), channel_id=1, replica_groups=mesh['section'=8,'zh'=2,'y'=4,'x'=4] {'zh','y','x'}, dimensions={0} | all-to-all | bytes 524288 | tf_op jit(solution)/shard_map/all_to_all | solution.py:30
  112.4 4.1 %shard_map.152 = (bf16[256,2048]{1,0:T(8,128)(2,1)S(1)}, f32[24,128]{1,0:T(8,128)S(1)}, f32[24,128]{1,0:T(8,128)S(1)}, f32[32,128]{1,0:T(8,128)S(1)}, f32[128,2048]{1,0:T(8,128)S(1)}, /*index=5*/f32[8,2048]{1,0:T(8,128)S(1)}) custom-call(f32[1]{0:T(128)S(6)} %copy.17.scale_ref, s32[3]{0:T(128)S(1)} %add_convert_fusion.1.flags_ref, ...), custom_call_target="tpu_custom_call" | custom-call | flops 600000000 | bytes 4000000 | tf_op jit(solution)/shard_map/pallas_call | solution.py:54
  116.4 0.1 collective-permute-start.3
  116.5 1.4 collective-permute-done.3.moved_ref
  117.9 0.6 shard_map.153
  118.5 17.8 %all_to_all.45.mixed_in_ref = bf16[32,16,128]{2,1,0:T(8,128)(2,1)S(1)} all-to-all(bf16[32,16,128]{2,1,0:T(8,128)(2,1)S(1)} %get-tuple-element.90), channel_id=1, replica_groups=mesh['section'=8,'zh'=2,'y'=4,'x'=4] {'zh','y','x'}, dimensions={0} | all-to-all | bytes 262144 | tf_op jit(solution)/shard_map/all_to_all | solution.py:30
  136.3 1.3 shard_map.154
  137.6 16.3 %all_to_all.46.sums_ref = bf16[32,16,128]{2,1,0:T(8,128)(2,1)S(1)} all-to-all(bf16[32,16,128]{2,1,0:T(8,128)(2,1)S(1)} %get-tuple-element.92), channel_id=1, replica_groups=mesh['section'=8,'zh'=2,'y'=4,'x'=4] {'zh','y','x'}, dimensions={0} | all-to-all | bytes 262144 | tf_op jit(solution)/shard_map/all_to_all | solution.py:30
  154.0 0.0 collective-permute-start.5
  154.0 3.2 %shard_map.155 = (bf16[256,2048]{1,0:T(8,128)(2,1)S(1)}, f32[16,128]{1,0:T(8,128)S(1)}, bf16[16,144,128]{2,1,0:T(8,128)(2,1)S(1)}) custom-call(f32[1]{0:T(128)S(6)} %copy.17.scale_ref, bf16[32,16,128]{2,1,0:T(8,128)(2,1)S(1)} %all_to_all.46.sums_ref, f32[24,128]{1,0:T(8,128)S(1)} %get-tuple-element.95.kept_ref, ...), custom_call_target="tpu_custom_call" | custom-call | flops 600000000 | bytes 4000000 | tf_op jit(solution)/shard_map/pallas_call | solution.py:54
  157.1 16.2 %all_to_all.47.chunks_ref = bf16[16,144,128]{2,1,0:T(8,128)(2,1)S(1)} all-to-all(bf16[16,144,128]{2,1,0:T(8,128)(2,1)S(1)} %get-tuple-element.101), channel_id=1, replica_groups=mesh['section'=8,'zh'=2,'y'=4,'x'=4] {'y','x'}, dimensions={0} | all-to-all | bytes 1179648 | tf_op jit(solution)/shard_map/all_to_all | solution.py:30
  173.3 0.6 shard_map.156
  174.0 0.6 collective-permute-start.4
  174.6 1.4 convolution_convert_fusion.1
  176.1 1.4 convolution_convert_fusion
  177.5 0.0 collective-permute-done.5
  177.5 0.6 fusion
  178.1 0.0 copy-start.6
  178.1 1.5 pad_maximum_fusion
  179.6 2.4 %collective-permute-done.4.taken_ref = f32[80,128]{1,0:T(8,128)S(1)} collective-permute-done((f32[80,128]{1,0:T(8,128)S(1)}, f32[80,128]{1,0:T(8,128)S(1)}, u32[]{:S(2)}, u32[]{:S(2)}) %collective-permute-start.4) | collective-permute-done | bytes 40992 | tf_op jit(solution)/shard_map/ppermute | solution.py:40
  182.0 0.7 shard_map.157
  (9 shorter events, 0.1 us)
Async XLA Ops:
  0.6 9.7 %copy-start.4 = (f32[1,2048]{1,0:T(1,128)S(1)}, f32[1,2048]{1,0:T(1,128)}, u32[]{:S(2)}) copy-start(f32[1,2048]{1,0:T(1,128)} %gain_ref.7) | copy-start | bytes 24580
  0.6 0.7 copy-start.5
  1.5 9.8 %collective-permute-start.1 = (bf16[64,128]{1,0:T(8,128)(2,1)S(1)}, bf16[64,128]{1,0:T(8,128)(2,1)S(1)}, u32[]{:S(2)}, u32[]{:S(2)}) collective-permute-start(bf16[64,128]{1,0:T(8,128)(2,1)S(1)} %shard_map.144.own_ref), channel_id=1, source_target_pairs={{0,16},{16,0},{1,17},{17,1},{2,18},{18,2},{3,19},{19,3},{4,20},{20... | collective-permute-start | bytes 49160 | tf_op jit(solution)/shard_map/ppermute | solution.py:40
  9.5 59.4 %collective-permute-start = (bf16[256,2048]{1,0:T(8,128)(2,1)S(1)}, bf16[256,2048]{1,0:T(8,128)(2,1)S(1)}, u32[]{:S(2)}, u32[]{:S(2)}) collective-permute-start(bf16[256,2048]{1,0:T(8,128)(2,1)S(1)} %select_bitcast_fusion.in_ref), channel_id=1, source_target_pairs={{0,32},{32,64},{64,96},{96,128},{128,160},{160,192},{192,224},{224... | collective-permute-start | bytes 3145736 | tf_op jit(solution)/shard_map/ppermute | solution.py:45
  10.4 39.5 %copy-start.1 = (bf16[1,2048,256]{2,1,0:T(8,128)(2,1)S(1)}, bf16[1,2048,256]{2,1,0:T(8,128)(2,1)}, u32[]{:S(2)}) copy-start(bf16[1,2048,256]{2,1,0:T(8,128)(2,1)} %param.16) | copy-start | bytes 3145732
  10.4 39.5 %copy-start.2 = (bf16[1,256,2048]{2,1,0:T(8,128)(2,1)S(1)}, bf16[1,256,2048]{2,1,0:T(8,128)(2,1)}, u32[]{:S(2)}) copy-start(bf16[1,256,2048]{2,1,0:T(8,128)(2,1)} %param.17) | copy-start | bytes 3145732
  31.8 37.2 %copy-start.7 = (bf16[2,1,256,2048]{3,2,1,0:T(8,128)(2,1)S(1)}, bf16[2,1,256,2048]{3,2,1,0:T(8,128)(2,1)}, u32[]{:S(2)}) copy-start(bf16[2,1,256,2048]{3,2,1,0:T(8,128)(2,1)} %param.9) | copy-start | bytes 6291460
  50.7 21.4 %copy-start = (bf16[2,1,256,2048]{3,2,1,0:T(8,128)(2,1)S(1)}, bf16[2,1,256,2048]{3,2,1,0:T(8,128)(2,1)}, u32[]{:S(2)}) copy-start(bf16[2,1,256,2048]{3,2,1,0:T(8,128)(2,1)} %cotangent_ref.3) | copy-start | bytes 6291460
  50.7 21.3 %copy-start.3 = (bf16[1,1,256,2048]{3,2,1,0:T(8,128)(2,1)S(1)}, bf16[1,1,256,2048]{3,2,1,0:T(8,128)(2,1)}, u32[]{:S(2)}) copy-start(bf16[1,1,256,2048]{3,2,1,0:T(8,128)(2,1)} %backflow_ref.1) | copy-start | bytes 3145732
  67.0 5.0 %collective-permute-start.2 = (f32[24,128]{1,0:T(8,128)S(1)}, f32[24,128]{1,0:T(8,128)S(1)}, u32[]{:S(2)}, u32[]{:S(2)}) collective-permute-start(f32[24,128]{1,0:T(8,128)S(1)} %shard_map.149.packed_ref), channel_id=1, source_target_pairs={{0,32},{32,64},{64,96},{96,128},{128,160},{160,192},{192,224},{1,3... | collective-permute-start | bytes 36872 | tf_op jit(solution)/shard_map/ppermute | solution.py:36
  116.4 1.5 collective-permute-start.3
  154.0 23.5 %collective-permute-start.5 = (bf16[256,2048]{1,0:T(8,128)(2,1)S(1)}, bf16[256,2048]{1,0:T(8,128)(2,1)S(1)}, u32[]{:S(2)}, u32[]{:S(2)}) collective-permute-start(bf16[256,2048]{1,0:T(8,128)(2,1)S(1)} %get-tuple-element.113), channel_id=1, source_target_pairs={{0,224},{32,0},{64,32},{96,64},{128,96},{160,128},{192,160},{224,1... | collective-permute-start | bytes 3145736 | tf_op jit(solution)/shard_map/ppermute | solution.py:45
  174.0 8.0 %collective-permute-start.4 = (f32[80,128]{1,0:T(8,128)S(1)}, f32[80,128]{1,0:T(8,128)S(1)}, u32[]{:S(2)}, u32[]{:S(2)}) collective-permute-start(f32[80,128]{1,0:T(8,128)S(1)} %get-tuple-element.112), channel_id=1, source_target_pairs={{0,16},{16,0},{1,17},{17,1},{2,18},{18,2},{3,19},{19,3},{4,20},{20... | collective-permute-start | bytes 122888 | tf_op jit(solution)/shard_map/ppermute | solution.py:40
  178.1 3.9 %copy-start.6 = (bf16[1,2048,4]{1,2,0:T(4,128)(2,1)S(1)}, bf16[1,2048,4]{1,2,0:T(4,128)(2,1)}, u32[]{:S(2)}) copy-start(bf16[1,2048,4]{1,2,0:T(4,128)(2,1)} %param.15) | copy-start | bytes 49156

commit v9 on v8

--- a/solution.py
+++ b/solution.py
@@ -472,7 +472,8 @@
     low, high, gain = total[:count], total[count : 2 * count], total[2 * count :]
     upper = flags_ref[2] != 0
     kept_ref[...] = jnp.concatenate([jnp.where(upper, high, low), gain], axis=0)
-    given_ref[...] = jnp.concatenate([jnp.where(upper, low, high), gain], axis=0)
+    given = jnp.concatenate([jnp.where(upper, low, high), gain], axis=0)
+    given_ref[...] = given.astype(BF)
 
 
 def final_kernel(
@@ -480,7 +481,7 @@
     router_ref, gain_ref, slot_out_ref, slot_grad_ref,
 ):
     weights, inverse = scaled_weights(weights_ref)
-    total = kept_ref[...] + taken_ref[...]
+    total = kept_ref[...] + taken_ref[...].astype(F32)
     count = weights.shape[0]
     chunk = weights.shape[1] // LANES
     rows = [to_row(total[k * chunk : (k + 1) * chunk]) for k in range(count)]
@@ -675,7 +676,7 @@
     )
     half_rows = (((local + 1) * chunk, LANES), F32)
     kept_sums, given_sums = run(
-        plane_kernel, [half_rows, half_rows], [], 1000000, 2, flags, exchange(finals, PLANE)
+        plane_kernel, [half_rows, (half_rows[0], BF)], [], 1000000, 2, flags, exchange(finals, PLANE)
     )
     (
         given_sums, dinput, slot_early, slot_late, pre_grad_early, pre_grad_late, act_early, act_late,

time: 183 us -> 183 us (level)
  no operation moved by 1% of the time
where the time goes in v9:
time: 183 us; the launch traced here: 182 us
  blocking collectives  139 us (76%)
  Pallas kernels  18.6 us (10%)
  starting transfers between devices  9.1 us (5%)
  waiting for transfers between devices  6.52 us (4%)
  other arithmetic  3.92 us (2%)
  matrix products  2.87 us (2%)
    all_to_all x8, blocking collectives, exchange(): return lax.all_to_all(chunks, axes, 0, 0, tiled=True)  139 us
    pallas_call x14, Pallas kernels, run(): pl.pallas_call(body, out_shape=[jax.ShapeDtypeStruct(item[0], item[1]) fo...  18.6 us
    ppermute x2, starting transfers between devices, other_half(): return lax.ppermute(block, 'zh', [(0, 1), (1, 0)])  7.02 us
  transfers between devices with their start and end apart: 6, of which 3 were waited for; matrix products, arithmetic and copies ran while one was open for 4% of the time, Pallas kernels for 4%

profile of v9, /device:TPU:32, one launch (start us, length us, event | category | flops | bytes accessed | tf_op | source)
XLA Modules:
  0.0 182.5 jit_solution(12097339223698486711)
XLA Ops:
  0.6 0.0 copy-start.5
  0.7 0.7 copy-done.5
  1.4 0.1 shard_map.144.own_ref
  1.5 6.4 %collective-permute-start.1 = (bf16[64,128]{1,0:T(8,128)(2,1)S(1)}, bf16[64,128]{1,0:T(8,128)(2,1)S(1)}, u32[]{:S(2)}, u32[]{:S(2)}) collective-permute-start(bf16[64,128]{1,0:T(8,128)(2,1)S(1)} %shard_map.144.own_ref), channel_id=1, source_target_pairs={{0,16},{16,0},{1,17},{17,1},{2,18},{18,2},{3,19},{19,3},{4,20},{20... | collective-permute-start | bytes 49160 | tf_op jit(solution)/shard_map/ppermute | solution.py:40
  7.9 1.7 select_bitcast_fusion.in_ref
  9.5 0.1 collective-permute-start
  9.6 0.1 add_convert_fusion.1.flags_ref
  10.4 0.0 copy-start.1
  10.4 0.0 copy-start.2
  10.4 0.8 shard_map.145
  11.2 0.0 collective-permute-done.1.other_ref
  11.3 0.6 shard_map.146
  11.9 19.9 %all_to_all.40.chunks_ref = bf16[16,128,128]{2,1,0:T(8,128)(2,1)S(1)} all-to-all(bf16[16,128,128]{2,1,0:T(8,128)(2,1)S(1)} %shard_map.146), channel_id=1, replica_groups=mesh['section'=8,'zh'=2,'y'=4,'x'=4] {'y','x'}, dimensions={0} | all-to-all | bytes 1048576 | tf_op jit(solution)/shard_map/all_to_all | solution.py:30
  31.8 1.3 shard_map.147
  33.0 16.8 %all_to_all.41.slots_ref = bf16[32,16,128]{2,1,0:T(8,128)(2,1)S(1)} all-to-all(bf16[32,16,128]{2,1,0:T(8,128)(2,1)S(1)} %get-tuple-element.75), channel_id=1, replica_groups=mesh['section'=8,'zh'=2,'y'=4,'x'=4] {'zh','y','x'}, dimensions={0} | all-to-all | bytes 262144 | tf_op jit(solution)/shard_map/all_to_all | solution.py:30
  49.8 0.0 copy-done.1
  49.8 0.8 shard_map.148
  50.7 0.0 copy-start
  50.7 0.0 copy-start.3
  50.7 16.3 %all_to_all.42.sums_ref = bf16[32,16,128]{2,1,0:T(8,128)(2,1)S(1)} all-to-all(bf16[32,16,128]{2,1,0:T(8,128)(2,1)S(1)} %get-tuple-element.76), channel_id=1, replica_groups=mesh['section'=8,'zh'=2,'y'=4,'x'=4] {'zh','y','x'}, dimensions={0} | all-to-all | bytes 262144 | tf_op jit(solution)/shard_map/all_to_all | solution.py:30
  67.0 1.9 %collective-permute-start.2 = (f32[24,128]{1,0:T(8,128)S(1)}, f32[24,128]{1,0:T(8,128)S(1)}, u32[]{:S(2)}, u32[]{:S(2)}) collective-permute-start(f32[24,128]{1,0:T(8,128)S(1)} %shard_map.149.packed_ref), channel_id=1, source_target_pairs={{0,32},{32,64},{64,96},{96,128},{128,160},{160,192},{192,224},{1,3... | collective-permute-start | bytes 36872 | tf_op jit(solution)/shard_map/ppermute | solution.py:36
  68.9 0.0 collective-permute-done
  69.0 0.1 bitcast_select_fusion.1.base_ref
  69.1 2.9 %collective-permute-done.2.moved_ref = f32[24,128]{1,0:T(8,128)S(1)} collective-permute-done((f32[24,128]{1,0:T(8,128)S(1)}, f32[24,128]{1,0:T(8,128)S(1)}, u32[]{:S(2)}, u32[]{:S(2)}) %collective-permute-start.2) | collective-permute-done | bytes 12320 | tf_op jit(solution)/shard_map/ppermute | solution.py:36
  72.0 3.2 %shard_map.150 = (bf16[32,32,128]{2,1,0:T(8,128)(2,1)S(1)}, bf16[256,2048]{1,0:T(8,128)(2,1)S(1)}, bf16[256,2048]{1,0:T(8,128)(2,1)S(1)}, f32[256,128]{1,0:T(8,1...) custom-call(f32[1]{0:T(128)S(6)} %copy.17.scale_ref, ...), custom_call_target="tpu_custom_call" | custom-call | flops 400000000 | bytes 4000000 | tf_op jit(solution)/shard_map/pallas_call | solution.py:54
  75.3 17.0 %all_to_all.43.pairs_ref = bf16[32,32,128]{2,1,0:T(8,128)(2,1)S(1)} all-to-all(bf16[32,32,128]{2,1,0:T(8,128)(2,1)S(1)} %get-tuple-element.79), channel_id=1, replica_groups=mesh['section'=8,'zh'=2,'y'=4,'x'=4] {'zh','y','x'}, dimensions={0} | all-to-all | bytes 524288 | tf_op jit(solution)/shard_map/all_to_all | solution.py:30
  92.3 1.2 shard_map.151
  93.5 18.8 %all_to_all.44.sums_ref = bf16[32,32,128]{2,1,0:T(8,128)(2,1)S(1)} all-to-all(bf16[32,32,128]{2,1,0:T(8,128)(2,1)S(1)} %get-tuple-element.80), channel_id=1, replica_groups=mesh['section'=8,'zh'=2,'y'=4,'x'=4] {'zh','y','x'}, dimensions={0} | all-to-all | bytes 524288 | tf_op jit(solution)/shard_map/all_to_all | solution.py:30
  112.4 4.1 %shard_map.152 = (bf16[256,2048]{1,0:T(8,128)(2,1)S(1)}, f32[24,128]{1,0:T(8,128)S(1)}, f32[24,128]{1,0:T(8,128)S(1)}, f32[32,128]{1,0:T(8,128)S(1)}, f32[128,2048]{1,0:T(8,128)S(1)}, /*index=5*/f32[8,2048]{1,0:T(8,128)S(1)}) custom-call(f32[1]{0:T(128)S(6)} %copy.17.scale_ref, s32[3]{0:T(128)S(1)} %add_convert_fusion.1.flags_ref, ...), custom_call_target="tpu_custom_call" | custom-call | flops 600000000 | bytes 4000000 | tf_op jit(solution)/shard_map/pallas_call | solution.py:54
  116.4 0.1 collective-permute-start.3
  116.5 1.4 collective-permute-done.3.moved_ref
  117.9 0.6 shard_map.153
  118.5 17.8 %all_to_all.45.mixed_in_ref = bf16[32,16,128]{2,1,0:T(8,128)(2,1)S(1)} all-to-all(bf16[32,16,128]{2,1,0:T(8,128)(2,1)S(1)} %get-tuple-element.90), channel_id=1, replica_groups=mesh['section'=8,'zh'=2,'y'=4,'x'=4] {'zh','y','x'}, dimensions={0} | all-to-all | bytes 262144 | tf_op jit(solution)/shard_map/all_to_all | solution.py:30
  136.3 1.3 shard_map.154
  137.6 16.3 %all_to_all.46.sums_ref = bf16[32,16,128]{2,1,0:T(8,128)(2,1)S(1)} all-to-all(bf16[32,16,128]{2,1,0:T(8,128)(2,1)S(1)} %get-tuple-element.92), channel_id=1, replica_groups=mesh['section'=8,'zh'=2,'y'=4,'x'=4] {'zh','y','x'}, dimensions={0} | all-to-all | bytes 262144 | tf_op jit(solution)/shard_map/all_to_all | solution.py:30
  154.0 0.0 collective-permute-start.5
  154.0 3.2 %shard_map.155 = (bf16[256,2048]{1,0:T(8,128)(2,1)S(1)}, f32[16,128]{1,0:T(8,128)S(1)}, bf16[16,144,128]{2,1,0:T(8,128)(2,1)S(1)}) custom-call(f32[1]{0:T(128)S(6)} %copy.17.scale_ref, bf16[32,16,128]{2,1,0:T(8,128)(2,1)S(1)} %all_to_all.46.sums_ref, f32[24,128]{1,0:T(8,128)S(1)} %get-tuple-element.95.kept_ref, ...), custom_call_target="tpu_custom_call" | custom-call | flops 600000000 | bytes 4000000 | tf_op jit(solution)/shard_map/pallas_call | solution.py:54
  157.1 16.2 %all_to_all.47.chunks_ref = bf16[16,144,128]{2,1,0:T(8,128)(2,1)S(1)} all-to-all(bf16[16,144,128]{2,1,0:T(8,128)(2,1)S(1)} %get-tuple-element.101), channel_id=1, replica_groups=mesh['section'=8,'zh'=2,'y'=4,'x'=4] {'y','x'}, dimensions={0} | all-to-all | bytes 1179648 | tf_op jit(solution)/shard_map/all_to_all | solution.py:30
  173.3 0.6 shard_map.156
  174.0 0.6 collective-permute-start.4
  174.6 1.4 convolution_convert_fusion.1
  176.1 1.4 convolution_convert_fusion
  177.5 0.0 collective-permute-done.5
  177.5 0.6 fusion
  178.1 0.0 copy-start.6
  178.1 1.5 pad_maximum_fusion
  179.6 2.2 %collective-permute-done.4.taken_ref = bf16[80,128]{1,0:T(8,128)(2,1)S(1)} collective-permute-done((bf16[80,128]{1,0:T(8,128)(2,1)S(1)}, bf16[80,128]{1,0:T(8,128)(2,1)S(1)}, u32[]{:S(2)}, u32[]{:S(2)}) %collective-permute-start.4) | collective-permute-done | bytes 20512 | tf_op jit(solution)/shard_map/ppermute | solution.py:40
  181.8 0.7 shard_map.157
  (9 shorter events, 0.1 us)
Async XLA Ops:
  0.6 9.7 %copy-start.4 = (f32[1,2048]{1,0:T(1,128)S(1)}, f32[1,2048]{1,0:T(1,128)}, u32[]{:S(2)}) copy-start(f32[1,2048]{1,0:T(1,128)} %gain_ref.7) | copy-start | bytes 24580
  0.6 0.7 copy-start.5
  1.5 9.8 %collective-permute-start.1 = (bf16[64,128]{1,0:T(8,128)(2,1)S(1)}, bf16[64,128]{1,0:T(8,128)(2,1)S(1)}, u32[]{:S(2)}, u32[]{:S(2)}) collective-permute-start(bf16[64,128]{1,0:T(8,128)(2,1)S(1)} %shard_map.144.own_ref), channel_id=1, source_target_pairs={{0,16},{16,0},{1,17},{17,1},{2,18},{18,2},{3,19},{19,3},{4,20},{20... | collective-permute-start | bytes 49160 | tf_op jit(solution)/shard_map/ppermute | solution.py:40
  9.5 59.4 %collective-permute-start = (bf16[256,2048]{1,0:T(8,128)(2,1)S(1)}, bf16[256,2048]{1,0:T(8,128)(2,1)S(1)}, u32[]{:S(2)}, u32[]{:S(2)}) collective-permute-start(bf16[256,2048]{1,0:T(8,128)(2,1)S(1)} %select_bitcast_fusion.in_ref), channel_id=1, source_target_pairs={{0,32},{32,64},{64,96},{96,128},{128,160},{160,192},{192,224},{224... | collective-permute-start | bytes 3145736 | tf_op jit(solution)/shard_map/ppermute | solution.py:45
  10.4 39.5 %copy-start.1 = (bf16[1,2048,256]{2,1,0:T(8,128)(2,1)S(1)}, bf16[1,2048,256]{2,1,0:T(8,128)(2,1)}, u32[]{:S(2)}) copy-start(bf16[1,2048,256]{2,1,0:T(8,128)(2,1)} %param.16) | copy-start | bytes 3145732
  10.4 39.5 %copy-start.2 = (bf16[1,256,2048]{2,1,0:T(8,128)(2,1)S(1)}, bf16[1,256,2048]{2,1,0:T(8,128)(2,1)}, u32[]{:S(2)}) copy-start(bf16[1,256,2048]{2,1,0:T(8,128)(2,1)} %param.17) | copy-start | bytes 3145732
  31.8 37.2 %copy-start.7 = (bf16[2,1,256,2048]{3,2,1,0:T(8,128)(2,1)S(1)}, bf16[2,1,256,2048]{3,2,1,0:T(8,128)(2,1)}, u32[]{:S(2)}) copy-start(bf16[2,1,256,2048]{3,2,1,0:T(8,128)(2,1)} %param.9) | copy-start | bytes 6291460
  50.7 21.4 %copy-start = (bf16[2,1,256,2048]{3,2,1,0:T(8,128)(2,1)S(1)}, bf16[2,1,256,2048]{3,2,1,0:T(8,128)(2,1)}, u32[]{:S(2)}) copy-start(bf16[2,1,256,2048]{3,2,1,0:T(8,128)(2,1)} %cotangent_ref.3) | copy-start | bytes 6291460
  50.7 21.3 %copy-start.3 = (bf16[1,1,256,2048]{3,2,1,0:T(8,128)(2,1)S(1)}, bf16[1,1,256,2048]{3,2,1,0:T(8,128)(2,1)}, u32[]{:S(2)}) copy-start(bf16[1,1,256,2048]{3,2,1,0:T(8,128)(2,1)} %backflow_ref.1) | copy-start | bytes 3145732
  67.0 5.0 %collective-permute-start.2 = (f32[24,128]{1,0:T(8,128)S(1)}, f32[24,128]{1,0:T(8,128)S(1)}, u32[]{:S(2)}, u32[]{:S(2)}) collective-permute-start(f32[24,128]{1,0:T(8,128)S(1)} %shard_map.149.packed_ref), channel_id=1, source_target_pairs={{0,32},{32,64},{64,96},{96,128},{128,160},{160,192},{192,224},{1,3... | collective-permute-start | bytes 36872 | tf_op jit(solution)/shard_map/ppermute | solution.py:36
  116.4 1.5 collective-permute-start.3
  154.0 23.5 %collective-permute-start.5 = (bf16[256,2048]{1,0:T(8,128)(2,1)S(1)}, bf16[256,2048]{1,0:T(8,128)(2,1)S(1)}, u32[]{:S(2)}, u32[]{:S(2)}) collective-permute-start(bf16[256,2048]{1,0:T(8,128)(2,1)S(1)} %get-tuple-element.113), channel_id=1, source_target_pairs={{0,224},{32,0},{64,32},{96,64},{128,96},{160,128},{192,160},{224,1... | collective-permute-start | bytes 3145736 | tf_op jit(solution)/shard_map/ppermute | solution.py:45
  174.0 7.8 %collective-permute-start.4 = (bf16[80,128]{1,0:T(8,128)(2,1)S(1)}, bf16[80,128]{1,0:T(8,128)(2,1)S(1)}, u32[]{:S(2)}, u32[]{:S(2)}) collective-permute-start(bf16[80,128]{1,0:T(8,128)(2,1)S(1)} %get-tuple-element.112), channel_id=1, source_target_pairs={{0,16},{16,0},{1,17},{17,1},{2,18},{18,2},{3,19},{19,3},{4,20},{20... | collective-permute-start | bytes 61448 | tf_op jit(solution)/shard_map/ppermute | solution.py:40
  178.1 3.7 %copy-start.6 = (bf16[1,2048,4]{1,2,0:T(4,128)(2,1)S(1)}, bf16[1,2048,4]{1,2,0:T(4,128)(2,1)}, u32[]{:S(2)}) copy-start(bf16[1,2048,4]{1,2,0:T(4,128)(2,1)} %param.15) | copy-start | bytes 49156
